TPU v7x, 32 devices: a whole 2x2x4 slice. The times are simulated.
32 devices in a mesh: dp: 4 (over y, x), fsdp: 8 (over z, core).
Axes of the slice: x: 2, y: 2, z: 4, core: 2. Of those that a mesh axis runs over, the one named last changes fastest.
Arguments:
- inputs: bfloat16 [32, 2048, 256], P(('dp', 'fsdp')), may hold values from -6 to 6
- inject: bfloat16 [32, 2048, 256], P(('dp', 'fsdp')), may hold values from -6 to 6
- segments: int32 [32, 2048], P(('dp', 'fsdp')), may hold values from -1 to 45, as said below
- cotangent: bfloat16 [32, 2048, 256], P(('dp', 'fsdp')), may hold values from -6 to 6
- qkv_weight: bfloat16 [256, 768], P(None, 'fsdp'), may hold values from -0.5 to 0.5
- out_weight: bfloat16 [256, 256], P(None, 'fsdp'), may hold values from -1 to 1
- up_weight: bfloat16 [256, 1024], P(None, 'fsdp'), may hold values from -0.375 to 0.375
- down_weight: bfloat16 [1024, 256], P(None, 'fsdp'), may hold values from -0.1875 to 0.1875
- query_bias: bfloat16 [256], P('fsdp'), may hold values from -1.796875 to 1.796875
- value_bias: bfloat16 [256], P('fsdp'), may hold values from -1.796875 to 1.796875
- out_bias: bfloat16 [256], P('fsdp'), may hold values from -1.796875 to 1.796875
- up_bias: bfloat16 [1024], P('fsdp'), may hold values from -1.796875 to 1.796875
- down_bias: bfloat16 [256], P('fsdp'), may hold values from -1.796875 to 1.796875
- attn_gain: bfloat16 [256], P('fsdp'), may hold values from 0.5 to 1.5
- attn_shift: bfloat16 [256], P('fsdp'), may hold values from -1.796875 to 1.796875
- mlp_gain: bfloat16 [256], P('fsdp'), may hold values from 0.5 to 1.5
- mlp_shift: bfloat16 [256], P('fsdp'), may hold values from -1.796875 to 1.796875
Outputs:
- result: bfloat16 [32, 2048, 256], P(('dp', 'fsdp'))
- grad_inputs: bfloat16 [32, 2048, 256], P(('dp', 'fsdp'))
- grad_inject: bfloat16 [32, 2048, 256], P(('dp', 'fsdp'))
- grad_qkv_weight: float32 [256, 768], P(None, 'fsdp')
- grad_out_weight: float32 [256, 256], P(None, 'fsdp')
- grad_up_weight: float32 [256, 1024], P(None, 'fsdp')
- grad_down_weight: float32 [1024, 256], P(None, 'fsdp')
- grad_query_bias: float32 [256], P('fsdp')
- grad_value_bias: float32 [256], P('fsdp')
- grad_out_bias: float32 [256], P('fsdp')
- grad_up_bias: float32 [1024], P('fsdp')
- grad_down_bias: float32 [256], P('fsdp')
- grad_attn_gain: float32 [256], P('fsdp')
- grad_attn_shift: float32 [256], P('fsdp')
- grad_mlp_gain: float32 [256], P('fsdp')
- grad_mlp_shift: float32 [256], P('fsdp')
Inputs may be any that keep to these rules, and one draw needn't show every extreme that they name: `segments`: in each row ids start at 0 and rise by one from prompt to prompt; every prompt covers 41 to 101 positions and one prompt of each row covers exactly 101; the positions after the last prompt hold -1, and there are 102 or more of them.
All inputs are finite; a program needn't handle non-finite values.
Results may differ from a plain program's by a relative error of at most 0.018.
Values may be sent and summed in bfloat16 or wider, within the bound.
No kernel may reach another device: no remote copies, remote signals or barrier semaphores. Data moves between devices by JAX's collectives and lax.ppermute only.
A program may use at most 192 MiB of HBM per device.

v0:
```python
from functools import partial

import jax
import jax.numpy as jnp
from jax import lax
from jax.sharding import PartitionSpec as P

HEADS = 8
HD = 32
LOOPS = 2
MARGIN = 128
QBLOCK = 512


norm_eps = 1e-05
masked_score = -1e30


def shortened(shard):

    def short(part):
        return part.astype(jnp.bfloat16) if part.dtype == jnp.float32 else part

    return jax.tree.map(short, shard)


def product(left_op, right_op):
    return jnp.dot(left_op, right_op, preferred_element_type=jnp.float32)


def product_tn(left_op, right_op):
    return lax.dot_general(
        left_op, right_op, (((0,), (0,)), ((), ())), preferred_element_type=jnp.float32
    )


def product_nt(left_op, right_op):
    return lax.dot_general(
        left_op, right_op, (((1,), (1,)), ((), ())), preferred_element_type=jnp.float32
    )


def column_sum(values):
    return jnp.sum(values.astype(jnp.float32), axis=0)


def norm_parts(values):
    centre = values - jnp.mean(values, axis=-1, keepdims=True)
    inverse = lax.rsqrt(jnp.mean(centre * centre, axis=-1, keepdims=True) + norm_eps)
    return (centre * inverse, inverse)


def norm_back(grad_normed, unit_rows, inverse, gain_vec):
    scaled = grad_normed * gain_vec
    return inverse * (
        scaled
        - jnp.mean(scaled, axis=-1, keepdims=True)
        - unit_rows * jnp.mean(scaled * unit_rows, axis=-1, keepdims=True)
    )


def allowed_pairs(seg_query, seg_keys):
    query_len = seg_query.shape[0]
    keys_len = seg_keys.shape[0]
    query_place = lax.broadcasted_iota(jnp.int32, (query_len, keys_len), 0) + (keys_len - query_len)
    key_place = lax.broadcasted_iota(jnp.int32, (query_len, keys_len), 1)
    same_prompt = (
        (seg_query[:, None] == seg_keys[None, :])
        & (seg_query[:, None] >= 0)
        & (key_place <= query_place)
    )
    return same_prompt | (key_place == query_place)


def padded(key_rows, value_rows, segments):
    keys_pad = jnp.pad(key_rows, ((0, 0), (MARGIN, 0), (0, 0)))
    values_pad = jnp.pad(value_rows, ((0, 0), (MARGIN, 0), (0, 0)))
    seg_pad = jnp.pad(segments, ((0, 0), (MARGIN, 0)), constant_values=-2)
    return (keys_pad, values_pad, seg_pad)


def block_tiles(block_id, per_row, query_rows, keys_pad, values_pad, segments, seg_pad):
    model_dim = query_rows.shape[2]
    row_id = block_id // per_row
    block_start = block_id % per_row * QBLOCK
    query_tile = lax.dynamic_slice(query_rows, (row_id, block_start, 0), (1, QBLOCK, model_dim))[0]
    key_tile = lax.dynamic_slice(
        keys_pad, (row_id, block_start, 0), (1, QBLOCK + MARGIN, model_dim)
    )[0]
    value_tile = lax.dynamic_slice(
        values_pad, (row_id, block_start, 0), (1, QBLOCK + MARGIN, model_dim)
    )[0]
    seg_query = lax.dynamic_slice(segments, (row_id, block_start), (1, QBLOCK))[0]
    seg_keys = lax.dynamic_slice(seg_pad, (row_id, block_start), (1, QBLOCK + MARGIN))[0]
    return (
        row_id,
        block_start,
        query_tile.reshape(QBLOCK, HEADS, HD),
        key_tile.reshape(QBLOCK + MARGIN, HEADS, HD),
        value_tile.reshape(QBLOCK + MARGIN, HEADS, HD),
        allowed_pairs(seg_query, seg_keys),
    )


def masked_scores(query_tile, key_tile, allowed):
    scores = jnp.einsum(
        "qhd,khd->hqk", query_tile, key_tile, preferred_element_type=jnp.float32
    ) * HD ** (-0.5)
    return jnp.where(allowed[None], scores, masked_score)


def attend_forward(query_rows, key_rows, value_rows, segments):
    row_count = query_rows.shape[0]
    per_row = query_rows.shape[1] // QBLOCK
    keys_pad, values_pad, seg_pad = padded(key_rows, value_rows, segments)

    def one_block(block_id):
        tile_data = block_tiles(
            block_id, per_row, query_rows, keys_pad, values_pad, segments, seg_pad
        )
        query_tile, key_tile, value_tile, allowed = tile_data[2:]
        scores = masked_scores(query_tile, key_tile, allowed)
        row_max = jnp.max(scores, axis=-1, keepdims=True)
        exp_scores = jnp.exp(scores - row_max)
        row_total = jnp.sum(exp_scores, axis=-1, keepdims=True)
        prob_low = (exp_scores / row_total).astype(jnp.bfloat16)
        context = jnp.einsum(
            "hqk,khd->qhd", prob_low, value_tile, preferred_element_type=jnp.float32
        )
        return (
            context.reshape(QBLOCK, HEADS * HD).astype(jnp.bfloat16),
            (row_max + jnp.log(row_total))[:, :, 0],
        )

    context, log_total = lax.map(one_block, jnp.arange(row_count * per_row, dtype=jnp.int32))
    return (context.reshape(query_rows.shape), log_total)


def attend_backward(query_rows, key_rows, value_rows, segments, log_total, grad_context):
    row_count, length, model_dim = query_rows.shape
    per_row = length // QBLOCK
    keys_pad, values_pad, seg_pad = padded(key_rows, value_rows, segments)

    def one_block(grads_pad, block_id):
        key_grad_pad, value_grad_pad = grads_pad
        row_id, block_start, query_tile, key_tile, value_tile, allowed = block_tiles(
            block_id, per_row, query_rows, keys_pad, values_pad, segments, seg_pad
        )
        grad_tile = lax.dynamic_slice(
            grad_context, (row_id, block_start, 0), (1, QBLOCK, model_dim)
        )[0].reshape(QBLOCK, HEADS, HD)
        probs_full = jnp.exp(
            masked_scores(query_tile, key_tile, allowed) - log_total[block_id][:, :, None]
        )
        value_part = jnp.einsum(
            "hqk,qhd->khd",
            probs_full.astype(jnp.bfloat16),
            grad_tile,
            preferred_element_type=jnp.float32,
        )
        grad_probs = jnp.einsum(
            "qhd,khd->hqk", grad_tile, value_tile, preferred_element_type=jnp.float32
        )
        centred = grad_probs - jnp.sum(probs_full * grad_probs, axis=-1, keepdims=True)
        grad_scores = (probs_full * centred).astype(jnp.bfloat16)
        query_part = jnp.einsum(
            "hqk,khd->qhd", grad_scores, key_tile, preferred_element_type=jnp.float32
        ) * HD ** (-0.5)
        key_part = jnp.einsum(
            "hqk,qhd->khd", grad_scores, query_tile, preferred_element_type=jnp.float32
        ) * HD ** (-0.5)
        corner = (row_id, block_start, 0)
        window = (1, QBLOCK + MARGIN, model_dim)
        key_grad_pad = lax.dynamic_update_slice(
            key_grad_pad,
            lax.dynamic_slice(key_grad_pad, corner, window) + key_part.reshape(window),
            corner,
        )
        value_grad_pad = lax.dynamic_update_slice(
            value_grad_pad,
            lax.dynamic_slice(value_grad_pad, corner, window) + value_part.reshape(window),
            corner,
        )
        return ((key_grad_pad, value_grad_pad), query_part.reshape(QBLOCK, model_dim))

    zero_pad = jnp.zeros((row_count, length + MARGIN, model_dim), jnp.float32)
    grads_pad, query_grad = lax.scan(
        one_block, (zero_pad, zero_pad), jnp.arange(row_count * per_row, dtype=jnp.int32)
    )
    return (
        query_grad.reshape(query_rows.shape),
        grads_pad[0][:, MARGIN:],
        grads_pad[1][:, MARGIN:],
    )


def reduce_grads(grad_terms):
    owned_sum = (
        lax.psum_scatter(grad_terms[0], "fsdp", scatter_dimension=1, tiled=True),
        lax.psum_scatter(grad_terms[1], "fsdp", scatter_dimension=1, tiled=True),
        lax.psum_scatter(grad_terms[2], "fsdp", scatter_dimension=1, tiled=True),
        lax.psum_scatter(grad_terms[3], "fsdp", scatter_dimension=1, tiled=True),
        lax.psum_scatter(grad_terms[4], "fsdp", scatter_dimension=0, tiled=True),
        lax.psum_scatter(grad_terms[5], "fsdp", scatter_dimension=0, tiled=True),
        lax.psum_scatter(grad_terms[6], "fsdp", scatter_dimension=0, tiled=True),
        lax.psum_scatter(grad_terms[7], "fsdp", scatter_dimension=0, tiled=True),
        lax.psum_scatter(grad_terms[8], "fsdp", scatter_dimension=0, tiled=True),
        lax.psum_scatter(grad_terms[9], "fsdp", scatter_dimension=0, tiled=True),
        lax.psum_scatter(grad_terms[10], "fsdp", scatter_dimension=0, tiled=True),
        lax.psum_scatter(grad_terms[11], "fsdp", scatter_dimension=0, tiled=True),
        lax.psum_scatter(grad_terms[12], "fsdp", scatter_dimension=0, tiled=True),
    )
    reduced = jax.tree.map(
        lambda part: part.astype(jnp.float32), lax.psum(shortened(owned_sum), "dp")
    )
    return reduced


def add_tuples(first_terms, second_terms):
    if first_terms is None:
        return tuple(second_terms)
    return tuple((running + addend for running, addend in zip(first_terms, second_terms)))


def local(
    inputs,
    inject,
    segments,
    cotangent,
    qkv_weight,
    out_weight,
    up_weight,
    down_weight,
    query_bias,
    value_bias,
    out_bias,
    up_bias,
    down_bias,
    attn_gain,
    attn_shift,
    mlp_gain,
    mlp_shift,
):
    gathered = (
        lax.all_gather(qkv_weight, "fsdp", axis=1, tiled=True),
        lax.all_gather(out_weight, "fsdp", axis=1, tiled=True),
        lax.all_gather(up_weight, "fsdp", axis=1, tiled=True),
        lax.all_gather(down_weight, "fsdp", axis=1, tiled=True),
        lax.all_gather(query_bias, "fsdp", axis=0, tiled=True),
        lax.all_gather(value_bias, "fsdp", axis=0, tiled=True),
        lax.all_gather(out_bias, "fsdp", axis=0, tiled=True),
        lax.all_gather(up_bias, "fsdp", axis=0, tiled=True),
        lax.all_gather(down_bias, "fsdp", axis=0, tiled=True),
        lax.all_gather(attn_gain, "fsdp", axis=0, tiled=True),
        lax.all_gather(attn_shift, "fsdp", axis=0, tiled=True),
        lax.all_gather(mlp_gain, "fsdp", axis=0, tiled=True),
        lax.all_gather(mlp_shift, "fsdp", axis=0, tiled=True),
    )
    qkv_full, out_full, up_full, down_full = gathered[:4]
    (
        bias_query,
        bias_value,
        bias_out,
        bias_up,
        bias_down,
        gain_attn,
        shift_attn,
        gain_mlp,
        shift_mlp,
    ) = tuple((vector.astype(jnp.float32) for vector in gathered[4:]))
    row_count, length, model_dim = inputs.shape
    token_count = row_count * length
    bias_qkv = jnp.concatenate([bias_query, jnp.zeros_like(bias_query), bias_value])
    hidden_state = inputs.astype(jnp.float32).reshape(token_count, model_dim)
    inject_rows = inject.astype(jnp.float32).reshape(token_count, model_dim)
    saved_loops = []
    for repeat in range(LOOPS):
        injected = hidden_state + inject_rows
        unit_attn, inverse_attn = norm_parts(injected)
        normed = (unit_attn * gain_attn + shift_attn).astype(jnp.bfloat16)
        qkv_rows = (product(normed, qkv_full) + bias_qkv).astype(jnp.bfloat16)
        query_rows = qkv_rows[:, :model_dim].reshape(row_count, length, model_dim)
        key_rows = qkv_rows[:, model_dim : 2 * model_dim].reshape(row_count, length, model_dim)
        value_rows = qkv_rows[:, 2 * model_dim :].reshape(row_count, length, model_dim)
        context, log_total = attend_forward(query_rows, key_rows, value_rows, segments)
        context_rows = context.reshape(token_count, model_dim)
        after_attn = injected + (product(context_rows, out_full) + bias_out)
        unit_mlp, inverse_mlp = norm_parts(after_attn)
        normed_mlp = (unit_mlp * gain_mlp + shift_mlp).astype(jnp.bfloat16)
        pre_act = product(normed_mlp, up_full) + bias_up
        hidden = jax.nn.gelu(pre_act, approximate=True).astype(jnp.bfloat16)
        hidden_state = after_attn + (product(hidden, down_full) + bias_down)
        saved_loops.append(
            (
                unit_attn,
                inverse_attn,
                normed,
                query_rows,
                key_rows,
                value_rows,
                log_total,
                context_rows,
                unit_mlp,
                inverse_mlp,
                normed_mlp,
                pre_act,
                hidden,
            )
        )
    result = hidden_state.astype(jnp.bfloat16).reshape(inputs.shape)
    grad_state = cotangent.astype(jnp.float32).reshape(token_count, model_dim)
    grad_inject = jnp.zeros_like(grad_state)
    summed_grads = None
    owned_grads = None
    for repeat in reversed(range(LOOPS)):
        (
            unit_attn,
            inverse_attn,
            normed,
            query_rows,
            key_rows,
            value_rows,
            log_total,
            context_rows,
            unit_mlp,
            inverse_mlp,
            normed_mlp,
            pre_act,
            hidden,
        ) = saved_loops[repeat]
        grad_down_out = grad_state.astype(jnp.bfloat16)
        grad_down_mat = product_tn(hidden, grad_down_out)
        grad_hidden = product_nt(grad_down_out, down_full)
        gelu_value, gelu_pull = jax.vjp(partial(jax.nn.gelu, approximate=True), pre_act)
        grad_pre = gelu_pull(grad_hidden)[0].astype(jnp.bfloat16)
        grad_up_mat = product_tn(normed_mlp, grad_pre)
        grad_normed_mlp = product_nt(grad_pre, up_full)
        grad_mid = grad_state + norm_back(grad_normed_mlp, unit_mlp, inverse_mlp, gain_mlp)
        grad_branch = grad_mid.astype(jnp.bfloat16)
        grad_out_mat = product_tn(context_rows, grad_branch)
        grad_context = (
            product_nt(grad_branch, out_full)
            .astype(jnp.bfloat16)
            .reshape(row_count, length, model_dim)
        )
        grad_query, grad_keys, grad_values = attend_backward(
            query_rows, key_rows, value_rows, segments, log_total, grad_context
        )
        grad_qkv = (
            jnp.concatenate([grad_query, grad_keys, grad_values], axis=-1)
            .reshape(token_count, 3 * model_dim)
            .astype(jnp.bfloat16)
        )
        grad_qkv_mat = product_tn(normed, grad_qkv)
        grad_normed = product_nt(grad_qkv, qkv_full)
        grad_in = grad_mid + norm_back(grad_normed, unit_attn, inverse_attn, gain_attn)
        grad_inject = grad_inject + grad_in
        grad_state = grad_in
        qkv_sums = column_sum(grad_qkv)
        loop_grads = (
            grad_qkv_mat,
            grad_out_mat,
            grad_up_mat,
            grad_down_mat,
            qkv_sums[:model_dim],
            qkv_sums[2 * model_dim :],
            column_sum(grad_branch),
            column_sum(grad_pre),
            column_sum(grad_down_out),
            jnp.sum(grad_normed * unit_attn, axis=0),
            jnp.sum(grad_normed, axis=0),
            jnp.sum(grad_normed_mlp * unit_mlp, axis=0),
            jnp.sum(grad_normed_mlp, axis=0),
        )
        summed_grads = add_tuples(summed_grads, loop_grads)
    owned_grads = reduce_grads(summed_grads)
    grad_inputs = grad_state.astype(jnp.bfloat16).reshape(inputs.shape)
    grad_inject_out = grad_inject.astype(jnp.bfloat16).reshape(inputs.shape)
    return (result, grad_inputs, grad_inject_out) + owned_grads


def solution(mesh):
    placed = (
        P(("dp", "fsdp"), None, None),
        P(("dp", "fsdp"), None, None),
        P(("dp", "fsdp"), None),
        P(("dp", "fsdp"), None, None),
        P(None, "fsdp"),
        P(None, "fsdp"),
        P(None, "fsdp"),
        P(None, "fsdp"),
        P("fsdp"),
        P("fsdp"),
        P("fsdp"),
        P("fsdp"),
        P("fsdp"),
        P("fsdp"),
        P("fsdp"),
        P("fsdp"),
        P("fsdp"),
    )
    return jax.shard_map(
        local,
        mesh=mesh,
        in_specs=placed,
        out_specs=(
            P(("dp", "fsdp"), None, None),
            P(("dp", "fsdp"), None, None),
            P(("dp", "fsdp"), None, None),
            P(None, "fsdp"),
            P(None, "fsdp"),
            P(None, "fsdp"),
            P(None, "fsdp"),
            P("fsdp"),
            P("fsdp"),
            P("fsdp"),
            P("fsdp"),
            P("fsdp"),
            P("fsdp"),
            P("fsdp"),
            P("fsdp"),
            P("fsdp"),
        ),
        check_vma=False,
    )
```

profile of v0, /device:TPU:0, one launch (start us, length us, event | category | flops | bytes accessed | tf_op | source)
XLA Modules:
  0.0 906.4 jit_solution(17328413272361587225)
XLA Ops:
  16.0 18.1 %all-reduce.23 = (bf16[256]{0:T(256)(128)(2,1)S(1)}, bf16[256]{0:T(256)(128)(2,1)S(1)}, bf16[256]{0:T(256)(128)(2,1)S(1)}, bf16[256]{0:T(256)(128)(2,1)S(1)}, bf...) all-reduce(bf16[256]{0:T(256)(128)(2,1)S(1)} %dynamic-update-slice., ...), channel_id=1, replica_groups=mesh['dp'=4,'fsdp'=8] {'fsdp'}, use_global_device_ids=true, to_apply=%add.8 | all-reduce | flops 2048 | bytes 8192
  38.6 8.6 all-gather
  47.8 15.2 %all_gather.44 = bf16[256,256]{0,1:T(8,128)(2,1)} all-gather(bf16[256,32]{0,1:T(8,128)(2,1)} %param.30), channel_id=1, replica_groups=mesh['dp'=4,'fsdp'=8] {'fsdp'}, dimensions={1}, use_global_device_ids=true | all-gather | bytes 147456 | tf_op jit(solution)/shard_map/all_gather | solution.py:246
  63.0 14.7 %all_gather.41 = bf16[256,768]{0,1:T(8,128)(2,1)S(1)} all-gather(bf16[256,96]{0,1:T(8,128)(2,1)} %param.29), channel_id=1, replica_groups=mesh['dp'=4,'fsdp'=8] {'fsdp'}, dimensions={1}, use_global_device_ids=true | all-gather | bytes 442368 | tf_op jit(solution)/shard_map/all_gather | solution.py:245
  77.6 14.9 %all_gather.48 = bf16[256,1024]{1,0:T(8,128)(2,1)} all-gather(bf16[256,128]{1,0:T(8,128)(2,1)} %param.31), channel_id=1, replica_groups=mesh['dp'=4,'fsdp'=8] {'fsdp'}, dimensions={1}, use_global_device_ids=true | all-gather | bytes 589824 | tf_op jit(solution)/shard_map/all_gather | solution.py:247
  92.5 16.2 %all_gather.50 = bf16[1024,256]{0,1:T(8,128)(2,1)} all-gather(bf16[1024,32]{0,1:T(8,128)(2,1)} %param.32), channel_id=1, replica_groups=mesh['dp'=4,'fsdp'=8] {'fsdp'}, dimensions={1}, use_global_device_ids=true | all-gather | bytes 589824 | tf_op jit(solution)/shard_map/all_gather | solution.py:248
  131.5 74.9 %while.60 = (s32[]{:T(128)}, bf16[4,512,256]{2,1,0:T(8,128)(2,1)}, f32[4,8,512]{2,1,0:T(8,128)}, s32[4]{0:T(128)S(1)}, bf16[1,2176,256]{1,2,0:T(8,128)(2,1)}, /*...) while((s32[]{:T(128)}, bf16[4,512,256]{2,1,0:T(8,128)(2,1)}, ...), condition=%wide.region_5.6_spmd, body=%wide.region_2.5_spmd.sunk | while | flops 369095680 | bytes 36983668 | solution.py:135
  223.1 84.1 %while.61 = (s32[]{:T(128)}, bf16[4,512,256]{2,1,0:T(8,128)(2,1)S(1)}, f32[4,8,512]{2,1,0:T(8,128)}, s32[4]{0:T(128)}, bf16[1,2176,256]{1,2,0:T(8,128)(2,1)S(1)}...) while((s32[]{:T(128)}, ...), condition=%wide.region_13.14_spmd, body=%wide.region_10.13_spmd.sunk | while | flops 369095680 | bytes 37049232 | solution.py:135
  316.1 7.3 convert_reduce_fusion.1
  341.7 154.8 %while.62 = (s32[]{:T(128)}, f32[1,2176,256]{2,1,0:T(8,128)}, f32[1,2176,256]{2,1,0:T(8,128)}, bf16[4,512,256]{2,1,0:T(8,128)(2,1)}, s32[4]{0:T(128)S(1)}, /*ind...) while((s32[]{:T(128)}, f32[1,2176,256]{2,1,0:T(8,128)}, ...), condition=%wide.region_20.21_spmd, body=%wide.region_18.20_spmd.sunk | while | flops 880899072 | bytes 181736560 | solution.py:187
  365.3 7.1 multiply_reduce_fusion.20
  403.9 7.1 multiply_reduce_fusion.20
  442.5 7.1 multiply_reduce_fusion.20
  481.1 7.1 multiply_reduce_fusion.20
  511.5 10.2 %convert_reduce_fusion = (f32[1024]{0:T(1024)}, bf16[2048,1024]{1,0:T(8,128)(2,1)S(1)}) fusion(f32[2048,1024]{1,0:T(8,128)} %copy-done.33, f32[1024]{0:T(1024)S(1)} %bitcast.386, bf16[1024,256]{0,1:T(8,128)(2,1)S(1)} %copy-done.61, f32[2048,256]{0,1:T(8,128)S(1)} %get-tuple-element.861), kind=kOutput, calls=%fused_computation.124 | convolution fusion | flops 1122499584 | bytes 15212544 | tf_op jit(solution)/shard_map/dot_general | solution.py:38
  544.7 155.0 %while.63 = (s32[]{:T(128)}, f32[1,2176,256]{2,1,0:T(8,128)}, f32[1,2176,256]{2,1,0:T(8,128)}, bf16[4,512,256]{2,1,0:T(8,128)(2,1)}, s32[4]{0:T(128)S(1)}, /*ind...) while((s32[]{:T(128)}, f32[1,2176,256]{2,1,0:T(8,128)}, ...), condition=%wide.region_27.28_spmd, body=%wide.region_25.27_spmd.sunk | while | flops 880899072 | bytes 181736560 | solution.py:187
  568.1 7.1 multiply_reduce_fusion.21
  606.7 7.1 multiply_reduce_fusion.21
  645.4 7.1 multiply_reduce_fusion.21
  684.0 7.1 multiply_reduce_fusion.21
  741.0 26.6 %all-reduce.22 = (bf16[256]{0:T(256)(128)(2,1)S(1)}, bf16[256]{0:T(256)(128)(2,1)S(1)}, bf16[256]{0:T(256)(128)(2,1)S(1)}, bf16[1024]{0:T(1024)(128)(2,1)S(1)}, ...) all-reduce(f32[256]{0:T(256)S(1)} %get-tuple-element.892, ...), channel_id=6, replica_groups=mesh['dp'=4,'fsdp'=8] {'fsdp'}, use_global_device_ids=true, to_apply=%region_40.41.clone | all-reduce | flops 3072 | bytes 18432
  782.5 19.3 %reduce-scatter.11.cloned.1.call-done = f32[1024,32]{0,1:T(8,128)} async-done(((f32[1024,256]{0,1:T(8,128)}), f32[1024,32]{0,1:T(8,128)}) %reduce-scatter.11.cloned.1.call-update) | async-done | bytes 131088 | tf_op jit(solution)/shard_map/reduce_scatter | solution.py:202
  811.7 36.8 %all-reduce.29.cloned.1.call-done = (bf16[256,96]{0,1:T(8,128)(2,1)}, bf16[256,32]{0,1:T(8,128)(2,1)}, bf16[32]{0:T(256)(128)(2,1)}, bf16[32]{0:T(256)(128)(2,1)...) async-done(((bf16[256,96]{0,1:T(8,128)(2,1)}, ...) | async-done | bytes 66320 | tf_op jit(solution)/shard_map/psum | solution.py:214
  861.5 34.5 %all-reduce.31.cloned.1.call-done = (bf16[256,128]{1,0:T(8,128)(2,1)}, bf16[1024,32]{0,1:T(8,128)(2,1)}) async-done(((bf16[256,128]{1,0:T(8,128)(2,1)}, bf16[1024,32]{0,1:T(8,128)(2,1)}), (bf16[256,128]{1,0:T(8,128)(2,1)}, bf16[1024,32]{0,1:T(8,128)(2,1)})) %all-reduce.31.cloned.1.call-update) | async-done | bytes 131088 | tf_op jit(solution)/shard_map/psum | solution.py:214
  (866 shorter events, 553.4 us)
Async XLA Ops:
  7.2 103.1 %copy-start.56 = (bf16[1,2048,256]{2,1,0:T(8,128)(2,1)S(1)}, bf16[1,2048,256]{2,1,0:T(8,128)(2,1)}, u32[]{:S(2)}) copy-start(bf16[1,2048,256]{2,1,0:T(8,128)(2,1)} %param.25) | copy-start | bytes 3145732
  7.2 765.7 %reduce-scatter.7.cloned.1.call-start = ((), (), s32[]{:S(2)}) async-start(), calls=%async_computation.5 | async-start | bytes 294912 | tf_op jit(solution)/shard_map/reduce_scatter | solution.py:200
  77.6 37.1 %copy-start.65 = (bf16[256,768]{0,1:T(8,128)(2,1)}, bf16[256,768]{0,1:T(8,128)(2,1)S(1)}, u32[]{:S(2)}) copy-start(bf16[256,768]{0,1:T(8,128)(2,1)S(1)} %all_gather.41) | copy-start | bytes 1179652
  110.3 100.3 %copy-start.9 = (bf16[1,2048,256]{1,2,0:T(8,128)(2,1)}, bf16[1,2048,256]{1,2,0:T(8,128)(2,1)S(1)}, u32[]{:S(2)}) copy-start(bf16[1,2048,256]{1,2,0:T(8,128)(2,1)S(1)} %copy.102) | copy-start | bytes 3145732
  110.9 95.5 %copy-start.11 = (bf16[1,2048,256]{1,2,0:T(8,128)(2,1)}, bf16[1,2048,256]{1,2,0:T(8,128)(2,1)S(1)}, u32[]{:S(2)}) copy-start(bf16[1,2048,256]{1,2,0:T(8,128)(2,1)S(1)} %copy.101) | copy-start | bytes 3145732
  131.5 74.9 %copy-start.95 = (f32[256]{0:T(256)S(1)}, f32[256]{0:T(256)}, u32[]{:S(2)}) copy-start(f32[256]{0:T(256)} %convert_element_type.297) | copy-start | bytes 3076
  310.7 22.0 %copy-start.16 = (f32[2048,256]{0,1:T(8,128)}, f32[2048,256]{0,1:T(8,128)S(1)}, u32[]{:S(2)}) copy-start(f32[2048,256]{0,1:T(8,128)S(1)} %get-tuple-element.900) | copy-start | bytes 6291460
  310.8 22.0 %copy-start.76 = (f32[2048]{0:T(1024)}, f32[2048]{0:T(1024)S(1)}, u32[]{:S(2)}) copy-start(f32[2048]{0:T(1024)S(1)} %broadcast_multiply_fusion.8) | copy-start | bytes 24580
  311.1 21.7 %copy-start.82 = (f32[2048]{0:T(1024)}, f32[2048]{0:T(1024)S(1)}, u32[]{:S(2)}) copy-start(f32[2048]{0:T(1024)S(1)} %add_rsqrt_fusion) | copy-start | bytes 24580
  401.6 9.5 %slice-start = ((s8[10485760]{0:T(1024)(128)(4,1)}), s8[2097152]{0:T(1024)(128)(4,1)S(1)}, s32[]{:S(2)}) async-start(s8[10485760]{0:T(1024)(128)(4,1)} %bitcast.336), calls=%async_computation.10 | async-start | bytes 4194304 | tf_op jit(solution)/shard_map/while
  440.2 9.5 %slice-start = ((s8[10485760]{0:T(1024)(128)(4,1)}), s8[2097152]{0:T(1024)(128)(4,1)S(1)}, s32[]{:S(2)}) async-start(s8[10485760]{0:T(1024)(128)(4,1)} %bitcast.336), calls=%async_computation.10 | async-start | bytes 4194304 | tf_op jit(solution)/shard_map/while
  498.4 36.7 %copy-start.35 = (bf16[1,2048,256]{2,1,0:T(8,128)(2,1)}, bf16[1,2048,256]{2,1,0:T(8,128)(2,1)S(1)}, u32[]{:S(2)}) copy-start(bf16[1,2048,256]{2,1,0:T(8,128)(2,1)S(1)} %slice.81) | copy-start | bytes 3145732
  511.4 10.2 %copy-start.24 = (f32[2048,256]{0,1:T(8,128)}, f32[2048,256]{0,1:T(8,128)S(1)}, u32[]{:S(2)}) copy-start(f32[2048,256]{0,1:T(8,128)S(1)} %get-tuple-element.861) | copy-start | bytes 6291460
  511.5 10.2 %copy-start.53 = (bf16[256,1024]{1,0:T(8,128)(2,1)S(1)}, bf16[256,1024]{1,0:T(8,128)(2,1)}, u32[]{:S(2)}) copy-start(bf16[256,1024]{1,0:T(8,128)(2,1)} %all_gather.48) | copy-start | bytes 1572868
  535.0 239.2 %reduce-scatter.5.cloned.1.call-start = ((), (), s32[]{:S(2)}) async-start(), calls=%async_computation.4 | async-start | bytes 884736 | tf_op jit(solution)/shard_map/reduce_scatter | solution.py:199
  565.7 9.5 %slice-start.3 = ((s8[10485760]{0:T(1024)(128)(4,1)}), s8[2097152]{0:T(1024)(128)(4,1)S(1)}, s32[]{:S(2)}) async-start(s8[10485760]{0:T(1024)(128)(4,1)} %bitcast.338), calls=%async_computation.13 | async-start | bytes 4194304 | tf_op jit(solution)/shard_map/while
  604.4 9.5 %slice-start.3 = ((s8[10485760]{0:T(1024)(128)(4,1)}), s8[2097152]{0:T(1024)(128)(4,1)S(1)}, s32[]{:S(2)}) async-start(s8[10485760]{0:T(1024)(128)(4,1)} %bitcast.338), calls=%async_computation.13 | async-start | bytes 4194304 | tf_op jit(solution)/shard_map/while
  643.0 9.5 %slice-start.3 = ((s8[10485760]{0:T(1024)(128)(4,1)}), s8[2097152]{0:T(1024)(128)(4,1)S(1)}, s32[]{:S(2)}) async-start(s8[10485760]{0:T(1024)(128)(4,1)} %bitcast.338), calls=%async_computation.13 | async-start | bytes 4194304 | tf_op jit(solution)/shard_map/while
  681.7 9.5 %slice-start.3 = ((s8[10485760]{0:T(1024)(128)(4,1)}), s8[2097152]{0:T(1024)(128)(4,1)S(1)}, s32[]{:S(2)}) async-start(s8[10485760]{0:T(1024)(128)(4,1)} %bitcast.338), calls=%async_computation.13 | async-start | bytes 4194304 | tf_op jit(solution)/shard_map/while
  705.9 75.1 %reduce-scatter.9.cloned.1.call-start = ((), (), s32[]{:S(2)}) async-start(), calls=%async_computation.6 | async-start | bytes 1179648 | tf_op jit(solution)/shard_map/reduce_scatter | solution.py:201
  713.1 88.8 %reduce-scatter.11.cloned.1.call-start = ((), (), s32[]{:S(2)}) async-start(), calls=%async_computation.7 | async-start | bytes 1179648 | tf_op jit(solution)/shard_map/reduce_scatter | solution.py:202
  724.1 124.5 %all-reduce.29.cloned.1.call-start = ((), (), s32[]{:S(2)}) async-start(), calls=%async_computation.8 | async-start | bytes 140288 | tf_op jit(solution)/shard_map/psum | solution.py:214
  775.8 27.6 %copy-start.116 = (f32[256]{0:T(256)S(1)}, f32[256]{0:T(256)}, u32[]{:S(2)}) copy-start(f32[256]{0:T(256)} %convert_element_type.303) | copy-start | bytes 3076
  775.8 120.3 %all-reduce.31.cloned.1.call-start = ((), (), s32[]{:S(2)}) async-start(), calls=%async_computation.9 | async-start | bytes 262144 | tf_op jit(solution)/shard_map/psum | solution.py:214
  (157 other events, 598.4 us)
Sparse Core Ops, SparseCore 0:
  535.2 28.8 reduce-scatter.6
  706.0 30.0 reduce-scatter.4
  738.4 30.7 reduce-scatter.8
  771.3 30.4 reduce-scatter.10
  806.9 41.6 all-reduce.28
  852.1 43.8 all-reduce.30
where the time goes:
time: 916 us; the launch traced here: 906 us
  matrix products  252 us (28%)
  local copies, waits for them, and re-layouts  251 us (27%)
  other arithmetic  124 us (14%)
  blocking collectives  114 us (12%)
  waiting for transfers between devices  90.8 us (10%)
  loops' own time  55.1 us (6%)
  between operations  18.2 us (2%)
    psum x2, waiting for transfers between devices, reduce_grads(): lax.psum(shortened(owned_sum), 'dp')  71.4 us
    dot_general x8, matrix products, one_block(): jnp.einsum('qhd,khd->hqk', grad_tile, value_tile, preferred_element_type=...  57.1 us
    unnamed x2, blocking collectives  44.7 us
    dot_general x8, matrix products, one_block(): jnp.einsum('hqk,khd->qhd', prob_low, value_tile, preferred_element_type=j...  35.4 us
    dot_general x8, matrix products, product_nt(): lax.dot_general(left_op, right_op, (((1,), (1,)), ((), ())), preferred_el...  34.1 us
    dot_general x16, matrix products, masked_scores(): jnp.einsum('qhd,khd->hqk', query_tile, key_tile, preferred_element_type=j...  32.5 us
    unnamed x266, local copies, waits for them, and re-layouts  32.5 us
    another operation x2, loops' own time, attend_backward(): lax.scan(one_block, (zero_pad, zero_pad), jnp.arange(row_count * per_row,...  28.3 us
  transfers between devices with their start and end apart: 6, of which 3 were waited for; matrix products, arithmetic and copies ran while one was open for 24% of the time, Pallas kernels for 0%

commit v1 on v0

v1 whole, which is shorter than its diff:
```python
import math
from functools import partial

import jax
import jax.numpy as jnp
from jax import lax
from jax.experimental import pallas as pl
from jax.experimental.pallas import tpu as pltpu
from jax.sharding import PartitionSpec as P

HEADS = 8
HD = 32
CHUNK = 256
BLOCK = 128
PAIRS = HEADS // 2

norm_eps = 1e-05
masked_score = -1e30
score_scale = HD ** (-0.5)
exp2_scale = score_scale * math.log2(math.e)
gelu_c0 = math.sqrt(2.0 / math.pi)
gelu_c1 = 0.044715 * gelu_c0

f32 = jnp.float32
bf16 = jnp.bfloat16

(
    Q_BIAS,
    V_BIAS,
    OUT_BIAS,
    DOWN_BIAS,
    ATTN_GAIN,
    ATTN_SHIFT,
    MLP_GAIN,
    MLP_SHIFT,
    UP_BIAS,
) = range(9)


def mm(left_op, right_op):
    return lax.dot_general(
        left_op, right_op, (((1,), (0,)), ((), ())), preferred_element_type=f32
    )


def mm_nt(left_op, right_op):
    return lax.dot_general(
        left_op, right_op, (((1,), (1,)), ((), ())), preferred_element_type=f32
    )


def identity(size):
    rows = lax.broadcasted_iota(jnp.int32, (size, size), 0)
    cols = lax.broadcasted_iota(jnp.int32, (size, size), 1)
    return jnp.where(rows == cols, 1.0, 0.0).astype(bf16)


def flipped(block):
    return mm_nt(identity(block.shape[1]), block).astype(bf16)


def half(index):
    return slice(index * BLOCK, (index + 1) * BLOCK)


def spread(column):
    return jnp.broadcast_to(column, (column.shape[0], BLOCK))


def row_sum(values):
    return jnp.sum(values, axis=0, keepdims=True)


def norm_forward(values, gain, shift):
    scale = 1.0 / values.shape[0]
    centre = values - row_sum(values) * scale
    inverse = lax.rsqrt(row_sum(centre * centre) * scale + norm_eps)
    unit = centre * inverse
    return unit, inverse, unit * gain + shift


def norm_backward(grad_normed, unit, inverse, gain):
    scale = 1.0 / unit.shape[0]
    scaled = grad_normed * gain
    gain_term = grad_normed * unit
    mean_scaled = row_sum(scaled) * scale
    mean_unit = row_sum(gain_term * gain) * scale
    return inverse * (scaled - mean_scaled - unit * mean_unit), gain_term


def below_mask():
    key_at = lax.broadcasted_iota(jnp.int32, (BLOCK, BLOCK), 0)
    query_at = lax.broadcasted_iota(jnp.int32, (BLOCK, BLOCK), 1)
    return key_at <= query_at, key_at == query_at


def stack(side, pair):
    base = (side * PAIRS + pair) * BLOCK
    return slice(base, base + BLOCK)


def twice(values):
    return jnp.concatenate([values, values], axis=1)


def set_pairs(dest, source, lanes):
    for pair in range(PAIRS):
        base = 64 * (pair % 2)
        for side in range(2):
            dest[pair, base + HD * side : base + HD * (side + 1), half(side)] = source[
                64 * pair + HD * side : 64 * pair + HD * (side + 1), lanes
            ]


def front(u_ref, seg_ref, first, bcast, w_qkv, out, carry, q_pairs):
    unit_o, inv_o, normed_o, qk_o, vtok_o, probs_o, context_o, v_s, ktok_s = out
    kprev, vprev, segprev = carry
    for side in range(2):
        unit, inverse, normed = norm_forward(
            u_ref[:, half(side)], bcast[ATTN_GAIN], bcast[ATTN_SHIFT]
        )
        unit_o[:, half(side)] = unit.astype(bf16)
        inv_o[:, half(side)] = inverse
        normed_o[:, half(side)] = normed.astype(bf16)
    normed = normed_o[...]
    model = w_qkv.shape[1]
    for part in range(3):
        rows = mm(w_qkv[model * part : model * (part + 1), :], normed)
        if part == 0:
            qk_o[:model, :] = (rows + twice(bcast[Q_BIAS])).astype(bf16)
        elif part == 1:
            qk_o[model:, :] = rows.astype(bf16)
        else:
            v_s[...] = (rows + twice(bcast[V_BIAS])).astype(bf16)
    eye = identity(model)
    ktok_s[...] = mm_nt(eye, qk_o[model:, :]).astype(bf16)
    vtok_o[...] = mm_nt(eye, v_s[...]).astype(bf16)

    @pl.when(first)
    def _():
        segprev[...] = jnp.full(segprev.shape, -2.0, f32)

    below, diagonal = below_mask()
    below2 = twice(below)
    for side in range(2):
        lanes = half(side)
        seg_row = seg_ref[:, lanes].astype(f32)
        seg_col = jnp.transpose(jnp.broadcast_to(seg_row, (BLOCK, BLOCK)))
        seg_key = jnp.where(below, seg_col, segprev[...])
        segprev[...] = seg_col
        allowed = ((seg_key == seg_row) & (seg_row >= 0)) | diagonal
        bias = twice(jnp.where(allowed, 0.0, masked_score))
        set_pairs(q_pairs.at[side], qk_o, lanes)
        if side == 0:
            key_win = jnp.concatenate([kprev[...], ktok_s[:BLOCK, :]], axis=0)
            value_win = jnp.concatenate([vprev[...], v_s[:, :BLOCK]], axis=1)
        else:
            key_win = ktok_s[...]
            value_win = v_s[...]
        for pair in range(PAIRS):
            group = pair // 2
            scores = mm(key_win[:, half(group)], q_pairs[side, pair])
            folded = jnp.where(below2, scores[BLOCK:], scores[:BLOCK]) * exp2_scale + bias
            top = jnp.max(folded, axis=0, keepdims=True)
            weights = jnp.exp2(folded - top)
            probs = (weights * (1.0 / row_sum(weights))).astype(bf16)
            probs_o[stack(side, pair), :] = probs
            zero = jnp.zeros_like(probs)
            window = jnp.concatenate(
                [jnp.where(below2, zero, probs), jnp.where(below2, probs, zero)], axis=0
            )
            both = mm(value_win[64 * pair : 64 * (pair + 1), :], window)
            context_o[64 * pair : 64 * pair + HD, lanes] = both[:HD, :BLOCK].astype(bf16)
            context_o[64 * pair + HD : 64 * (pair + 1), lanes] = both[HD:, BLOCK:].astype(bf16)
    kprev[...] = ktok_s[BLOCK:, :]
    vprev[...] = v_s[:, BLOCK:]


def feed_forward(u_ref, m_ref, h_ref, context, bcast, up_bias, w_out, w_up, w_down, out):
    unit_o, inv_o, normed_o, hidden_o, slope_o = out
    mixed = mm(w_out[...], context)
    for side in range(2):
        lanes = half(side)
        after = u_ref[:, lanes] + (mixed[:, lanes] + bcast[OUT_BIAS])
        m_ref[:, lanes] = after
        unit, inverse, normed = norm_forward(after, bcast[MLP_GAIN], bcast[MLP_SHIFT])
        unit_o[:, lanes] = unit.astype(bf16)
        inv_o[:, lanes] = inverse
        normed_o[:, lanes] = normed.astype(bf16)
    normed = normed_o[...]
    ff = w_up.shape[0]
    total = None
    for part in range(ff // CHUNK):
        rows = slice(part * CHUNK, (part + 1) * CHUNK)
        pre = mm(w_up[rows, :], normed)
        for side in range(2):
            lanes = half(side)
            z = pre[:, lanes] + up_bias[rows, :]
            z2 = z * z
            gate = 0.5 * jnp.tanh(z * (gelu_c0 + gelu_c1 * z2)) + 0.5
            act = z * gate
            slope = gate + (act * (1.0 - gate)) * (2.0 * gelu_c0 + 6.0 * gelu_c1 * z2)
            hidden_o[rows, lanes] = act.astype(bf16)
            slope_o[rows, lanes] = slope.astype(bf16)
        term = mm(w_down[:, rows], hidden_o[rows, :])
        total = term if total is None else total + term
    for side in range(2):
        lanes = half(side)
        h_ref[:, lanes] = m_ref[:, lanes] + (total[:, lanes] + bcast[DOWN_BIAS])


def back_feed_forward(g_ref, dm_ref, saved, bcast, weights, sums, dy_s, dz_s, db_s, do_ref):
    unit, inverse, normed, hidden, slope = saved
    w_down_n, w_up_n = weights
    sum_down, sum_up, sum_up_bias, sum_vec = sums
    for side in range(2):
        lanes = half(side)
        grad = g_ref[:, lanes]
        sum_vec[DOWN_BIAS] += grad
        dy_s[:, lanes] = grad.astype(bf16)
    dy = dy_s[...]
    ff = w_down_n.shape[0]
    total = None
    for part in range(ff // CHUNK):
        rows = slice(part * CHUNK, (part + 1) * CHUNK)
        grad_hidden = mm(w_down_n[rows, :], dy)
        for side in range(2):
            lanes = half(side)
            dz = grad_hidden[:, lanes] * slope[rows, lanes].astype(f32)
            sum_up_bias[rows, :] += dz
            dz_s[rows, lanes] = dz.astype(bf16)
        term = mm(w_up_n[:, rows], dz_s[rows, :])
        total = term if total is None else total + term
    sum_down[...] += mm_nt(hidden[...], dy)
    sum_up[...] += mm_nt(dz_s[...], normed[...])
    for side in range(2):
        lanes = half(side)
        grad_normed = total[:, lanes]
        back, gain_term = norm_backward(
            grad_normed, unit[:, lanes].astype(f32), inverse[:, lanes], bcast[MLP_GAIN]
        )
        sum_vec[MLP_GAIN] += gain_term
        sum_vec[MLP_SHIFT] += grad_normed
        dm = g_ref[:, lanes] + back
        dm_ref[:, lanes] = dm
        sum_vec[OUT_BIAS] += dm
        do_ref[:, lanes] = dm.astype(bf16)


def back_out(do_ref, context, w_out_n, sum_out, dc_ref):
    grad = do_ref[...]
    sum_out[...] += mm_nt(grad, context[...])
    dc_ref[...] = mm(w_out_n[...], grad).astype(bf16)


def back_attention(dc_ref, context, qk, kt_prev, vtok, vtok_prev, probs_ref, pairs, sums, carry, dqkv):
    q_pairs, c_pairs = pairs
    dk_carry, dv_carry = carry
    model = vtok.shape[1]
    below, _ = below_mask()
    below2 = twice(below)
    for side in (1, 0):
        lanes = half(side)
        set_pairs(q_pairs.at[side], qk, lanes)
        set_pairs(c_pairs.at[side], dc_ref, lanes)
        weighted = dc_ref[:, lanes].astype(f32) * context[:, lanes].astype(f32)
        if side == 1:
            key_win = qk[model:, :]
            value_win = vtok[...]
        else:
            key_win = jnp.concatenate([kt_prev[...], qk[model:, :BLOCK]], axis=1)
            value_win = jnp.concatenate([vtok_prev[...], vtok[:BLOCK, :]], axis=0)
        for pair in range(PAIRS):
            group = pair // 2
            base = 64 * (pair % 2)
            rows = slice(64 * pair, 64 * (pair + 1))
            grad_probs = mm(value_win[:, half(group)], c_pairs[side, pair])
            folded = jnp.where(below2, grad_probs[BLOCK:], grad_probs[:BLOCK])
            delta = jnp.concatenate(
                [
                    row_sum(weighted[64 * pair : 64 * pair + HD]),
                    row_sum(weighted[64 * pair + HD : 64 * (pair + 1)]),
                ],
                axis=1,
            )
            probs = probs_ref[stack(side, pair), :]
            grad_scores = (probs.astype(f32) * (folded - delta)).astype(bf16)
            zero = jnp.zeros_like(probs)
            prob_win = jnp.concatenate(
                [jnp.where(below2, zero, probs), jnp.where(below2, probs, zero)], axis=0
            )
            grad_win = jnp.concatenate(
                [jnp.where(below2, zero, grad_scores), jnp.where(below2, grad_scores, zero)],
                axis=0,
            )
            dq = mm(key_win[rows, :], grad_win) * score_scale
            dqkv[64 * pair : 64 * pair + HD, lanes] = dq[:HD, :BLOCK].astype(bf16)
            dqkv[64 * pair + HD : 64 * (pair + 1), lanes] = dq[HD:, BLOCK:].astype(bf16)
            dk = mm_nt(q_pairs[side, pair, base : base + 64, :], grad_win) * score_scale
            dv = mm_nt(c_pairs[side, pair, base : base + 64, :], prob_win)
            krows = slice(model + 64 * pair, model + 64 * (pair + 1))
            vrows = slice(2 * model + 64 * pair, 2 * model + 64 * (pair + 1))
            dqkv[krows, lanes] = (dk[:, BLOCK:] + dk_carry[rows, :]).astype(bf16)
            dqkv[vrows, lanes] = (dv[:, BLOCK:] + dv_carry[rows, :]).astype(bf16)
            dk_carry[rows, :] = dk[:, :BLOCK]
            dv_carry[rows, :] = dv[:, :BLOCK]


def back_front(dm_ref, dqkv, unit, inverse, normed, bcast, w_qkv_n, sum_qkv, sum_vec, du_ref):
    grads = dqkv[...]
    model = dm_ref.shape[0]
    sum_qkv[...] += mm_nt(grads, normed[...])
    grad_normed_all = mm(w_qkv_n[...], grads)
    for side in range(2):
        lanes = half(side)
        sum_vec[Q_BIAS] += dqkv[:model, lanes].astype(f32)
        sum_vec[V_BIAS] += dqkv[2 * model :, lanes].astype(f32)
        grad_normed = grad_normed_all[:, lanes]
        back, gain_term = norm_backward(
            grad_normed, unit[:, lanes].astype(f32), inverse[:, lanes], bcast[ATTN_GAIN]
        )
        sum_vec[ATTN_GAIN] += gain_term
        sum_vec[ATTN_SHIFT] += grad_normed
        du_ref[:, lanes] = dm_ref[:, lanes] + back


def unpack_first(packed, w_qkv, vec):
    owners, _, model = packed.shape
    rows = 3 * model // owners
    for owner in range(owners):
        w_qkv[rows * owner : rows * (owner + 1), :] = packed[owner, :rows, :]
        vec[32 * owner : 32 * (owner + 1), :] = packed[owner, rows:, :BLOCK].astype(f32)


def unpack_second(packed, w_out, w_up_n, w_down):
    owners = packed.shape[0]
    for owner in range(owners):
        rows = slice(32 * owner, 32 * (owner + 1))
        w_out[rows, :] = packed[owner, :32, :]
        for side in range(2):
            w_up_n[half(side), half(owner)] = packed[owner, 32:160, half(side)]
        for part in range(4):
            w_down[rows, part * CHUNK : (part + 1) * CHUNK] = packed[
                owner, 160 + 32 * part : 192 + 32 * part, :
            ]


def spread_vectors(vec, bcast, which):
    values = vec[...]
    for index in which:
        bcast[index] = spread(values[:, index : index + 1])


def token_sum(left_tokens, right_tokens, dest):
    eye = identity(left_tokens.shape[1])
    dest[...] = mm_nt(eye, left_tokens) + mm_nt(eye, right_tokens)


def kernel_one(
    rows_chunks, x, inj, seg, first_weights,
    u_o, unit_o, inv_o, normed_o, qk_o, vtok_o, probs_o, context_o,
    w_qkv, vec, bcast, v_s, ktok_s, kprev, vprev, segprev, q_pairs,
):
    step = pl.program_id(0)

    @pl.when(step == 0)
    def _():
        unpack_first(first_weights, w_qkv, vec)
        spread_vectors(vec, bcast, (Q_BIAS, V_BIAS, ATTN_GAIN, ATTN_SHIFT))
        kprev[...] = jnp.zeros_like(kprev)
        vprev[...] = jnp.zeros_like(vprev)
        q_pairs[...] = jnp.zeros_like(q_pairs)

    token_sum(x[...], inj[...], u_o.at[0])
    out = [r.at[0] for r in (unit_o, inv_o, normed_o, qk_o, vtok_o, probs_o, context_o)]
    front(
        u_o.at[0], seg.at[0], lax.rem(step, rows_chunks) == 0, bcast, w_qkv,
        out + [v_s, ktok_s], (kprev, vprev, segprev), q_pairs,
    )


def kernel_two(
    rows_chunks, chunks,
    u1, c1, inj, cot, seg, first_weights, second_weights,
    result_o, dm_o, dc_o, du_o, grads_o, sum_qkv_o, vec_o,
    w_qkv, vec, w_out, w_up_n, w_down, bcast, up_bias, w_up, w_down_n, w_out_n, w_qkv_n,
    u_s, m_s, h_s, g_s, v_s, ktok_s, kprev, vprev, segprev, q_pairs, c_pairs,
    unit_m1, inv_m1, norm_m1, hid1, slope1,
    unit2, inv2, norm2, qk2, vtok2, probs2, ctx2,
    unit_m2, inv_m2, norm_m2, hid2, slope2,
    dy_s, dz_s, do_s, dc_s, dqkv_s, dk_carry, dv_carry,
    sum_down, sum_up, sum_out, sum_up_bias, sum_vec, pcopy,
):
    step = pl.program_id(0)
    model = w_out.shape[0]
    ff = w_up.shape[0]

    @pl.when(step == 0)
    def _():
        unpack_first(first_weights, w_qkv, vec)
        unpack_second(second_weights, w_out, w_up_n, w_down)
        spread_vectors(vec, bcast, range(8))
        values = vec[...]
        for owner in range(ff // BLOCK):
            for col in range(4):
                up_bias[BLOCK * owner + 32 * col : BLOCK * owner + 32 * (col + 1), :] = spread(
                    values[32 * owner : 32 * (owner + 1), UP_BIAS + col : UP_BIAS + col + 1]
                )
        for part in range(ff // CHUNK):
            rows = slice(part * CHUNK, (part + 1) * CHUNK)
            w_up[rows, :] = flipped(w_up_n[:, rows])
            w_down_n[rows, :] = flipped(w_down[:, rows])
        w_out_n[...] = flipped(w_out[...])
        for part in range(3):
            rows = slice(part * model, (part + 1) * model)
            w_qkv_n[:, rows] = flipped(w_qkv[rows, :])
        for ref in (kprev, vprev, q_pairs, c_pairs, dk_carry, dv_carry,
                    sum_down, sum_up, sum_out, sum_up_bias, sum_vec):
            ref[...] = jnp.zeros_like(ref)
        sum_qkv_o[...] = jnp.zeros_like(sum_qkv_o)

    @pl.when(step < chunks)
    def _():
        i = step
        feed_forward(
            u1.at[0], m_s, h_s, c1[0], bcast, up_bias, w_out, w_up, w_down,
            [r.at[i] for r in (unit_m1, inv_m1, norm_m1, hid1, slope1)],
        )
        u_s[...] = h_s[...] + mm_nt(identity(model), inj[...])
        out = [r.at[i] for r in (unit2, inv2, norm2, qk2, vtok2, probs2, ctx2)]
        front(
            u_s, seg.at[0], lax.rem(step, rows_chunks) == 0, bcast, w_qkv,
            out + [v_s, ktok_s], (kprev, vprev, segprev), q_pairs,
        )
        feed_forward(
            u_s, m_s, h_s, ctx2[i], bcast, up_bias, w_out, w_up, w_down,
            [r.at[i] for r in (unit_m2, inv_m2, norm_m2, hid2, slope2)],
        )
        result_o[...] = mm_nt(identity(CHUNK), h_s[...].astype(bf16)).astype(bf16)

    @pl.when(step >= chunks)
    def _():
        i = 2 * chunks - 1 - step
        before = jnp.maximum(i - 1, 0)
        g_s[...] = mm_nt(identity(model), cot[...])
        pcopy[...] = probs2[i]
        sums = (sum_down, sum_up, sum_up_bias, sum_vec)
        back_feed_forward(
            g_s, m_s, [r.at[i] for r in (unit_m2, inv_m2, norm_m2, hid2, slope2)],
            bcast, (w_down_n, w_up_n), sums, dy_s, dz_s, None, do_s,
        )
        back_out(do_s, ctx2.at[i], w_out_n, sum_out, dc_s)
        back_attention(
            dc_s, ctx2.at[i], qk2.at[i], qk2.at[before, model:, BLOCK:], vtok2.at[i],
            vtok2.at[before, BLOCK:, :], pcopy, (q_pairs, c_pairs), None,
            (dk_carry, dv_carry), dqkv_s,
        )
        back_front(
            m_s, dqkv_s, unit2.at[i], inv2.at[i], norm2.at[i], bcast, w_qkv_n,
            sum_qkv_o, sum_vec, g_s,
        )
        du_o[0] = g_s[...]
        back_feed_forward(
            g_s, dm_o.at[0], [r.at[i] for r in (unit_m1, inv_m1, norm_m1, hid1, slope1)],
            bcast, (w_down_n, w_up_n), sums, dy_s, dz_s, None, do_s,
        )
        back_out(do_s, c1.at[0], w_out_n, sum_out, dc_o.at[0])

    @pl.when(step == 2 * chunks - 1)
    def _():
        owners = grads_o.shape[0]
        for part in range(ff // CHUNK):
            rows = slice(part * CHUNK, (part + 1) * CHUNK)
            up_block = flipped(sum_up[rows, :].astype(bf16))
            for within in range(2):
                for side in range(2):
                    grads_o[2 * part + within, 32:160, half(side)] = up_block[
                        half(side), half(within)
                    ]
            down_block = flipped(sum_down[rows, :].astype(bf16))
            for owner in range(owners):
                grads_o[owner, 160 + 32 * part : 192 + 32 * part, :] = down_block[
                    32 * owner : 32 * (owner + 1), :
                ]
        for owner in range(owners):
            grads_o[owner, :32, :] = sum_out[32 * owner : 32 * (owner + 1), :].astype(bf16)
        vec_o[...] = jnp.zeros_like(vec_o)
        for index in range(8):
            vec_o[:, index : index + 1] = jnp.sum(sum_vec[index], axis=1, keepdims=True)
        for owner in range(ff // BLOCK):
            for col in range(4):
                vec_o[32 * owner : 32 * (owner + 1), UP_BIAS + col : UP_BIAS + col + 1] = jnp.sum(
                    sum_up_bias[BLOCK * owner + 32 * col : BLOCK * owner + 32 * (col + 1), :],
                    axis=1, keepdims=True,
                )


def kernel_three(
    chunks,
    unit, inv, normed, qk, kt_prev, vtok, vtok_prev, probs, ctx, dm, dc, du2, first_weights, sum_qkv_i, vec_i,
    gin_o, ginj_o, grads_o,
    w_qkv, vec, bcast, w_qkv_n, q_pairs, c_pairs, dqkv_s, dk_carry, dv_carry, g_s, sum_qkv, sum_vec,
):
    step = pl.program_id(0)
    model = w_qkv.shape[1]
    owners = grads_o.shape[0]

    @pl.when(step == 0)
    def _():
        unpack_first(first_weights, w_qkv, vec)
        spread_vectors(vec, bcast, (ATTN_GAIN,))
        for part in range(3):
            rows = slice(part * model, (part + 1) * model)
            w_qkv_n[:, rows] = flipped(w_qkv[rows, :])
        for ref in (q_pairs, c_pairs, dk_carry, dv_carry, sum_vec):
            ref[...] = jnp.zeros_like(ref)
        sum_qkv[...] = sum_qkv_i[...]

    back_attention(
        dc.at[0], ctx.at[0], qk.at[0], kt_prev.at[0], vtok.at[0], vtok_prev.at[0], probs.at[0],
        (q_pairs, c_pairs), None, (dk_carry, dv_carry), dqkv_s,
    )
    back_front(
        dm.at[0], dqkv_s, unit.at[0], inv.at[0], normed.at[0], bcast, w_qkv_n,
        sum_qkv, sum_vec, g_s,
    )
    eye = identity(CHUNK)
    gin_o[...] = mm_nt(eye, g_s[...].astype(bf16)).astype(bf16)
    ginj_o[...] = mm_nt(eye, (g_s[...] + du2[0]).astype(bf16)).astype(bf16)

    @pl.when(step == chunks - 1)
    def _():
        rows = 3 * model // owners
        vec[...] = vec_i[...]
        for index in (Q_BIAS, V_BIAS, ATTN_GAIN, ATTN_SHIFT):
            vec[:, index : index + 1] += jnp.sum(sum_vec[index], axis=1, keepdims=True)
        for owner in range(owners):
            grads_o[owner, :rows, :] = sum_qkv[rows * owner : rows * (owner + 1), :].astype(bf16)
            grads_o[owner, rows:, :] = twice(vec[32 * owner : 32 * (owner + 1), :].astype(bf16))


def whole(array):
    zeros = (0,) * len(array.shape)
    return pl.BlockSpec(array.shape, lambda j: zeros)


def shape(dims, kind):
    return jax.ShapeDtypeStruct(dims, kind)


def vmem(dims, kind):
    return pltpu.VMEM(dims, kind)


params = pltpu.CompilerParams(vmem_limit_bytes=62 * 1024 * 1024)


def run_one(x, inj, seg, first_weights, per_row):
    tokens, model = x.shape
    chunks = tokens // CHUNK

    def lead(dims):
        return pl.BlockSpec((1,) + dims, lambda j: (j,) + (0,) * len(dims))

    token_spec = pl.BlockSpec((CHUNK, model), lambda j: (j, 0))
    outs = [
        ((model, CHUNK), f32),
        ((model, CHUNK), bf16),
        ((1, CHUNK), f32),
        ((model, CHUNK), bf16),
        ((2 * model, CHUNK), bf16),
        ((CHUNK, model), bf16),
        ((2 * PAIRS * BLOCK, CHUNK), bf16),
        ((model, CHUNK), bf16),
    ]
    return pl.pallas_call(
        partial(kernel_one, per_row),
        grid=(chunks,),
        in_specs=[token_spec, token_spec, lead((1, CHUNK)), whole(first_weights)],
        out_specs=[lead(dims) for dims, _ in outs],
        out_shape=[shape((chunks,) + dims, kind) for dims, kind in outs],
        scratch_shapes=[
            vmem((3 * model, model), bf16),
            vmem((model, BLOCK), f32),
            vmem((8, model, BLOCK), f32),
            vmem((model, CHUNK), bf16),
            vmem((CHUNK, model), bf16),
            vmem((BLOCK, model), bf16),
            vmem((model, BLOCK), bf16),
            vmem((BLOCK, BLOCK), f32),
            vmem((2, PAIRS, BLOCK, CHUNK), bf16),
        ],
        compiler_params=params,
        name="attend_first",
    )(x, inj, seg, first_weights)


def run_two(u1, c1, inj, cot, seg, first_weights, second_weights, per_row):
    chunks, model, _ = u1.shape
    tokens = chunks * CHUNK
    owners = second_weights.shape[0]
    ff = BLOCK * owners
    last = chunks - 1

    def up_then_hold(j):
        return jnp.minimum(j, last)

    def up_then_down(j):
        return jnp.where(j < chunks, j, 2 * chunks - 1 - j)

    def hold_then_down(j):
        return jnp.where(j < chunks, last, 2 * chunks - 1 - j)

    def lead(dims, order):
        return pl.BlockSpec((1,) + dims, lambda j: (order(j),) + (0,) * len(dims))

    def tok(order):
        return pl.BlockSpec((CHUNK, model), lambda j: (order(j), 0))

    square = (model, CHUNK)
    mlp_saved = [
        vmem((chunks,) + square, bf16),
        vmem((chunks, 1, CHUNK), f32),
        vmem((chunks,) + square, bf16),
        vmem((chunks, ff, CHUNK), bf16),
        vmem((chunks, ff, CHUNK), bf16),
    ]
    return pl.pallas_call(
        partial(kernel_two, per_row, chunks),
        grid=(2 * chunks,),
        in_specs=[
            lead(square, up_then_hold),
            lead(square, up_then_down),
            tok(up_then_hold),
            tok(hold_then_down),
            lead((1, CHUNK), up_then_hold),
            whole(first_weights),
            whole(second_weights),
        ],
        out_specs=[
            tok(up_then_hold),
            lead(square, hold_then_down),
            lead(square, hold_then_down),
            lead(square, hold_then_down),
            whole(second_weights),
            pl.BlockSpec((3 * model, model), lambda j: (0, 0)),
            pl.BlockSpec((model, BLOCK), lambda j: (0, 0)),
        ],
        out_shape=[
            shape((tokens, model), bf16),
            shape((chunks,) + square, f32),
            shape((chunks,) + square, bf16),
            shape((chunks,) + square, f32),
            shape(second_weights.shape, bf16),
            shape((3 * model, model), f32),
            shape((model, BLOCK), f32),
        ],
        scratch_shapes=[
            vmem((3 * model, model), bf16),
            vmem((model, BLOCK), f32),
            vmem((model, model), bf16),
            vmem((model, ff), bf16),
            vmem((model, ff), bf16),
            vmem((8, model, BLOCK), f32),
            vmem((ff, BLOCK), f32),
            vmem((ff, model), bf16),
            vmem((ff, model), bf16),
            vmem((model, model), bf16),
            vmem((model, 3 * model), bf16),
            vmem(square, f32),
            vmem(square, f32),
            vmem(square, f32),
            vmem(square, f32),
            vmem(square, bf16),
            vmem((CHUNK, model), bf16),
            vmem((BLOCK, model), bf16),
            vmem((model, BLOCK), bf16),
            vmem((BLOCK, BLOCK), f32),
            vmem((2, PAIRS, BLOCK, CHUNK), bf16),
            vmem((2, PAIRS, BLOCK, CHUNK), bf16),
        ]
        + mlp_saved
        + [
            vmem((chunks,) + square, bf16),
            vmem((chunks, 1, CHUNK), f32),
            vmem((chunks,) + square, bf16),
            vmem((chunks, 2 * model, CHUNK), bf16),
            vmem((chunks, CHUNK, model), bf16),
            vmem((chunks, 2 * PAIRS * BLOCK, CHUNK), bf16),
            vmem((chunks,) + square, bf16),
        ]
        + mlp_saved
        + [
            vmem(square, bf16),
            vmem((ff, CHUNK), bf16),
            vmem(square, bf16),
            vmem(square, bf16),
            vmem((3 * model, CHUNK), bf16),
            vmem((model, BLOCK), f32),
            vmem((model, BLOCK), f32),
            vmem((ff, model), f32),
            vmem((ff, model), f32),
            vmem((model, model), f32),
            vmem((ff, BLOCK), f32),
            vmem((8, model, BLOCK), f32),
            vmem((2 * PAIRS * BLOCK, CHUNK), bf16),
        ],
        compiler_params=params,
        name="middle",
    )(u1, c1, inj, cot, seg, first_weights, second_weights)


def run_three(saved, dm, dc, du2, first_weights, sum_qkv, vec_in):
    unit, inv, normed, qk, vtok, probs, ctx = saved
    chunks, model, _ = dm.shape
    tokens = chunks * CHUNK

    def at(j):
        return chunks - 1 - j

    def before(j):
        return jnp.maximum(chunks - 2 - j, 0)

    def lead(array):
        dims = array.shape[1:]
        return pl.BlockSpec((1,) + dims, lambda j: (at(j),) + (0,) * len(dims))

    tok = pl.BlockSpec((CHUNK, model), lambda j: (at(j), 0))
    return pl.pallas_call(
        partial(kernel_three, chunks),
        grid=(chunks,),
        in_specs=[
            lead(unit),
            lead(inv),
            lead(normed),
            lead(qk),
            pl.BlockSpec((1, model, BLOCK), lambda j: (before(j), 1, 1)),
            lead(vtok),
            pl.BlockSpec((1, BLOCK, model), lambda j: (before(j), 1, 0)),
            lead(probs),
            lead(ctx),
            lead(dm),
            lead(dc),
            lead(du2),
            whole(first_weights),
            whole(sum_qkv),
            whole(vec_in),
        ],
        out_specs=[
            tok,
            tok,
            whole(first_weights),
        ],
        out_shape=[
            shape((tokens, model), bf16),
            shape((tokens, model), bf16),
            shape(first_weights.shape, bf16),
        ],
        scratch_shapes=[
            vmem((3 * model, model), bf16),
            vmem((model, BLOCK), f32),
            vmem((8, model, BLOCK), f32),
            vmem((model, 3 * model), bf16),
            vmem((2, PAIRS, BLOCK, CHUNK), bf16),
            vmem((2, PAIRS, BLOCK, CHUNK), bf16),
            vmem((3 * model, CHUNK), bf16),
            vmem((model, BLOCK), f32),
            vmem((model, BLOCK), f32),
            vmem((model, CHUNK), f32),
            vmem((3 * model, model), f32),
            vmem((8, model, BLOCK), f32),
        ],
        compiler_params=params,
        name="attend_back",
    )(unit, inv, normed, qk, qk, vtok, vtok, probs, ctx, dm, dc, du2, first_weights, sum_qkv, vec_in)


OWNERS = 8


def pack_first(qkv_t, vectors):
    rows, model = qkv_t.shape
    count = rows // 96
    columns = [vector.reshape(count, 1, 32) for vector in vectors[:3] + vectors[4:]]
    columns.insert(8, vectors[3].reshape(count, 4, 32))
    block = jnp.concatenate(columns, axis=1).transpose(0, 2, 1)
    block = jnp.pad(block, ((0, 0), (0, 0), (0, model - block.shape[2])))
    return jnp.concatenate([qkv_t.reshape(count, 96, model), block], axis=1)


def unpack_vectors(block):
    columns = [block[:, :, index].reshape(-1) for index in range(8)]
    columns.insert(3, block[:, :, 8:12].transpose(0, 2, 1).reshape(-1))
    return columns


def pack_second(out_t, up, down_t):
    rows, model = out_t.shape
    count = rows // 32
    up_part = up.reshape(2, model // 2, count, 128).transpose(2, 1, 0, 3).reshape(count, 128, 256)
    down_part = down_t.reshape(count, 32, 4, 256).transpose(0, 2, 1, 3).reshape(count, 128, 256)
    return jnp.concatenate([out_t.reshape(count, 32, model), up_part, down_part], axis=1)


def unpack_second_grads(block):
    count, _, model = block.shape
    out_t = block[:, :32].reshape(count * 32, model)
    up = block[:, 32:160].reshape(count, 128, 2, 128).transpose(2, 1, 0, 3)
    down_t = block[:, 160:].reshape(count, 4, 32, 256).transpose(0, 2, 1, 3)
    return out_t, up.reshape(model, 128 * count), down_t.reshape(32 * count, 1024)


def exchange(block, axis, size, distance):
    return lax.ppermute(block, axis, [(k, k ^ distance) for k in range(size)])


def scatter_sum(parts):
    me = lax.axis_index("fsdp")
    total = lax.dynamic_index_in_dim(parts, me, 0, False).astype(f32)
    for distance in range(1, OWNERS):
        block = lax.dynamic_index_in_dim(parts, me ^ distance, 0, False)
        total = total + exchange(block, "fsdp", OWNERS, distance).astype(f32)
    groups = lax.all_gather(total.astype(bf16), "dp", axis=0)
    return jnp.sum(groups.astype(f32), axis=0)


def scatter_sum_any(full, axis):
    own = lax.psum_scatter(full, "fsdp", scatter_dimension=axis, tiled=True)
    return lax.psum(own, "dp")


def local(
    inputs,
    inject,
    segments,
    cotangent,
    qkv_weight,
    out_weight,
    up_weight,
    down_weight,
    *vectors,
):
    row_count, length, model = inputs.shape
    tokens = row_count * length
    chunks = tokens // CHUNK
    x = inputs.reshape(tokens, model)
    inj = inject.reshape(tokens, model)
    cot = cotangent.reshape(tokens, model)
    seg = segments.reshape(chunks, 1, CHUNK)
    per_row = length // CHUNK
    packed = out_weight.shape[1] * OWNERS == model
    if packed:
        first_own = pack_first(qkv_weight.T, vectors)[0]
        second_own = pack_second(out_weight.T, up_weight, down_weight.T)[0]
        first_weights = lax.all_gather(first_own, "fsdp", axis=0)
        second_weights = lax.all_gather(second_own, "fsdp", axis=0)
    else:

        def gathered(array, axis):
            return lax.all_gather(array, "fsdp", axis=axis, tiled=True)

        first_weights = pack_first(
            gathered(qkv_weight, 1).T, tuple(gathered(vector, 0) for vector in vectors)
        )
        second_weights = pack_second(
            gathered(out_weight, 1).T, gathered(up_weight, 1), gathered(down_weight, 1).T
        )
    u1, *saved = run_one(x, inj, seg, first_weights, per_row)
    result, dm, dc, du2, second_grads, sum_qkv, vec_mid = run_two(
        u1, saved[-1], inj, cot, seg, first_weights, second_weights, per_row
    )
    if packed:
        second_sum = scatter_sum(second_grads)
    grad_inputs, grad_inject, first_grads = run_three(
        saved, dm, dc, du2, first_weights, sum_qkv, vec_mid
    )
    if packed:
        first_sum = scatter_sum(first_grads)[None]
        out_t, up, down_t = unpack_second_grads(second_sum[None])
        weight_grads = (first_sum[0, :96].T, out_t.T, up, down_t.T)
        vector_grads = unpack_vectors(first_sum[:, 96:])
    else:
        first_all = first_grads.astype(f32)
        out_t, up, down_t = unpack_second_grads(second_grads.astype(f32))
        weight_grads = tuple(
            scatter_sum_any(grad, 1)
            for grad in (first_all[:, :96].reshape(3 * model, model).T, out_t.T, up, down_t.T)
        )
        vector_grads = [scatter_sum_any(grad, 0) for grad in unpack_vectors(first_all[:, 96:])]
    dims = inputs.shape
    return (
        result.reshape(dims),
        grad_inputs.reshape(dims),
        grad_inject.reshape(dims),
        *weight_grads,
        *vector_grads,
    )


def solution(mesh):
    placed = (
        P(("dp", "fsdp"), None, None),
        P(("dp", "fsdp"), None, None),
        P(("dp", "fsdp"), None),
        P(("dp", "fsdp"), None, None),
        P(None, "fsdp"),
        P(None, "fsdp"),
        P(None, "fsdp"),
        P(None, "fsdp"),
        P("fsdp"),
        P("fsdp"),
        P("fsdp"),
        P("fsdp"),
        P("fsdp"),
        P("fsdp"),
        P("fsdp"),
        P("fsdp"),
        P("fsdp"),
    )
    return jax.shard_map(
        local,
        mesh=mesh,
        in_specs=placed,
        out_specs=(
            P(("dp", "fsdp"), None, None),
            P(("dp", "fsdp"), None, None),
            P(("dp", "fsdp"), None, None),
            P(None, "fsdp"),
            P(None, "fsdp"),
            P(None, "fsdp"),
            P(None, "fsdp"),
            P("fsdp"),
            P("fsdp"),
            P("fsdp"),
            P("fsdp"),
            P("fsdp"),
            P("fsdp"),
            P("fsdp"),
            P("fsdp"),
            P("fsdp"),
        ),
        check_vma=False,
    )
```

time: 916 us -> 246 us (0.27)
  matrix products: 252 us -> 0 us
  local copies, waits for them, and re-layouts: 251 us -> 8.94 us
  Pallas kernels: 0 us -> 150 us
  other arithmetic: 124 us -> 3.37 us
  waiting for transfers between devices: 90.8 us -> 12.9 us
  blocking collectives: 114 us -> 37.9 us
  loops' own time: 55.1 us -> 0 us
  starting transfers between devices: 0.54 us -> 18.2 us
    dot_general x80 -> x0, matrix products: 252 us -> none  [the longest x8 57.1 us: one_block(): jnp.einsum('qhd,khd->hqk', grad_tile, value_tile, preferred_element_type=...]
    pallas_call x0 -> x3, Pallas kernels: none -> 150 us  [the longest x1 93.4 us: run_two(): pl.pallas_call(partial(kernel_two, per_row, chunks), grid=(2 * chunks,),...]
    dynamic_slice x136 -> x0, local copies, waits for them, and re-layouts: 109 us -> none  [the longest x16 17.8 us: one_block(): lax.dynamic_slice(key_grad_pad, corner, window) + key_part.reshape(window)]
    psum x2 -> x0, waiting for transfers between devices: 71.4 us -> none  [reduce_grads(): lax.psum(shortened(owned_sum), 'dp')]
    another operation x4 -> x0, loops' own time: 55.1 us -> none  [the longest x2 28.3 us: attend_backward(): lax.scan(one_block, (zero_pad, zero_pad), jnp.arange(row_count * per_row,...]
    convert_element_type x34 -> x2, other arithmetic: 51.8 us -> 1.07 us  [scatter_sum(): groups = lax.all_gather(total.astype(bf16), 'dp', axis=0)]
    dynamic_update_slice x56 -> x0, local copies, waits for them, and re-layouts: 48.2 us -> none  [the longest x16 27.9 us: one_block(): lax.dynamic_update_slice(value_grad_pad, lax.dynamic_slice(value_grad_pad...]
    unnamed x2 -> x0, blocking collectives: 44.7 us -> none
  transfers between devices with their start and end apart: 6 -> 15, of which waited for: 3 -> 4; matrix products, arithmetic and copies ran while one was open for 24% -> 2% of each run, Pallas kernels for 0% -> 12%
where the time goes in v1:
time: 246 us; the launch traced here: 245 us
  Pallas kernels  150 us (61%)
  blocking collectives  37.9 us (15%)
  starting transfers between devices  18.2 us (7%)
  between operations  14.2 us (6%)
  waiting for transfers between devices  12.9 us (5%)
  local copies, waits for them, and re-layouts  8.94 us (4%)
  other arithmetic  3.37 us (1%)
    pallas_call x1, Pallas kernels, run_two(): pl.pallas_call(partial(kernel_two, per_row, chunks), grid=(2 * chunks,),...  93.4 us
    pallas_call x1, Pallas kernels, run_one(): pl.pallas_call(partial(kernel_one, per_row), grid=(chunks,), in_specs=[to...  29.7 us
    pallas_call x1, Pallas kernels, run_three(): pl.pallas_call(partial(kernel_three, chunks), grid=(chunks,), in_specs=[l...  26.8 us
    all_gather x2, blocking collectives, scatter_sum(): groups = lax.all_gather(total.astype(bf16), 'dp', axis=0)  19.1 us
    all_gather x1, blocking collectives, local(): first_weights = lax.all_gather(first_own, 'fsdp', axis=0)  18.9 us
    ppermute x14, starting transfers between devices, exchange(): return lax.ppermute(block, axis, [(k, k ^ distance) for k in range(size)])  18.1 us
    ppermute x14, waiting for transfers between devices, exchange(): return lax.ppermute(block, axis, [(k, k ^ distance) for k in range(size)])  12.9 us
  transfers between devices with their start and end apart: 15, of which 4 were waited for; matrix products, arithmetic and copies ran while one was open for 2% of the time, Pallas kernels for 12%

profile of v1, /device:TPU:0, one launch (start us, length us, event | category | flops | bytes accessed | tf_op | source)
XLA Modules:
  0.0 245.4 jit_solution(5109649062765352483)
XLA Ops:
  7.2 0.9 reshape.137
  8.1 0.9 copy.73
  9.1 1.4 pad_maximum_fusion
  11.3 0.8 concatenate.9
  12.2 0.8 fusion.15
  13.0 18.9 %all_gather.18.first_weights = bf16[8,128,256]{2,1,0:T(8,128)(2,1)} all-gather(bf16[1,128,256]{2,1,0:T(8,128)(2,1)S(1)} %fusion.15), channel_id=1, replica_groups=mesh['dp'=4,'fsdp'=8] {'fsdp'}, dimensions={0}, use_global_device_ids=true | all-gather | bytes 589824 | tf_op jit(solution)/shard_map/all_gather | solution.py:855
  31.9 29.7 %attend_first.1 = (f32[8,256,256]{2,1,0:T(8,128)}, bf16[8,256,256]{2,1,0:T(8,128)(2,1)}, f32[8,1,256]{2,1,0:T(1,128)}, bf16[8,256,256]{2,1,0:T(8,128)(2,1)}, bf1...) custom-call(bf16[2048,256]{1,0:T(8,128)(2,1)} %bitcast.104, ...), custom_call_target="tpu_custom_call" | custom-call | tf_op jit(solution)/shard_map/attend_first/pallas_call | solution.py:576
  61.6 93.4 %middle.1 = (bf16[2048,256]{1,0:T(8,128)(2,1)}, f32[8,256,256]{2,1,0:T(8,128)}, bf16[8,256,256]{2,1,0:T(8,128)(2,1)}, f32[8,256,256]{2,1,0:T(8,128)}, bf16[8,288...) custom-call(f32[8,256,256]{2,1,0:T(8,128)} %get-tuple-element.34.u1, ...), custom_call_target="tpu_custom_call" | custom-call | tf_op jit(solution)/shard_map/middle/pallas_call | solution.py:628
  155.0 26.8 %attend_back.1 = (bf16[2048,256]{1,0:T(8,128)(2,1)}, bf16[2048,256]{1,0:T(8,128)(2,1)}, bf16[8,128,256]{2,1,0:T(8,128)(2,1)}) custom-call(bf16[8,256,256]{2,1,0:T(8,128)(2,1)} %get-tuple-element.37.unit, f32[8,1,256]{2,1,0:T(1,128)} %get-tuple-element.38.inv, bf16[8,256,256]{2,1,0:T(8,128)(2,1)} %get-tuple-element.39.normed, ...), custom_call_target="tpu_custom_call" | custom-call | tf_op jit(solution)/shard_map/attend_back/pallas_call | solution.py:729
  181.8 1.1 dynamic-slice_bitcast_fusion.13
  183.3 1.2 collective-permute-start.1
  184.8 2.3 collective-permute-start.3
  187.7 3.3 %collective-permute-start.5 = (bf16[128,256]{1,0:T(8,128)(2,1)S(1)}, bf16[128,256]{1,0:T(8,128)(2,1)S(1)}, u32[]{:S(2)}, u32[]{:S(2)}) collective-permute-start(bf16[128,256]{1,0:T(8,128)(2,1)S(1)} %get-tuple-element.69), channel_id=1, source_target_pairs={{0,6},{1,7},{2,4},{3,5},{4,2},{5,3},{6,0},{7,1},{8,14},{9,15},{10,... | collective-permute-start | bytes 196616 | tf_op jit(solution)/shard_map/ppermute | solution.py:814
  191.7 2.3 collective-permute-start.11
  194.1 7.1 %collective-permute-done.4 = bf16[128,256]{1,0:T(8,128)(2,1)S(1)} collective-permute-done((bf16[128,256]{1,0:T(8,128)(2,1)S(1)}, bf16[128,256]{1,0:T(8,128)(2,1)S(1)}, u32[]{:S(2)}, u32[]{:S(2)}) %collective-permute-start.4) | collective-permute-done | bytes 65568 | tf_op jit(solution)/shard_map/ppermute | solution.py:814
  201.2 5.5 %collective-permute-start.12 = (bf16[288,256]{1,0:T(8,128)(2,1)S(1)}, bf16[288,256]{1,0:T(8,128)(2,1)S(1)}, u32[]{:S(2)}, u32[]{:S(2)}) collective-permute-start(bf16[288,256]{1,0:T(8,128)(2,1)S(1)} %get-tuple-element.62), channel_id=1, source_target_pairs={{0,6},{1,7},{2,4},{3,5},{4,2},{5,3},{6,0},{7,1},{8,14},{9,15},{10,... | collective-permute-start | bytes 442376 | tf_op jit(solution)/shard_map/ppermute | solution.py:814
  206.9 0.9 fusion.13
  207.8 8.8 %all-gather = bf16[512,256]{1,0:T(8,128)(2,1)S(1)} all-gather(bf16[128,256]{1,0:T(8,128)(2,1)S(1)} %fusion.13), channel_id=2, replica_groups=mesh['dp'=4,'fsdp'=8] {'dp'}, dimensions={0}, use_global_device_ids=true | all-gather | bytes 327680 | tf_op jit(solution)/shard_map/all_gather | solution.py:823
  217.3 1.4 collective-permute-start.8
  218.7 1.2 collective-permute-done.11
  220.6 0.8 slice_reduce_fusion
  221.4 1.6 collective-permute-done.8
  223.0 3.0 %collective-permute-done.9 = bf16[288,256]{1,0:T(8,128)(2,1)S(1)} collective-permute-done((bf16[288,256]{1,0:T(8,128)(2,1)S(1)}, bf16[288,256]{1,0:T(8,128)(2,1)S(1)}, u32[]{:S(2)}, u32[]{:S(2)}) %collective-permute-start.9) | collective-permute-done | bytes 147488 | tf_op jit(solution)/shard_map/ppermute | solution.py:814
  226.2 10.3 %all-gather.1 = bf16[1152,256]{1,0:T(8,128)(2,1)S(1)} all-gather(bf16[288,256]{1,0:T(8,128)(2,1)S(1)} %fusion.6), channel_id=3, replica_groups=mesh['dp'=4,'fsdp'=8] {'dp'}, dimensions={0}, use_global_device_ids=true | all-gather | bytes 737280 | tf_op jit(solution)/shard_map/all_gather | solution.py:823
  (40 shorter events, 6.8 us)
Async XLA Ops:
  7.2 54.4 %all-gather.4.cloned.1.call-start = ((), (), s32[]{:S(2)}) async-start(), calls=%async_computation | async-start | bytes 1327104 | tf_op jit(solution)/shard_map/all_gather | solution.py:856
  155.0 36.1 %copy-start = (bf16[8,288,256]{2,1,0:T(8,128)(2,1)S(1)}, bf16[8,288,256]{2,1,0:T(8,128)(2,1)}, u32[]{:S(2)}) copy-start(bf16[8,288,256]{2,1,0:T(8,128)(2,1)} %get-tuple-element.51) | copy-start | bytes 3538948
  182.9 4.8 %collective-permute-start = (bf16[128,256]{1,0:T(8,128)(2,1)S(1)}, bf16[128,256]{1,0:T(8,128)(2,1)S(1)}, u32[]{:S(2)}, u32[]{:S(2)}) collective-permute-start(bf16[128,256]{1,0:T(8,128)(2,1)S(1)} %get-tuple-element.67), channel_id=1, source_target_pairs={{0,1},{1,0},{2,3},{3,2},{4,5},{5,4},{6,7},{7,6},{8,9},{9,8},{10,11... | collective-permute-start | bytes 196616 | tf_op jit(solution)/shard_map/ppermute | solution.py:814
  183.3 7.7 %collective-permute-start.1 = (bf16[128,256]{1,0:T(8,128)(2,1)S(1)}, bf16[128,256]{1,0:T(8,128)(2,1)S(1)}, u32[]{:S(2)}, u32[]{:S(2)}) collective-permute-start(bf16[128,256]{1,0:T(8,128)(2,1)S(1)} %get-tuple-element.73), channel_id=1, source_target_pairs={{0,2},{1,3},{2,0},{3,1},{4,6},{5,7},{6,4},{7,5},{8,10},{9,11},{10,... | collective-permute-start | bytes 196616 | tf_op jit(solution)/shard_map/ppermute | solution.py:814
  184.5 6.6 %collective-permute-start.2 = (bf16[128,256]{1,0:T(8,128)(2,1)S(1)}, bf16[128,256]{1,0:T(8,128)(2,1)S(1)}, u32[]{:S(2)}, u32[]{:S(2)}) collective-permute-start(bf16[128,256]{1,0:T(8,128)(2,1)S(1)} %get-tuple-element.72), channel_id=1, source_target_pairs={{0,3},{1,2},{2,1},{3,0},{4,7},{5,6},{6,5},{7,4},{8,11},{9,10},{10,... | collective-permute-start | bytes 196616 | tf_op jit(solution)/shard_map/ppermute | solution.py:814
  184.8 6.9 %collective-permute-start.3 = (bf16[128,256]{1,0:T(8,128)(2,1)S(1)}, bf16[128,256]{1,0:T(8,128)(2,1)S(1)}, u32[]{:S(2)}, u32[]{:S(2)}) collective-permute-start(bf16[128,256]{1,0:T(8,128)(2,1)S(1)} %get-tuple-element.71), channel_id=1, source_target_pairs={{0,4},{1,5},{2,6},{3,7},{4,0},{5,1},{6,2},{7,3},{8,12},{9,13},{10,... | collective-permute-start | bytes 196616 | tf_op jit(solution)/shard_map/ppermute | solution.py:814
  187.2 14.0 %collective-permute-start.4 = (bf16[128,256]{1,0:T(8,128)(2,1)S(1)}, bf16[128,256]{1,0:T(8,128)(2,1)S(1)}, u32[]{:S(2)}, u32[]{:S(2)}) collective-permute-start(bf16[128,256]{1,0:T(8,128)(2,1)S(1)} %get-tuple-element.70), channel_id=1, source_target_pairs={{0,5},{1,4},{2,7},{3,6},{4,1},{5,0},{6,3},{7,2},{8,13},{9,12},{10,... | collective-permute-start | bytes 196616 | tf_op jit(solution)/shard_map/ppermute | solution.py:814
  187.7 19.0 %collective-permute-start.5 = (bf16[128,256]{1,0:T(8,128)(2,1)S(1)}, bf16[128,256]{1,0:T(8,128)(2,1)S(1)}, u32[]{:S(2)}, u32[]{:S(2)}) collective-permute-start(bf16[128,256]{1,0:T(8,128)(2,1)S(1)} %get-tuple-element.69), channel_id=1, source_target_pairs={{0,6},{1,7},{2,4},{3,5},{4,2},{5,3},{6,0},{7,1},{8,14},{9,15},{10,... | collective-permute-start | bytes 196616 | tf_op jit(solution)/shard_map/ppermute | solution.py:814
  191.0 15.7 %collective-permute-start.6 = (bf16[128,256]{1,0:T(8,128)(2,1)S(1)}, bf16[128,256]{1,0:T(8,128)(2,1)S(1)}, u32[]{:S(2)}, u32[]{:S(2)}) collective-permute-start(bf16[128,256]{1,0:T(8,128)(2,1)S(1)} %get-tuple-element.68), channel_id=1, source_target_pairs={{0,7},{1,6},{2,5},{3,4},{4,3},{5,2},{6,1},{7,0},{8,15},{9,14},{10,... | collective-permute-start | bytes 196616 | tf_op jit(solution)/shard_map/ppermute | solution.py:814
  191.1 26.1 %collective-permute-start.10 = (bf16[288,256]{1,0:T(8,128)(2,1)S(1)}, bf16[288,256]{1,0:T(8,128)(2,1)S(1)}, u32[]{:S(2)}, u32[]{:S(2)}) collective-permute-start(bf16[288,256]{1,0:T(8,128)(2,1)S(1)} %get-tuple-element.64), channel_id=1, source_target_pairs={{0,4},{1,5},{2,6},{3,7},{4,0},{5,1},{6,2},{7,3},{8,12},{9,13},{10,... | collective-permute-start | bytes 442376 | tf_op jit(solution)/shard_map/ppermute | solution.py:814
  191.7 28.1 %collective-permute-start.11 = (bf16[288,256]{1,0:T(8,128)(2,1)S(1)}, bf16[288,256]{1,0:T(8,128)(2,1)S(1)}, u32[]{:S(2)}, u32[]{:S(2)}) collective-permute-start(bf16[288,256]{1,0:T(8,128)(2,1)S(1)} %get-tuple-element.63), channel_id=1, source_target_pairs={{0,5},{1,4},{2,7},{3,6},{4,1},{5,0},{6,3},{7,2},{8,13},{9,12},{10,... | collective-permute-start | bytes 442376 | tf_op jit(solution)/shard_map/ppermute | solution.py:814
  201.2 20.2 %collective-permute-start.12 = (bf16[288,256]{1,0:T(8,128)(2,1)S(1)}, bf16[288,256]{1,0:T(8,128)(2,1)S(1)}, u32[]{:S(2)}, u32[]{:S(2)}) collective-permute-start(bf16[288,256]{1,0:T(8,128)(2,1)S(1)} %get-tuple-element.62), channel_id=1, source_target_pairs={{0,6},{1,7},{2,4},{3,5},{4,2},{5,3},{6,0},{7,1},{8,14},{9,15},{10,... | collective-permute-start | bytes 442376 | tf_op jit(solution)/shard_map/ppermute | solution.py:814
  206.7 14.7 %collective-permute-start.13 = (bf16[288,256]{1,0:T(8,128)(2,1)S(1)}, bf16[288,256]{1,0:T(8,128)(2,1)S(1)}, u32[]{:S(2)}, u32[]{:S(2)}) collective-permute-start(bf16[288,256]{1,0:T(8,128)(2,1)S(1)} %get-tuple-element.61), channel_id=1, source_target_pairs={{0,7},{1,6},{2,5},{3,4},{4,3},{5,2},{6,1},{7,0},{8,15},{9,14},{10,... | collective-permute-start | bytes 442376 | tf_op jit(solution)/shard_map/ppermute | solution.py:814
  206.7 14.7 %collective-permute-start.7 = (bf16[288,256]{1,0:T(8,128)(2,1)S(1)}, bf16[288,256]{1,0:T(8,128)(2,1)S(1)}, u32[]{:S(2)}, u32[]{:S(2)}) collective-permute-start(bf16[288,256]{1,0:T(8,128)(2,1)S(1)} %get-tuple-element.60), channel_id=1, source_target_pairs={{0,1},{1,0},{2,3},{3,2},{4,5},{5,4},{6,7},{7,6},{8,9},{9,8},{10,11... | collective-permute-start | bytes 442376 | tf_op jit(solution)/shard_map/ppermute | solution.py:814
  217.3 5.8 %collective-permute-start.8 = (bf16[288,256]{1,0:T(8,128)(2,1)S(1)}, bf16[288,256]{1,0:T(8,128)(2,1)S(1)}, u32[]{:S(2)}, u32[]{:S(2)}) collective-permute-start(bf16[288,256]{1,0:T(8,128)(2,1)S(1)} %get-tuple-element.66), channel_id=1, source_target_pairs={{0,2},{1,3},{2,0},{3,1},{4,6},{5,7},{6,4},{7,5},{8,10},{9,11},{10,... | collective-permute-start | bytes 442376 | tf_op jit(solution)/shard_map/ppermute | solution.py:814
  219.9 6.1 %collective-permute-start.9 = (bf16[288,256]{1,0:T(8,128)(2,1)S(1)}, bf16[288,256]{1,0:T(8,128)(2,1)S(1)}, u32[]{:S(2)}, u32[]{:S(2)}) collective-permute-start(bf16[288,256]{1,0:T(8,128)(2,1)S(1)} %get-tuple-element.65), channel_id=1, source_target_pairs={{0,3},{1,2},{2,1},{3,0},{4,7},{5,6},{6,5},{7,4},{8,11},{9,10},{10,... | collective-permute-start | bytes 442376 | tf_op jit(solution)/shard_map/ppermute | solution.py:814
Sparse Core Ops, SparseCore 0:
  10.6 27.7 all-gather.3

commit v2 on v1

v2 whole, which is shorter than its diff:
```python
import math
from functools import partial

import jax
import jax.numpy as jnp
from jax import lax
from jax.experimental import pallas as pl
from jax.experimental.pallas import tpu as pltpu
from jax.sharding import PartitionSpec as P

HEADS = 8
HD = 32
CHUNK = 256
BLOCK = 128
PAIRS = HEADS // 2
OWNERS = 8

norm_eps = 1e-05
masked_score = -1e30
score_scale = HD ** (-0.5)
exp2_scale = score_scale * math.log2(math.e)
gelu_c0 = math.sqrt(2.0 / math.pi)
gelu_c1 = 0.044715 * gelu_c0

f32 = jnp.float32
bf16 = jnp.bfloat16

(
    Q_BIAS,
    V_BIAS,
    OUT_BIAS,
    DOWN_BIAS,
    ATTN_GAIN,
    ATTN_SHIFT,
    MLP_GAIN,
    MLP_SHIFT,
    UP_BIAS,
) = range(9)


def mm(left_op, right_op):
    return lax.dot_general(
        left_op, right_op, (((1,), (0,)), ((), ())), preferred_element_type=f32
    )


def mm_nt(left_op, right_op):
    return lax.dot_general(
        left_op, right_op, (((1,), (1,)), ((), ())), preferred_element_type=f32
    )


def identity(size):
    rows = lax.broadcasted_iota(jnp.int32, (size, size), 0)
    cols = lax.broadcasted_iota(jnp.int32, (size, size), 1)
    return jnp.where(rows == cols, 1.0, 0.0).astype(bf16)


def flipped(block):
    return mm_nt(identity(block.shape[1]), block).astype(bf16)


def half(index):
    return slice(index * BLOCK, (index + 1) * BLOCK)


def spread(column):
    return jnp.broadcast_to(column, (column.shape[0], BLOCK))


def row_sum(values):
    return jnp.sum(values, axis=0, keepdims=True)


def norm_forward(values, gain, shift):
    scale = 1.0 / values.shape[0]
    centre = values - row_sum(values) * scale
    inverse = lax.rsqrt(row_sum(centre * centre) * scale + norm_eps)
    unit = centre * inverse
    return unit, inverse, unit * gain + shift


def norm_backward(grad_normed, unit, inverse, gain):
    scale = 1.0 / unit.shape[0]
    scaled = grad_normed * gain
    gain_term = grad_normed * unit
    mean_scaled = row_sum(scaled) * scale
    mean_unit = row_sum(gain_term * gain) * scale
    return inverse * (scaled - mean_scaled - unit * mean_unit), gain_term


def below_mask():
    key_at = lax.broadcasted_iota(jnp.int32, (BLOCK, BLOCK), 0)
    query_at = lax.broadcasted_iota(jnp.int32, (BLOCK, BLOCK), 1)
    return key_at <= query_at, key_at == query_at


def set_masks(masks):
    below, _ = below_mask()
    own = jnp.where(twice(below), 1.0, 0.0)
    masks[0] = (1.0 - own).astype(bf16)
    masks[1] = own.astype(bf16)


def stack(side, pair):
    base = (side * PAIRS + pair) * BLOCK
    return slice(base, base + BLOCK)


def twice(values):
    return jnp.concatenate([values, values], axis=1)


def set_pairs(dest, source, lanes):
    for pair in range(PAIRS):
        base = 64 * (pair % 2)
        for side in range(2):
            rows = source[64 * pair + HD * side : 64 * pair + HD * (side + 1), :]
            dest[pair, base + HD * side : base + HD * (side + 1), half(side)] = rows[:, lanes]


def weave(*streams):
    order = []
    for index, (_, steps) in enumerate(streams):
        order += [((turn + 0.5) / steps, index) for turn in range(steps)]
    for _, index in sorted(order):
        next(streams[index][0], None)
    for generator, _ in streams:
        for _ in generator:
            pass


def project(u_ref, bcast, w_qkv, out):
    unit_o, inv_o, normed_o, qk_o, vtok_o, v_s, ktok_s = out
    model = w_qkv.shape[1]
    for side in range(2):
        unit, inverse, normed = norm_forward(
            u_ref[:, half(side)], bcast[ATTN_GAIN], bcast[ATTN_SHIFT]
        )
        unit_o[:, half(side)] = unit.astype(bf16)
        inv_o[:, half(side)] = inverse
        normed_o[:, half(side)] = normed.astype(bf16)
        yield
    eye = identity(model)
    normed = normed_o[...]
    rows = mm(w_qkv[model : 2 * model, :], normed)
    qk_o[model:, :] = rows.astype(bf16)
    yield
    rows = mm(w_qkv[2 * model :, :], normed)
    v_s[...] = (rows + twice(bcast[V_BIAS])).astype(bf16)
    yield
    rows = mm(w_qkv[:model, :], normed)
    qk_o[:model, :] = (rows + twice(bcast[Q_BIAS])).astype(bf16)
    yield
    ktok_s[...] = mm_nt(eye, qk_o[model:, :]).astype(bf16)
    yield
    vtok_o[...] = mm_nt(eye, v_s[...]).astype(bf16)
    yield


def hand_over(qk, v_s, ktok_s, q_pairs, key_win, value_win):
    key_win[:BLOCK, :] = key_win[CHUNK:, :]
    value_win[:, :BLOCK] = value_win[:, CHUNK:]
    key_win[BLOCK:, :] = ktok_s[...]
    value_win[:, BLOCK:] = v_s[...]
    for side in range(2):
        set_pairs(q_pairs.at[side], qk, half(side))


def attend(seg_ref, segprev, masks, q_pairs, key_win, value_win, probs_o, context_o):
    below, diagonal = below_mask()
    below2 = twice(below)
    items = [(side, pair) for side in range(2) for pair in range(PAIRS)]
    biases, scores, windows = {}, {}, {}
    for turn in range(len(items) + 2):
        if turn < len(items):
            side, pair = items[turn]
            span = slice(side * BLOCK, side * BLOCK + CHUNK)
            scores[turn] = mm(key_win[span, half(pair // 2)], q_pairs[side, pair])
            if pair == 0:
                seg_row = seg_ref[:, half(side)].astype(f32)
                seg_col = jnp.transpose(jnp.broadcast_to(seg_row, (BLOCK, BLOCK)))
                seg_key = jnp.where(below, seg_col, segprev[...])
                segprev[...] = seg_col
                allowed = ((seg_key == seg_row) & (seg_row >= 0)) | diagonal
                biases[side] = jnp.where(allowed, 0.0, masked_score)
        if turn >= 2:
            side, pair = items[turn - 2]
            lanes = half(side)
            span = slice(side * BLOCK, side * BLOCK + CHUNK)
            both = mm(value_win[64 * pair : 64 * (pair + 1), span], windows.pop(turn - 2))
            context_o[64 * pair : 64 * pair + HD, lanes] = both[:HD, :BLOCK].astype(bf16)
            context_o[64 * pair + HD : 64 * (pair + 1), lanes] = both[HD:, BLOCK:].astype(bf16)
        if 1 <= turn <= len(items):
            side, pair = items[turn - 1]
            table = scores.pop(turn - 1)
            folded = jnp.where(below2, table[BLOCK:], table[:BLOCK]) * exp2_scale + twice(
                biases[side]
            )
            top = jnp.max(folded, axis=0, keepdims=True)
            weights = jnp.exp2(folded - top)
            probs = (weights * (1.0 / row_sum(weights))).astype(bf16)
            probs_o[stack(side, pair), :] = probs
            windows[turn - 1] = jnp.concatenate([probs * masks[0], probs * masks[1]], axis=0)
        yield


def feed_forward(u_ref, m_ref, context, bcast, up_bias, w_out, w_up, w_down, out, finish):
    unit_o, inv_o, normed_o, hidden_o, slope_o = out
    mixed = mm(w_out[...], context)
    yield
    for side in range(2):
        lanes = half(side)
        after = u_ref[:, lanes] + (mixed[:, lanes] + bcast[OUT_BIAS])
        m_ref[:, lanes] = after
        unit, inverse, normed = norm_forward(after, bcast[MLP_GAIN], bcast[MLP_SHIFT])
        unit_o[:, lanes] = unit.astype(bf16)
        inv_o[:, lanes] = inverse
        normed_o[:, lanes] = normed.astype(bf16)
        yield
    normed = normed_o[...]
    parts = w_up.shape[0] // CHUNK

    def rows_of(part):
        return slice(part * CHUNK, (part + 1) * CHUNK)

    pre = mm(w_up[rows_of(0), :], normed)
    for part in range(parts):
        rows = rows_of(part)
        current = pre
        if part + 1 < parts:
            pre = mm(w_up[rows_of(part + 1), :], normed)
        for piece in range(2):
            inner = slice(piece * BLOCK, (piece + 1) * BLOCK)
            outer = slice(part * CHUNK + piece * BLOCK, part * CHUNK + (piece + 1) * BLOCK)
            z = (current[inner, :] + twice(up_bias[outer, :])).astype(bf16)
            z2 = z * z
            gate = 0.5 * jnp.tanh(z * (gelu_c0 + gelu_c1 * z2)) + 0.5
            act = z * gate
            slope = gate + (act * (1.0 - gate)) * (2.0 * gelu_c0 + 6.0 * gelu_c1 * z2)
            hidden_o[outer, :] = act
            slope_o[outer, :] = slope
            yield
    total = mm(w_down[...], hidden_o[...])
    yield
    for side in range(2):
        lanes = half(side)
        finish(side, m_ref[:, lanes] + (total[:, lanes] + bcast[DOWN_BIAS]))
    yield


def back_feed_forward(g_ref, dm_ref, saved, bcast, weights, sums, dy_s, dz_s, do_ref):
    unit, inverse, normed, hidden, slope = saved
    w_down_n, w_up_n = weights
    sum_down, sum_up, sum_up_bias, sum_vec = sums
    for side in range(2):
        lanes = half(side)
        grad = g_ref[:, lanes]
        sum_vec[DOWN_BIAS] += grad
        dy_s[:, lanes] = grad.astype(bf16)
    dy = dy_s[...]
    yield
    parts = w_down_n.shape[0] // CHUNK

    def rows_of(part):
        return slice(part * CHUNK, (part + 1) * CHUNK)

    ahead = mm(w_down_n[rows_of(0), :], dy)
    for part in range(parts):
        rows = rows_of(part)
        current = ahead
        if part + 1 < parts:
            ahead = mm(w_down_n[rows_of(part + 1), :], dy)
        dz = current.astype(bf16) * slope[rows, :]
        dz_s[rows, :] = dz
        wide = dz.astype(f32)
        sum_up_bias[rows, :] += wide[:, :BLOCK] + wide[:, BLOCK:]
        yield
    total = mm(w_up_n[...], dz_s[...])
    yield
    sum_down[...] += mm_nt(hidden[...], dy)
    yield
    units = unit[...]
    for side in range(2):
        lanes = half(side)
        grad_normed = total[:, lanes]
        back, gain_term = norm_backward(
            grad_normed, units[:, lanes].astype(f32), inverse[:, lanes], bcast[MLP_GAIN]
        )
        sum_vec[MLP_GAIN] += gain_term
        sum_vec[MLP_SHIFT] += grad_normed
        dm = g_ref[:, lanes] + back
        if dm_ref is not None:
            dm_ref[:, lanes] = dm
        sum_vec[OUT_BIAS] += dm
        do_ref[:, lanes] = dm.astype(bf16)
        yield
    sum_up[...] += mm_nt(dz_s[...], normed[...])
    yield


def back_out(do_ref, context, w_out_n, sum_out, dc_ref):
    grad = do_ref[...]
    dc_ref[...] = mm(w_out_n[...], grad).astype(bf16)
    yield
    sum_out[...] += mm_nt(grad, context[...])
    yield


def back_attention(
    dc_ref, context, qk, kt_prev, vtok, vtok_prev, probs_ref, masks, pairs, carry, dqkv
):
    q_pairs, c_pairs = pairs
    dk_carry, dv_carry = carry
    model = vtok.shape[1]
    below, _ = below_mask()
    below2 = twice(below)
    items = [(side, pair) for side in (1, 0) for pair in range(PAIRS)]
    key_win, value_win, weighted, grads, windows = {}, {}, {}, {}, {}
    for turn in range(len(items) + 2):
        if turn < len(items):
            side, pair = items[turn]
            if pair == 0:
                lanes = half(side)
                set_pairs(q_pairs.at[side], qk, lanes)
                set_pairs(c_pairs.at[side], dc_ref, lanes)
                weighted[side] = dc_ref[...][:, lanes].astype(f32) * context[...][:, lanes].astype(f32)
                if side == 1:
                    key_win[side] = qk[model:, :]
                    value_win[side] = vtok[...]
                else:
                    key_win[side] = jnp.concatenate([kt_prev[...], qk[model:, :][:, :BLOCK]], axis=1)
                    value_win[side] = jnp.concatenate([vtok_prev[...], vtok[:BLOCK, :]], axis=0)
            grads[turn] = mm(value_win[side][:, half(pair // 2)], c_pairs[side, pair])
        if turn >= 2:
            side, pair = items[turn - 2]
            lanes = half(side)
            base = 64 * (pair % 2)
            rows = slice(64 * pair, 64 * (pair + 1))
            prob_win, grad_win = windows.pop(turn - 2)
            dq = mm(key_win[side][rows, :], grad_win) * score_scale
            dk = mm_nt(q_pairs[side, pair, base : base + 64, :], grad_win) * score_scale
            dv = mm_nt(c_pairs[side, pair, base : base + 64, :], prob_win)
            dqkv[64 * pair : 64 * pair + HD, lanes] = dq[:HD, :BLOCK].astype(bf16)
            dqkv[64 * pair + HD : 64 * (pair + 1), lanes] = dq[HD:, BLOCK:].astype(bf16)
            krows = slice(model + 64 * pair, model + 64 * (pair + 1))
            vrows = slice(2 * model + 64 * pair, 2 * model + 64 * (pair + 1))
            dqkv[krows, lanes] = (dk[:, BLOCK:] + dk_carry[rows, :]).astype(bf16)
            dqkv[vrows, lanes] = (dv[:, BLOCK:] + dv_carry[rows, :]).astype(bf16)
            dk_carry[rows, :] = dk[:, :BLOCK]
            dv_carry[rows, :] = dv[:, :BLOCK]
        if 1 <= turn <= len(items):
            side, pair = items[turn - 1]
            table = grads.pop(turn - 1)
            folded = jnp.where(below2, table[BLOCK:], table[:BLOCK])
            product = weighted[side]
            delta = jnp.concatenate(
                [
                    row_sum(product[64 * pair : 64 * pair + HD]),
                    row_sum(product[64 * pair + HD : 64 * (pair + 1)]),
                ],
                axis=1,
            )
            probs = probs_ref[stack(side, pair), :]
            grad_scores = probs * (folded - delta).astype(bf16)
            prob_win = jnp.concatenate([probs * masks[0], probs * masks[1]], axis=0)
            grad_win = jnp.concatenate([grad_scores * masks[0], grad_scores * masks[1]], axis=0)
            windows[turn - 1] = (prob_win, grad_win)
        yield


def back_project(dm_ref, dqkv, unit, inverse, normed, bcast, w_qkv_n, sum_qkv, sum_vec, finish):
    grads = dqkv[...]
    model = dm_ref.shape[0]
    total = mm(w_qkv_n[...], grads)
    for side in range(2):
        sum_vec[Q_BIAS] += grads[:model, half(side)].astype(f32)
        sum_vec[V_BIAS] += grads[2 * model :, half(side)].astype(f32)
    yield
    sum_qkv[...] += mm_nt(grads, normed[...])
    yield
    units = unit[...]
    for side in range(2):
        lanes = half(side)
        grad_normed = total[:, lanes]
        back, gain_term = norm_backward(
            grad_normed, units[:, lanes].astype(f32), inverse[:, lanes], bcast[ATTN_GAIN]
        )
        sum_vec[ATTN_GAIN] += gain_term
        sum_vec[ATTN_SHIFT] += grad_normed
        finish(side, dm_ref[:, lanes].astype(f32) + back)
        yield


def unpack_first(packed, w_qkv, vec):
    owners, _, model = packed.shape
    rows = 3 * model // owners
    for owner in range(owners):
        w_qkv[rows * owner : rows * (owner + 1), :] = packed[owner, :rows, :]
        vec[32 * owner : 32 * (owner + 1), :] = packed[owner, rows:, :BLOCK].astype(f32)


def unpack_second(packed, w_out, w_up_n, w_down):
    owners = packed.shape[0]
    for owner in range(owners):
        rows = slice(32 * owner, 32 * (owner + 1))
        w_out[rows, :] = packed[owner, :32, :]
        for side in range(2):
            w_up_n[half(side), half(owner)] = packed[owner, 32:160, half(side)]
        for part in range(4):
            w_down[rows, part * CHUNK : (part + 1) * CHUNK] = packed[
                owner, 160 + 32 * part : 192 + 32 * part, :
            ]


def spread_vectors(vec, bcast, which):
    values = vec[...]
    for index in which:
        bcast[index] = spread(values[:, index : index + 1])


def token_sum(left_tokens, right_tokens, dest):
    eye = identity(left_tokens.shape[1])
    dest[...] = mm_nt(eye, left_tokens) + mm_nt(eye, right_tokens)


def kernel_one(
    rows_chunks, chunks, x, inj, seg, first_weights,
    unit_o, inv_o, normed_o, qk_o, vtok_o, probs_o, context_o,
    w_qkv, vec, bcast, u_s, v_s, ktok_s, key_win, value_win, segprev, q_pairs, masks,
):
    step = pl.program_id(0)

    @pl.when(step == 0)
    def _():
        unpack_first(first_weights, w_qkv, vec)
        spread_vectors(vec, bcast, (Q_BIAS, V_BIAS, ATTN_GAIN, ATTN_SHIFT))
        key_win[...] = jnp.zeros_like(key_win)
        value_win[...] = jnp.zeros_like(value_win)
        q_pairs[...] = jnp.zeros_like(q_pairs)
        set_masks(masks)

    @pl.when(lax.rem(step - 1, rows_chunks) == 0)
    def _():
        segprev[...] = jnp.full(segprev.shape, -2.0, f32)

    def first():
        token_sum(x[...], inj[...], u_s)
        yield
        yield from project(
            u_s, bcast, w_qkv,
            [r.at[0] for r in (unit_o, inv_o, normed_o, qk_o, vtok_o)] + [v_s, ktok_s],
        )

    def second():
        return attend(seg.at[0], segprev, masks, q_pairs, key_win, value_win, probs_o.at[0], context_o.at[0])

    def finish():
        hand_over(qk_o.at[0], v_s, ktok_s, q_pairs, key_win, value_win)

    @pl.when(step == 0)
    def _():
        weave((first(), 8))
        finish()

    @pl.when((step > 0) & (step < chunks))
    def _():
        weave((second(), 10), (first(), 8))
        finish()

    @pl.when(step == chunks)
    def _():
        weave((second(), 10))


def kernel_two(
    rows_chunks, chunks,
    x, c1, inj, cot, seg, first_weights, second_weights,
    result_o, dm_o, dc_o, du_o, grads_o, sum_qkv_o, vec_o,
    w_qkv, vec, w_out, w_up_n, w_down, bcast, up_bias, w_up, w_down_n, w_out_n, w_qkv_n,
    u1_s, u_s, m1_s, m2_s, g1_s, g2_s, v_s, ktok_s, key_win, value_win, segprev, q_pairs, c_pairs, masks,
    unit_m1, inv_m1, norm_m1, hid1, slope1,
    u2, dm2, unit2, inv2, norm2, qk2, vtok2, probs2, ctx2,
    unit_m2, inv_m2, norm_m2, hid2, slope2,
    dy1_s, dz1_s, dy2_s, dz2_s, do2_s, dc_s, dqkv_s, dk_carry, dv_carry, probs_s, slope1_s, slope2_s, unit_m1_s, unit_m2_s, unit2_s,
    norm_m1_s, norm_m2_s, norm2_s, inv_m1_s, inv_m2_s, inv2_s, dm2_s,
    sum_down, sum_up, sum_out, sum_up_bias, sum_vec,
):
    step = pl.program_id(0)
    model = w_out.shape[0]
    ff = w_up.shape[0]
    turn = chunks + 2

    @pl.when(step == 0)
    def _():
        unpack_first(first_weights, w_qkv, vec)
        unpack_second(second_weights, w_out, w_up_n, w_down)
        spread_vectors(vec, bcast, range(8))
        values = vec[...]
        for owner in range(ff // BLOCK):
            for col in range(4):
                up_bias[BLOCK * owner + 32 * col : BLOCK * owner + 32 * (col + 1), :] = spread(
                    values[32 * owner : 32 * (owner + 1), UP_BIAS + col : UP_BIAS + col + 1]
                )
        for part in range(ff // CHUNK):
            rows = slice(part * CHUNK, (part + 1) * CHUNK)
            w_up[rows, :] = flipped(w_up_n[:, rows])
            w_down_n[rows, :] = flipped(w_down[:, rows])
        w_out_n[...] = flipped(w_out[...])
        for part in range(3):
            rows = slice(part * model, (part + 1) * model)
            w_qkv_n[:, rows] = flipped(w_qkv[rows, :])
        for ref in (key_win, value_win, q_pairs, c_pairs, dk_carry, dv_carry,
                    sum_down, sum_up, sum_out, sum_up_bias, sum_vec):
            ref[...] = jnp.zeros_like(ref)
        sum_qkv_o[...] = jnp.zeros_like(sum_qkv_o)
        set_masks(masks)

    @pl.when(lax.rem(step - 1, rows_chunks) == 0)
    def _():
        segprev[...] = jnp.full(segprev.shape, -2.0, f32)

    def mlp_one():
        i = step

        def finish(side, h):
            again = mm_nt(identity(model), inj[half(side), :])
            u_s[:, half(side)] = h + again
            u2[i, :, half(side)] = h + again

        token_sum(x[...], inj[...], u1_s)
        yield
        yield from feed_forward(
            u1_s, m1_s, c1[0], bcast, up_bias, w_out, w_up, w_down,
            [r.at[i] for r in (unit_m1, inv_m1, norm_m1, hid1, slope1)], finish,
        )
        out = [r.at[i] for r in (unit2, inv2, norm2, qk2, vtok2)]
        yield from project(u_s, bcast, w_qkv, out + [v_s, ktok_s])

    def attention():
        i = step - 1
        return attend(seg.at[0], segprev, masks, q_pairs, key_win, value_win, probs2.at[i], ctx2.at[i])

    def mlp_two():
        i = step - 2

        def finish(side, h):
            low = h.astype(bf16)
            result_o[half(side), :] = mm_nt(identity(BLOCK), low).astype(bf16)

        yield from feed_forward(
            u2.at[i], m2_s, ctx2[i], bcast, up_bias, w_out, w_up, w_down,
            [r.at[i] for r in (unit_m2, inv_m2, norm_m2, hid2, slope2)], finish,
        )

    lengths = {mlp_one: 21, attention: 10, mlp_two: 13}

    def forward_turn(*which):
        weave(*[(stream(), lengths[stream]) for stream in which])
        if mlp_one in which:
            hand_over(qk2.at[step], v_s, ktok_s, q_pairs, key_win, value_win)

    @pl.when(step == 0)
    def _():
        forward_turn(mlp_one)

    @pl.when(step == 1)
    def _():
        forward_turn(attention, mlp_one)

    @pl.when((step >= 2) & (step < chunks))
    def _():
        forward_turn(mlp_two, attention, mlp_one)

    @pl.when(step == chunks)
    def _():
        forward_turn(mlp_two, attention)

    @pl.when(step == chunks + 1)
    def _():
        forward_turn(mlp_two)

    @pl.when(step == turn - 1)
    def _():
        slope2_s[...] = slope2[chunks - 1]
        unit_m2_s[...] = unit_m2[chunks - 1]
        norm_m2_s[...] = norm_m2[chunks - 1]
        inv_m2_s[...] = inv_m2[chunks - 1]

    at = step - turn
    sums = (sum_down, sum_up, sum_up_bias, sum_vec)

    def back_mlp_two():
        i = chunks - 1 - at
        g2_s[...] = mm_nt(identity(model), cot[...])
        yield
        yield from back_feed_forward(
            g2_s, dm2.at[i], [unit_m2_s, inv_m2_s, norm_m2_s, hid2.at[i], slope2_s],
            bcast, (w_down_n, w_up_n), sums, dy2_s, dz2_s, do2_s,
        )
        yield from back_out(do2_s, ctx2.at[i], w_out_n, sum_out, dc_s)

    def back_attend():
        i = chunks - at
        before = jnp.maximum(i - 1, 0)
        return back_attention(
            dc_s, ctx2.at[i], qk2.at[i], qk2.at[before, model:, BLOCK:], vtok2.at[i],
            vtok2.at[before, BLOCK:, :], probs_s, masks, (q_pairs, c_pairs),
            (dk_carry, dv_carry), dqkv_s,
        )

    def back_rest():
        i = chunks + 1 - at

        def finish(side, du):
            g1_s[:, half(side)] = du
            du_o[0, :, half(side)] = du.astype(bf16)

        yield from back_project(
            dm2_s, dqkv_s, unit2_s, inv2_s, norm2_s, bcast, w_qkv_n,
            sum_qkv_o, sum_vec, finish,
        )
        yield from back_feed_forward(
            g1_s, None, [unit_m1_s, inv_m1_s, norm_m1_s, hid1.at[i], slope1_s],
            bcast, (w_down_n, w_up_n), sums, dy1_s, dz1_s, dm_o.at[0],
        )
        yield from back_out(dm_o.at[0], c1.at[0], w_out_n, sum_out, dc_o.at[0])

    lengths_back = {back_mlp_two: 13, back_attend: 10, back_rest: 16}

    def backward_turn(*which):
        weave(*[(stream(), lengths_back[stream]) for stream in which])
        if back_mlp_two in which:
            probs_s[...] = probs2[chunks - 1 - at]
            slope2_s[...] = slope2[jnp.maximum(chunks - 2 - at, 0)]
            unit_m2_s[...] = unit_m2[jnp.maximum(chunks - 2 - at, 0)]
            norm_m2_s[...] = norm_m2[jnp.maximum(chunks - 2 - at, 0)]
            inv_m2_s[...] = inv_m2[jnp.maximum(chunks - 2 - at, 0)]
        if back_attend in which:
            slope1_s[...] = slope1[chunks - at]
            unit_m1_s[...] = unit_m1[chunks - at]
            unit2_s[...] = unit2[chunks - at]
            norm_m1_s[...] = norm_m1[chunks - at]
            norm2_s[...] = norm2[chunks - at]
            dm2_s[...] = dm2[chunks - at]
            inv_m1_s[...] = inv_m1[chunks - at]
            inv2_s[...] = inv2[chunks - at]

    @pl.when(at == 0)
    def _():
        backward_turn(back_mlp_two)

    @pl.when(at == 1)
    def _():
        backward_turn(back_attend, back_mlp_two)

    @pl.when((at >= 2) & (at < chunks))
    def _():
        backward_turn(back_rest, back_attend, back_mlp_two)

    @pl.when(at == chunks)
    def _():
        backward_turn(back_rest, back_attend)

    @pl.when(at == chunks + 1)
    def _():
        backward_turn(back_rest)
        owners = OWNERS
        for part in range(ff // CHUNK):
            rows = slice(part * CHUNK, (part + 1) * CHUNK)
            up_block = flipped(sum_up[rows, :].astype(bf16))
            for within in range(2):
                for side in range(2):
                    grads_o[within, part, 32:160, half(side)] = up_block[
                        half(side), half(within)
                    ]
            down_block = flipped(sum_down[rows, :].astype(bf16))
            for owner in range(owners):
                grads_o[owner % 2, owner // 2, 160 + 32 * part : 192 + 32 * part, :] = down_block[
                    32 * owner : 32 * (owner + 1), :
                ]
        for owner in range(owners):
            grads_o[owner % 2, owner // 2, :32, :] = sum_out[32 * owner : 32 * (owner + 1), :].astype(bf16)
        vec_o[...] = jnp.zeros_like(vec_o)
        for index in range(8):
            vec_o[:, index : index + 1] = jnp.sum(sum_vec[index], axis=1, keepdims=True)
        for owner in range(ff // BLOCK):
            for col in range(4):
                vec_o[32 * owner : 32 * (owner + 1), UP_BIAS + col : UP_BIAS + col + 1] = jnp.sum(
                    sum_up_bias[BLOCK * owner + 32 * col : BLOCK * owner + 32 * (col + 1), :],
                    axis=1, keepdims=True,
                )


def kernel_three(
    chunks,
    unit, inv, normed, qk, kt_prev, vtok, vtok_prev, probs, ctx, dm, dc, du2, first_weights, sum_qkv_i, vec_i,
    gin_o, ginj_o, grads_o,
    w_qkv, vec, bcast, w_qkv_n, q_pairs, c_pairs, masks, dqkv_s, dk_carry, dv_carry, sum_qkv, sum_vec,
):
    step = pl.program_id(0)
    model = w_qkv.shape[1]
    owners = OWNERS

    @pl.when(step == 0)
    def _():
        unpack_first(first_weights, w_qkv, vec)
        spread_vectors(vec, bcast, (ATTN_GAIN,))
        for part in range(3):
            rows = slice(part * model, (part + 1) * model)
            w_qkv_n[:, rows] = flipped(w_qkv[rows, :])
        for ref in (q_pairs, c_pairs, dk_carry, dv_carry, sum_vec):
            ref[...] = jnp.zeros_like(ref)
        sum_qkv[...] = sum_qkv_i[...]
        set_masks(masks)

    def attention():
        return back_attention(
            dc.at[0], ctx.at[0], qk.at[0], kt_prev.at[0], vtok.at[0], vtok_prev.at[0], probs.at[0],
            masks, (q_pairs, c_pairs), (dk_carry, dv_carry), dqkv_s,
        )

    def rest():
        eye = identity(BLOCK)

        def finish(side, du):
            gin_o[half(side), :] = mm_nt(eye, du.astype(bf16)).astype(bf16)
            both = du + du2[0, :, half(side)].astype(f32)
            ginj_o[half(side), :] = mm_nt(eye, both.astype(bf16)).astype(bf16)

        return back_project(
            dm.at[0], dqkv_s, unit.at[0], inv.at[0], normed.at[0], bcast, w_qkv_n,
            sum_qkv, sum_vec, finish,
        )

    @pl.when(step == 0)
    def _():
        weave((attention(), 10))

    @pl.when((step > 0) & (step < chunks))
    def _():
        weave((rest(), 4), (attention(), 10))

    @pl.when(step == chunks)
    def _():
        weave((rest(), 4))
        rows = 3 * model // owners
        vec[...] = vec_i[...]
        for index in (Q_BIAS, V_BIAS, ATTN_GAIN, ATTN_SHIFT):
            vec[:, index : index + 1] += jnp.sum(sum_vec[index], axis=1, keepdims=True)
        for owner in range(owners):
            grads_o[owner % 2, owner // 2, :rows, :] = sum_qkv[rows * owner : rows * (owner + 1), :].astype(bf16)
            grads_o[owner % 2, owner // 2, rows:, :] = twice(vec[32 * owner : 32 * (owner + 1), :].astype(bf16))


def cost(microseconds):
    return pl.CostEstimate(
        flops=int(microseconds * 1.1e9), bytes_accessed=int(microseconds * 3e6), transcendentals=0
    )


def whole(array):
    zeros = (0,) * len(array.shape)
    return pl.BlockSpec(array.shape, lambda j: zeros)


def shape(dims, kind):
    return jax.ShapeDtypeStruct(dims, kind)


def vmem(dims, kind):
    return pltpu.VMEM(dims, kind)


params = pltpu.CompilerParams(vmem_limit_bytes=62 * 1024 * 1024)


def run_one(x, inj, seg, first_weights, per_row):
    tokens, model = x.shape
    chunks = tokens // CHUNK
    last = chunks - 1

    def early(j):
        return jnp.minimum(j, last)

    def late(j):
        return jnp.maximum(j - 1, 0)

    def lead(dims, order):
        return pl.BlockSpec((1,) + dims, lambda j: (order(j),) + (0,) * len(dims))

    token_spec = pl.BlockSpec((CHUNK, model), lambda j: (early(j), 0))
    outs = [
        ((model, CHUNK), bf16, early),
        ((1, CHUNK), f32, early),
        ((model, CHUNK), bf16, early),
        ((2 * model, CHUNK), bf16, early),
        ((CHUNK, model), bf16, early),
        ((2 * PAIRS * BLOCK, CHUNK), bf16, late),
        ((model, CHUNK), bf16, late),
    ]
    return pl.pallas_call(
        partial(kernel_one, per_row, chunks),
        grid=(chunks + 1,),
        in_specs=[token_spec, token_spec, lead((1, CHUNK), late), whole(first_weights)],
        out_specs=[lead(dims, order) for dims, _, order in outs],
        out_shape=[shape((chunks,) + dims, kind) for dims, kind, _ in outs],
        scratch_shapes=[
            vmem((3 * model, model), bf16),
            vmem((model, BLOCK), f32),
            vmem((8, model, BLOCK), f32),
            vmem((model, CHUNK), f32),
            vmem((model, CHUNK), bf16),
            vmem((CHUNK, model), bf16),
            vmem((CHUNK + BLOCK, model), bf16),
            vmem((model, CHUNK + BLOCK), bf16),
            vmem((BLOCK, BLOCK), f32),
            vmem((2, PAIRS, BLOCK, CHUNK), bf16),
            vmem((2, BLOCK, CHUNK), bf16),
        ],
        compiler_params=params,
        name="attend_first",
        cost_estimate=cost(14),
    )(x, inj, seg, first_weights)


def run_two(x, c1, inj, cot, seg, first_weights, second_weights, per_row):
    tokens, model = x.shape
    chunks = tokens // CHUNK
    owners = second_weights.shape[0]
    ff = BLOCK * owners
    second_grads = shape((2, owners // 2) + second_weights.shape[1:], bf16)
    last = chunks - 1
    turn = chunks + 2

    def up(lag):
        return lambda j: jnp.clip(j - lag, 0, last)

    def down(lag):
        return lambda j: jnp.clip(last - (j - turn - lag), 0, last)

    def up_then_down(j):
        return jnp.where(j < turn, jnp.minimum(j, last), jnp.clip(last - (j - turn - 2), 0, last))

    def lead(dims, order):
        return pl.BlockSpec((1,) + dims, lambda j: (order(j),) + (0,) * len(dims))

    def tok(order):
        return pl.BlockSpec((CHUNK, model), lambda j: (order(j), 0))

    square = (model, CHUNK)
    mlp_saved = [
        vmem((chunks,) + square, bf16),
        vmem((chunks, 1, CHUNK), f32),
        vmem((chunks,) + square, bf16),
        vmem((chunks, ff, CHUNK), bf16),
        vmem((chunks, ff, CHUNK), bf16),
    ]
    back_buffers = [vmem(square, bf16), vmem((ff, CHUNK), bf16), vmem(square, bf16)]
    return pl.pallas_call(
        partial(kernel_two, per_row, chunks),
        grid=(2 * turn,),
        in_specs=[
            tok(up(0)),
            lead(square, up_then_down),
            tok(up(0)),
            tok(down(0)),
            lead((1, CHUNK), up(1)),
            whole(first_weights),
            whole(second_weights),
        ],
        out_specs=[
            tok(up(2)),
            lead(square, down(2)),
            lead(square, down(2)),
            lead(square, down(2)),
            whole(second_grads),
            pl.BlockSpec((3 * model, model), lambda j: (0, 0)),
            pl.BlockSpec((model, BLOCK), lambda j: (0, 0)),
        ],
        out_shape=[
            shape((tokens, model), bf16),
            shape((chunks,) + square, bf16),
            shape((chunks,) + square, bf16),
            shape((chunks,) + square, bf16),
            second_grads,
            shape((3 * model, model), f32),
            shape((model, BLOCK), f32),
        ],
        scratch_shapes=[
            vmem((3 * model, model), bf16),
            vmem((model, BLOCK), f32),
            vmem((model, model), bf16),
            vmem((model, ff), bf16),
            vmem((model, ff), bf16),
            vmem((8, model, BLOCK), f32),
            vmem((ff, BLOCK), f32),
            vmem((ff, model), bf16),
            vmem((ff, model), bf16),
            vmem((model, model), bf16),
            vmem((model, 3 * model), bf16),
        ]
        + [vmem(square, f32)] * 6
        + [
            vmem(square, bf16),
            vmem((CHUNK, model), bf16),
            vmem((CHUNK + BLOCK, model), bf16),
            vmem((model, CHUNK + BLOCK), bf16),
            vmem((BLOCK, BLOCK), f32),
            vmem((2, PAIRS, BLOCK, CHUNK), bf16),
            vmem((2, PAIRS, BLOCK, CHUNK), bf16),
            vmem((2, BLOCK, CHUNK), bf16),
        ]
        + mlp_saved
        + [
            vmem((chunks,) + square, f32),
            vmem((chunks,) + square, f32),
            vmem((chunks,) + square, bf16),
            vmem((chunks, 1, CHUNK), f32),
            vmem((chunks,) + square, bf16),
            vmem((chunks, 2 * model, CHUNK), bf16),
            vmem((chunks, CHUNK, model), bf16),
            vmem((chunks, 2 * PAIRS * BLOCK, CHUNK), bf16),
            vmem((chunks,) + square, bf16),
        ]
        + mlp_saved
        + back_buffers[:2]
        + back_buffers
        + [
            vmem(square, bf16),
            vmem((3 * model, CHUNK), bf16),
            vmem((model, BLOCK), f32),
            vmem((model, BLOCK), f32),
            vmem((2 * PAIRS * BLOCK, CHUNK), bf16),
            vmem((ff, CHUNK), bf16),
            vmem((ff, CHUNK), bf16),
            *[vmem(square, bf16)] * 6,
            *[vmem((1, CHUNK), f32)] * 3,
            vmem(square, f32),
            vmem((ff, model), f32),
            vmem((ff, model), f32),
            vmem((model, model), f32),
            vmem((ff, BLOCK), f32),
            vmem((8, model, BLOCK), f32),
        ],
        compiler_params=params,
        name="middle",
        cost_estimate=cost(60),
    )(x, c1, inj, cot, seg, first_weights, second_weights)


def run_three(saved, dm, dc, du2, first_weights, sum_qkv, vec_in):
    unit, inv, normed, qk, vtok, probs, ctx = saved
    chunks, model, _ = dm.shape
    tokens = chunks * CHUNK
    last = chunks - 1
    first_grads = shape((2, OWNERS // 2) + first_weights.shape[1:], bf16)

    def now(j):
        return jnp.maximum(last - j, 0)

    def past(j):
        return jnp.minimum(chunks - j, last)

    def before(j):
        return jnp.maximum(last - 1 - j, 0)

    def lead(array, order):
        dims = array.shape[1:]
        return pl.BlockSpec((1,) + dims, lambda j: (order(j),) + (0,) * len(dims))

    tok = pl.BlockSpec((CHUNK, model), lambda j: (past(j), 0))
    return pl.pallas_call(
        partial(kernel_three, chunks),
        grid=(chunks + 1,),
        in_specs=[
            lead(unit, past),
            lead(inv, past),
            lead(normed, past),
            lead(qk, now),
            pl.BlockSpec((1, model, BLOCK), lambda j: (before(j), 1, 1)),
            lead(vtok, now),
            pl.BlockSpec((1, BLOCK, model), lambda j: (before(j), 1, 0)),
            lead(probs, now),
            lead(ctx, now),
            lead(dm, past),
            lead(dc, now),
            lead(du2, past),
            whole(first_weights),
            whole(sum_qkv),
            whole(vec_in),
        ],
        out_specs=[
            tok,
            tok,
            whole(first_grads),
        ],
        out_shape=[
            shape((tokens, model), bf16),
            shape((tokens, model), bf16),
            first_grads,
        ],
        scratch_shapes=[
            vmem((3 * model, model), bf16),
            vmem((model, BLOCK), f32),
            vmem((8, model, BLOCK), f32),
            vmem((model, 3 * model), bf16),
            vmem((2, PAIRS, BLOCK, CHUNK), bf16),
            vmem((2, PAIRS, BLOCK, CHUNK), bf16),
            vmem((2, BLOCK, CHUNK), bf16),
            vmem((3 * model, CHUNK), bf16),
            vmem((model, BLOCK), f32),
            vmem((model, BLOCK), f32),
            vmem((3 * model, model), f32),
            vmem((8, model, BLOCK), f32),
        ],
        compiler_params=params,
        name="attend_back",
        cost_estimate=cost(16),
    )(unit, inv, normed, qk, qk, vtok, vtok, probs, ctx, dm, dc, du2, first_weights, sum_qkv, vec_in)


def pack_first(qkv_t, vectors):
    rows, model = qkv_t.shape
    count = rows // 96
    columns = [vector.reshape(count, 1, 32) for vector in vectors[:3] + vectors[4:]]
    columns.insert(8, vectors[3].reshape(count, 4, 32))
    block = jnp.concatenate(columns, axis=1).transpose(0, 2, 1)
    block = jnp.pad(block, ((0, 0), (0, 0), (0, model - block.shape[2])))
    return jnp.concatenate([qkv_t.reshape(count, 96, model), block], axis=1)


def unpack_vectors(block):
    columns = [block[:, :, index].reshape(-1) for index in range(8)]
    columns.insert(3, block[:, :, 8:12].transpose(0, 2, 1).reshape(-1))
    return columns


def pack_second(out_t, up, down_t):
    rows, model = out_t.shape
    count = rows // 32
    up_part = up.reshape(2, model // 2, count, 128).transpose(2, 1, 0, 3).reshape(count, 128, 256)
    down_part = down_t.reshape(count, 32, 4, 256).transpose(0, 2, 1, 3).reshape(count, 128, 256)
    return jnp.concatenate([out_t.reshape(count, 32, model), up_part, down_part], axis=1)


def unpack_second_grads(block):
    count, _, model = block.shape
    out_t = block[:, :32].reshape(count * 32, model)
    up = block[:, 32:160].reshape(count, 128, 2, 128).transpose(2, 1, 0, 3)
    down_t = block[:, 160:].reshape(count, 4, 32, 256).transpose(0, 2, 1, 3)
    return out_t, up.reshape(model, 128 * count), down_t.reshape(32 * count, 1024)


def exchange(block, axis, size, distance):
    return lax.ppermute(block, axis, [(k, k ^ distance) for k in range(size)])


def gather(block, aside):
    me = lax.axis_index("fsdp")
    block = block[None]
    for distance in (4, 2, 1):
        if distance == 2:
            block, aside = lax.optimization_barrier((block, aside))
        other = exchange(block, "fsdp", OWNERS, distance)
        upper = (me & distance) != 0
        pair = jnp.stack(
            [jnp.where(upper, other, block), jnp.where(upper, block, other)], axis=1
        )
        block = pair.reshape((-1,) + block.shape[1:])
    return block, aside


def pair_sum(parts):
    parity = lax.axis_index("fsdp") % 2
    own = lax.dynamic_index_in_dim(parts, parity, 0, False)
    away = lax.dynamic_index_in_dim(parts, 1 - parity, 0, False)
    got = exchange(away, "fsdp", OWNERS, 1)
    return (own.astype(f32) + got.astype(f32)).astype(bf16)


def column_sum(parts):
    place = lax.axis_index("fsdp") // 2
    got = [
        exchange(
            lax.dynamic_index_in_dim(parts, place ^ distance, 0, False),
            "fsdp", OWNERS, 2 * distance,
        )
        for distance in (3, 2, 1)
    ]
    total = lax.dynamic_index_in_dim(parts, place, 0, False).astype(f32)
    for block in got:
        total = total + block.astype(f32)
    return total


def group_sum(total):
    groups = lax.all_gather(total.astype(bf16), "dp", axis=0)
    return jnp.sum(groups.astype(f32), axis=0)


def in_order(parts):
    return parts.transpose(1, 0, 2, 3).reshape((-1,) + parts.shape[2:])


def scatter_sum_any(full, axis):
    own = lax.psum_scatter(full, "fsdp", scatter_dimension=axis, tiled=True)
    return lax.psum(own, "dp")


def local(
    inputs,
    inject,
    segments,
    cotangent,
    qkv_weight,
    out_weight,
    up_weight,
    down_weight,
    *vectors,
):
    row_count, length, model = inputs.shape
    tokens = row_count * length
    chunks = tokens // CHUNK
    x = inputs.reshape(tokens, model)
    inj = inject.reshape(tokens, model)
    cot = cotangent.reshape(tokens, model)
    seg = segments.reshape(chunks, 1, CHUNK)
    per_row = length // CHUNK
    packed = out_weight.shape[1] * OWNERS == model
    if packed:
        first_own = pack_first(qkv_weight.T, vectors)[0]
        first_own, out_own, up_own, down_own = lax.optimization_barrier(
            (first_own, out_weight.T, up_weight, down_weight.T)
        )
        second_own = pack_second(out_own, up_own, down_own)[0]
        first_weights, second_own = gather(first_own, second_own)
        second_weights = lax.all_gather(second_own, "fsdp", axis=0)
    else:

        def gathered(array, axis):
            return lax.all_gather(array, "fsdp", axis=axis, tiled=True)

        first_weights = pack_first(
            gathered(qkv_weight, 1).T, tuple(gathered(vector, 0) for vector in vectors)
        )
        second_weights = pack_second(
            gathered(out_weight, 1).T, gathered(up_weight, 1), gathered(down_weight, 1).T
        )
    saved = run_one(x, inj, seg, first_weights, per_row)
    result, dm, dc, du2, second_grads, sum_qkv, vec_mid = run_two(
        x, saved[-1], inj, cot, seg, first_weights, second_weights, per_row
    )
    if packed:
        second_pair, dm = lax.optimization_barrier((pair_sum(second_grads), dm))
        second_column = column_sum(second_pair).astype(bf16)
    grad_inputs, grad_inject, first_grads = run_three(
        saved, dm, dc, du2, first_weights, sum_qkv, vec_mid
    )
    if packed:
        second_column, first_grads = lax.optimization_barrier((second_column, first_grads))
        first_column = column_sum(pair_sum(first_grads)).astype(bf16)
        sums = group_sum(jnp.concatenate([first_column, second_column], axis=0))[None]
        first_sum, second_sum = sums[:, :128], sums[:, 128:]
        out_t, up, down_t = unpack_second_grads(second_sum)
        weight_grads = (first_sum[0, :96].T, out_t.T, up, down_t.T)
        vector_grads = unpack_vectors(first_sum[:, 96:])
    else:
        first_all = in_order(first_grads).astype(f32)
        out_t, up, down_t = unpack_second_grads(in_order(second_grads).astype(f32))
        weight_grads = tuple(
            scatter_sum_any(grad, 1)
            for grad in (first_all[:, :96].reshape(3 * model, model).T, out_t.T, up, down_t.T)
        )
        vector_grads = [scatter_sum_any(grad, 0) for grad in unpack_vectors(first_all[:, 96:])]
    dims = inputs.shape
    return (
        result.reshape(dims),
        grad_inputs.reshape(dims),
        grad_inject.reshape(dims),
        *weight_grads,
        *vector_grads,
    )


def solution(mesh):
    placed = (
        P(("dp", "fsdp"), None, None),
        P(("dp", "fsdp"), None, None),
        P(("dp", "fsdp"), None),
        P(("dp", "fsdp"), None, None),
        P(None, "fsdp"),
        P(None, "fsdp"),
        P(None, "fsdp"),
        P(None, "fsdp"),
        P("fsdp"),
        P("fsdp"),
        P("fsdp"),
        P("fsdp"),
        P("fsdp"),
        P("fsdp"),
        P("fsdp"),
        P("fsdp"),
        P("fsdp"),
    )
    return jax.shard_map(
        local,
        mesh=mesh,
        in_specs=placed,
        out_specs=(
            P(("dp", "fsdp"), None, None),
            P(("dp", "fsdp"), None, None),
            P(("dp", "fsdp"), None, None),
            P(None, "fsdp"),
            P(None, "fsdp"),
            P(None, "fsdp"),
            P(None, "fsdp"),
            P("fsdp"),
            P("fsdp"),
            P("fsdp"),
            P("fsdp"),
            P("fsdp"),
            P("fsdp"),
            P("fsdp"),
            P("fsdp"),
            P("fsdp"),
        ),
        check_vma=False,
    )
```

time: 246 us -> 167 us (0.68)
  Pallas kernels: 150 us -> 90.2 us
  blocking collectives: 37.9 us -> 11.4 us
  waiting for transfers between devices: 12.9 us -> 23.7 us
  starting transfers between devices: 18.2 us -> 13.7 us
    pallas_call x3, Pallas kernels: 150 us -> 90.2 us  [the longest x1 60.2 us: run_two(): pl.pallas_call(partial(kernel_two, per_row, chunks), grid=(2 * turn,), in...]
    all_gather x3 -> x1, blocking collectives: 37.9 us -> 11.4 us  [group_sum(): groups = lax.all_gather(total.astype(bf16), 'dp', axis=0)]
    all_gather x1, waiting for transfers between devices: 0.01 us -> 8.07 us  [local(): second_weights = lax.all_gather(second_own, 'fsdp', axis=0)]
    ppermute x14 -> x11, starting transfers between devices: 18.1 us -> 13.6 us  [exchange(): return lax.ppermute(block, axis, [(k, k ^ distance) for k in range(size)])]
    ppermute x14 -> x11, waiting for transfers between devices: 12.9 us -> 15.6 us  [exchange(): return lax.ppermute(block, axis, [(k, k ^ distance) for k in range(size)])]
  transfers between devices with their start and end apart: 15 -> 12, of which waited for: 4 -> 9; matrix products, arithmetic and copies ran while one was open for 2% -> 2% of each run, Pallas kernels for 12% -> 18%
where the time goes in v2:
time: 167 us
  Pallas kernels  90.2 us (54%)
  waiting for transfers between devices  23.7 us (14%)
  between operations  14.3 us (9%)
  starting transfers between devices  13.7 us (8%)
  blocking collectives  11.4 us (7%)
  local copies, waits for them, and re-layouts  10.8 us (6%)
  other arithmetic  2.84 us (2%)
    pallas_call x1, Pallas kernels, run_two(): pl.pallas_call(partial(kernel_two, per_row, chunks), grid=(2 * turn,), in...  60.2 us
    pallas_call x1, Pallas kernels, run_three(): pl.pallas_call(partial(kernel_three, chunks), grid=(chunks + 1,), in_spec...  16.4 us
    ppermute x11, waiting for transfers between devices, exchange(): return lax.ppermute(block, axis, [(k, k ^ distance) for k in range(size)])  15.6 us
    ppermute x11, starting transfers between devices, exchange(): return lax.ppermute(block, axis, [(k, k ^ distance) for k in range(size)])  13.6 us
    pallas_call x1, Pallas kernels, run_one(): pl.pallas_call(partial(kernel_one, per_row, chunks), grid=(chunks + 1,),...  13.6 us
    all_gather x1, blocking collectives, group_sum(): groups = lax.all_gather(total.astype(bf16), 'dp', axis=0)  11.4 us
    all_gather x1, waiting for transfers between devices, local(): second_weights = lax.all_gather(second_own, 'fsdp', axis=0)  8.07 us
  transfers between devices with their start and end apart: 12, of which 9 were waited for; matrix products, arithmetic and copies ran while one was open for 2% of the time, Pallas kernels for 18%

profile of v2, /device:TPU:0, one launch (start us, length us, event | category | flops | bytes accessed | tf_op | source)
XLA Modules:
  0.0 166.8 jit_solution(9142932826268508755)
XLA Ops:
  9.7 4.0 %collective-permute-start = (bf16[1,128,256]{2,1,0:T(8,128)(2,1)S(1)}, bf16[1,128,256]{2,1,0:T(8,128)(2,1)S(1)}, u32[]{:S(2)}, u32[]{:S(2)}) collective-permute-start(bf16[1,128,256]{2,1,0:T(8,128)(2,1)S(1)} %bitcast.130), channel_id=1, source_target_pairs={{0,4},{1,5},{2,6},{3,7},{4,0},{5,1},{6,2},{7,3},{8,12},{9,13},{10,... | collective-permute-start | bytes 196616 | tf_op jit(solution)/shard_map/ppermute | solution.py:1056
  13.7 0.9 reshape.150
  14.6 0.9 copy.55
  15.5 1.4 maximum_bitcast_fusion
  17.4 1.1 collective-permute-start.1
  18.6 3.9 %collective-permute-done.1 = bf16[2,128,256]{2,1,0:T(8,128)(2,1)S(1)} collective-permute-done((bf16[2,128,256]{2,1,0:T(8,128)(2,1)S(1)}, bf16[2,128,256]{2,1,0:T(8,128)(2,1)S(1)}, u32[]{:S(2)}, u32[]{:S(2)}) %collective-permute-start.1) | collective-permute-done | bytes 131104 | tf_op jit(solution)/shard_map/ppermute | solution.py:1056
  22.6 1.5 collective-permute-done.2
  24.2 0.8 copy.44
  25.1 13.6 %attend_first.1 = (bf16[8,256,256]{2,1,0:T(8,128)(2,1)}, f32[8,1,256]{2,1,0:T(1,128)}, bf16[8,256,256]{2,1,0:T(8,128)(2,1)}, bf16[8,512,256]{2,1,0:T(8,128)(2,1)...) custom-call(bf16[2048,256]{1,0:T(8,128)(2,1)} %bitcast.147, ...), custom_call_target="tpu_custom_call" | custom-call | flops 15399999488 | bytes 42000000 | tf_op jit(solution)/shard_map/attend_first/pallas_call | solution.py:802
  38.7 8.1 %all-gather.4.cloned.1.call-done = bf16[2304,256]{1,0:T(8,128)(2,1)} async-done(((bf16[288,256]{1,0:T(8,128)(2,1)}), bf16[2304,256]{1,0:T(8,128)(2,1)}) %all-gather.4.cloned.1.call-update) | async-done | bytes 1179664 | tf_op jit(solution)/shard_map/all_gather | solution.py:1138
  46.7 60.2 %middle.1 = (bf16[2048,256]{1,0:T(8,128)(2,1)}, bf16[8,256,256]{2,1,0:T(8,128)(2,1)}, bf16[8,256,256]{2,1,0:T(8,128)(2,1)}, bf16[8,256,256]{2,1,0:T(8,128)(2,1)}...) custom-call(bf16[2048,256]{1,0:T(8,128)(2,1)} %bitcast.148, ...), custom_call_target="tpu_custom_call" | custom-call | flops 65999998976 | bytes 180000000 | tf_op jit(solution)/shard_map/middle/pallas_call | solution.py:860
  107.0 1.2 dynamic-slice_bitcast_fusion
  108.5 1.8 %collective-permute-done.3 = bf16[4,288,256]{2,1,0:T(8,128)(2,1)S(1)} collective-permute-done((bf16[4,288,256]{2,1,0:T(8,128)(2,1)S(1)}, bf16[4,288,256]{2,1,0:T(8,128)(2,1)S(1)}, u32[]{:S(2)}, u32[]{:S(2)}) %collective-permute-start.3) | collective-permute-done | bytes 589856 | tf_op jit(solution)/shard_map/ppermute | solution.py:1056
  110.4 2.1 %collective-permute-start.4 = (bf16[288,256]{1,0:T(8,128)(2,1)S(1)}, bf16[288,256]{1,0:T(8,128)(2,1)S(1)}, u32[]{:S(2)}, u32[]{:S(2)}) collective-permute-start(bf16[288,256]{1,0:T(8,128)(2,1)S(1)} %get-tuple-element.78), channel_id=1, source_target_pairs={{0,6},{1,7},{2,4},{3,5},{4,2},{5,3},{6,0},{7,1},{8,14},{9,15},{10,... | collective-permute-start | bytes 442376 | tf_op jit(solution)/shard_map/ppermute | solution.py:1056
  112.5 1.1 collective-permute-start.5
  113.6 1.3 collective-permute-start.6
  114.9 16.4 %attend_back.1 = (bf16[2048,256]{1,0:T(8,128)(2,1)}, bf16[2048,256]{1,0:T(8,128)(2,1)}, bf16[2,4,128,256]{3,2,1,0:T(8,128)(2,1)}) custom-call(bf16[8,256,256]{2,1,0:T(8,128)(2,1)} %get-tuple-element.51.unit, f32[8,1,256]{2,1,0:T(1,128)} %get-tuple-element.52.inv, bf16[8,256,256]{2,1,0:T(8,128)(2,1)} %get-tuple-element.53.normed, ...), custom_call_target="tpu_custom_call" | custom-call | flops 17600000000 | bytes 48000000 | tf_op jit(solution)/shard_map/attend_back/pallas_call | solution.py:973
  131.4 1.0 dynamic-slice_bitcast_fusion.1
  132.5 1.5 collective-permute-done.7
  134.9 1.8 %collective-permute-start.8 = (bf16[128,256]{1,0:T(8,128)(2,1)S(1)}, bf16[128,256]{1,0:T(8,128)(2,1)S(1)}, u32[]{:S(2)}, u32[]{:S(2)}) collective-permute-start(bf16[128,256]{1,0:T(8,128)(2,1)S(1)} %get-tuple-element.85), channel_id=1, source_target_pairs={{0,6},{1,7},{2,4},{3,5},{4,2},{5,3},{6,0},{7,1},{8,14},{9,15},{10,... | collective-permute-start | bytes 196616 | tf_op jit(solution)/shard_map/ppermute | solution.py:1056
  136.8 0.9 collective-permute-start.9
  138.4 2.9 %collective-permute-done.8 = bf16[128,256]{1,0:T(8,128)(2,1)S(1)} collective-permute-done((bf16[128,256]{1,0:T(8,128)(2,1)S(1)}, bf16[128,256]{1,0:T(8,128)(2,1)S(1)}, u32[]{:S(2)}, u32[]{:S(2)}) %collective-permute-start.8) | collective-permute-done | bytes 65568 | tf_op jit(solution)/shard_map/ppermute | solution.py:1056
  141.4 2.7 %collective-permute-done.9 = bf16[128,256]{1,0:T(8,128)(2,1)S(1)} collective-permute-done((bf16[128,256]{1,0:T(8,128)(2,1)S(1)}, bf16[128,256]{1,0:T(8,128)(2,1)S(1)}, u32[]{:S(2)}, u32[]{:S(2)}) %collective-permute-start.9) | collective-permute-done | bytes 65568 | tf_op jit(solution)/shard_map/ppermute | solution.py:1056
  144.1 11.4 %all-gather.1 = bf16[1664,256]{1,0:T(8,128)(2,1)S(1)} all-gather(bf16[416,256]{1,0:T(8,128)(2,1)S(1)} %pad_maximum_fusion.2), channel_id=3, replica_groups=mesh['dp'=4,'fsdp'=8] {'dp'}, dimensions={0}, use_global_device_ids=true | all-gather | bytes 1064960 | tf_op jit(solution)/shard_map/all_gather | solution.py:1098
  (44 shorter events, 10.1 us)
Async XLA Ops:
  7.2 39.5 %all-gather.4.cloned.1.call-start = ((), (), s32[]{:S(2)}) async-start(), calls=%async_computation | async-start | bytes 1327104 | tf_op jit(solution)/shard_map/all_gather | solution.py:1138
  9.7 7.7 %collective-permute-start = (bf16[1,128,256]{2,1,0:T(8,128)(2,1)S(1)}, bf16[1,128,256]{2,1,0:T(8,128)(2,1)S(1)}, u32[]{:S(2)}, u32[]{:S(2)}) collective-permute-start(bf16[1,128,256]{2,1,0:T(8,128)(2,1)S(1)} %bitcast.130), channel_id=1, source_target_pairs={{0,4},{1,5},{2,6},{3,7},{4,0},{5,1},{6,2},{7,3},{8,12},{9,13},{10,... | collective-permute-start | bytes 196616 | tf_op jit(solution)/shard_map/ppermute | solution.py:1056
  17.4 5.0 %collective-permute-start.1 = (bf16[2,128,256]{2,1,0:T(8,128)(2,1)S(1)}, bf16[2,128,256]{2,1,0:T(8,128)(2,1)S(1)}, u32[]{:S(2)}, u32[]{:S(2)}) collective-permute-start(bf16[2,128,256]{2,1,0:T(8,128)(2,1)S(1)} %maximum_bitcast_fusion.1), channel_id=1, source_target_pairs={{0,2},{1,3},{2,0},{3,1},{4,6},{5,7},{6,4},{7,5},{8,10},{9,11},{10,... | collective-permute-start | bytes 393224 | tf_op jit(solution)/shard_map/ppermute | solution.py:1056
  22.5 1.6 collective-permute-start.2
  106.9 3.3 %copy-start = (bf16[2,4,288,256]{3,2,1,0:T(8,128)(2,1)S(1)}, bf16[2,4,288,256]{3,2,1,0:T(8,128)(2,1)}, u32[]{:S(2)}) copy-start(bf16[2,4,288,256]{3,2,1,0:T(8,128)(2,1)} %get-tuple-element.57) | copy-start | bytes 3538948
  108.2 2.1 %collective-permute-start.3 = (bf16[4,288,256]{2,1,0:T(8,128)(2,1)S(1)}, bf16[4,288,256]{2,1,0:T(8,128)(2,1)S(1)}, u32[]{:S(2)}, u32[]{:S(2)}) collective-permute-start(bf16[4,288,256]{2,1,0:T(8,128)(2,1)S(1)} %dynamic-slice_bitcast_fusion), channel_id=1, source_target_pairs={{0,1},{1,0},{2,3},{3,2},{4,5},{5,4},{6,7},{7,6},{8,9},{9,8},{10,11... | collective-permute-start | bytes 1769480 | tf_op jit(solution)/shard_map/ppermute | solution.py:1056
  110.4 20.8 %collective-permute-start.4 = (bf16[288,256]{1,0:T(8,128)(2,1)S(1)}, bf16[288,256]{1,0:T(8,128)(2,1)S(1)}, u32[]{:S(2)}, u32[]{:S(2)}) collective-permute-start(bf16[288,256]{1,0:T(8,128)(2,1)S(1)} %get-tuple-element.78), channel_id=1, source_target_pairs={{0,6},{1,7},{2,4},{3,5},{4,2},{5,3},{6,0},{7,1},{8,14},{9,15},{10,... | collective-permute-start | bytes 442376 | tf_op jit(solution)/shard_map/ppermute | solution.py:1056
  112.5 18.8 %collective-permute-start.5 = (bf16[288,256]{1,0:T(8,128)(2,1)S(1)}, bf16[288,256]{1,0:T(8,128)(2,1)S(1)}, u32[]{:S(2)}, u32[]{:S(2)}) collective-permute-start(bf16[288,256]{1,0:T(8,128)(2,1)S(1)} %get-tuple-element.80), channel_id=1, source_target_pairs={{0,4},{1,5},{2,6},{3,7},{4,0},{5,1},{6,2},{7,3},{8,12},{9,13},{10,... | collective-permute-start | bytes 442376 | tf_op jit(solution)/shard_map/ppermute | solution.py:1056
  113.6 17.7 %collective-permute-start.6 = (bf16[288,256]{1,0:T(8,128)(2,1)S(1)}, bf16[288,256]{1,0:T(8,128)(2,1)S(1)}, u32[]{:S(2)}, u32[]{:S(2)}) collective-permute-start(bf16[288,256]{1,0:T(8,128)(2,1)S(1)} %get-tuple-element.79), channel_id=1, source_target_pairs={{0,2},{1,3},{2,0},{3,1},{4,6},{5,7},{6,4},{7,5},{8,10},{9,11},{10,... | collective-permute-start | bytes 442376 | tf_op jit(solution)/shard_map/ppermute | solution.py:1056
  131.2 2.7 %copy-start.1 = (bf16[2,4,128,256]{3,2,1,0:T(8,128)(2,1)S(1)}, bf16[2,4,128,256]{3,2,1,0:T(8,128)(2,1)}, u32[]{:S(2)}) copy-start(bf16[2,4,128,256]{3,2,1,0:T(8,128)(2,1)} %get-tuple-element.68) | copy-start | bytes 1572868
  132.4 1.6 collective-permute-start.7
  134.1 4.3 %collective-permute-start.10 = (bf16[128,256]{1,0:T(8,128)(2,1)S(1)}, bf16[128,256]{1,0:T(8,128)(2,1)S(1)}, u32[]{:S(2)}, u32[]{:S(2)}) collective-permute-start(bf16[128,256]{1,0:T(8,128)(2,1)S(1)} %get-tuple-element.86), channel_id=1, source_target_pairs={{0,2},{1,3},{2,0},{3,1},{4,6},{5,7},{6,4},{7,5},{8,10},{9,11},{10,... | collective-permute-start | bytes 196616 | tf_op jit(solution)/shard_map/ppermute | solution.py:1056
  134.9 6.5 %collective-permute-start.8 = (bf16[128,256]{1,0:T(8,128)(2,1)S(1)}, bf16[128,256]{1,0:T(8,128)(2,1)S(1)}, u32[]{:S(2)}, u32[]{:S(2)}) collective-permute-start(bf16[128,256]{1,0:T(8,128)(2,1)S(1)} %get-tuple-element.85), channel_id=1, source_target_pairs={{0,6},{1,7},{2,4},{3,5},{4,2},{5,3},{6,0},{7,1},{8,14},{9,15},{10,... | collective-permute-start | bytes 196616 | tf_op jit(solution)/shard_map/ppermute | solution.py:1056
  136.8 7.3 %collective-permute-start.9 = (bf16[128,256]{1,0:T(8,128)(2,1)S(1)}, bf16[128,256]{1,0:T(8,128)(2,1)S(1)}, u32[]{:S(2)}, u32[]{:S(2)}) collective-permute-start(bf16[128,256]{1,0:T(8,128)(2,1)S(1)} %get-tuple-element.87), channel_id=1, source_target_pairs={{0,4},{1,5},{2,6},{3,7},{4,0},{5,1},{6,2},{7,3},{8,12},{9,13},{10,... | collective-permute-start | bytes 196616 | tf_op jit(solution)/shard_map/ppermute | solution.py:1056
Sparse Core Ops, SparseCore 0:
  22.7 23.9 all-gather.3

commit v3 on v2

--- a/solution.py
+++ b/solution.py
@@ -1052,23 +1052,86 @@
     return out_t, up.reshape(model, 128 * count), down_t.reshape(32 * count, 1024)
 
 
+def pack_kernel(qkv_t, out_t, up, down_t, *refs):
+    vectors, (first_o, second_o) = refs[:9], refs[9:]
+    rows = qkv_t.shape[0]
+    first_o[:rows, :] = qkv_t[...]
+    pieces = [vector[...].astype(f32) for vector in vectors[:3] + vectors[4:]]
+    up_bias = vectors[3][...].astype(f32)
+    pieces += [up_bias[:, 32 * col : 32 * (col + 1)] for col in range(4)]
+    table = jnp.concatenate(pieces + [jnp.zeros((4, 32), f32)], axis=0)
+    wide = jnp.concatenate([table, jnp.zeros((16, BLOCK - 32), f32)], axis=1)
+    tall = jnp.concatenate([wide, jnp.zeros((BLOCK - 16, BLOCK), f32)], axis=0)
+    columns = jnp.transpose(tall)[:32, :].astype(bf16)
+    first_o[rows:, :] = jnp.concatenate([columns, jnp.zeros_like(columns)], axis=1)
+    second_o[:32, :] = out_t[...]
+    for side in range(2):
+        second_o[32:160, half(side)] = up[half(side), :]
+    for part in range(4):
+        second_o[160 + 32 * part : 192 + 32 * part, :] = down_t[
+            :, part * CHUNK : (part + 1) * CHUNK
+        ]
+
+
+def pack_own(qkv_t, out_t, up, down_t, vectors):
+    rows, model = qkv_t.shape
+    return pl.pallas_call(
+        pack_kernel,
+        out_shape=[shape((rows + 32, model), bf16), shape((288, model), bf16)],
+        name="pack",
+        cost_estimate=cost(2),
+    )(qkv_t, out_t, up, down_t, *[vector.reshape(1, -1) for vector in vectors])
+
+
+def unpack_kernel(first, *refs):
+    seconds, (qkv_o, out_o, up_o, down_o, *vectors) = refs[:4], refs[4:]
+    total = seconds[0][...].astype(f32)
+    for second in seconds[1:]:
+        total = total + second[...].astype(f32)
+    out_o[...] = total[:32, :]
+    for side in range(2):
+        up_o[half(side), :] = total[32:160, half(side)]
+    for part in range(4):
+        start = 160 + 32 * part
+        down_o[:, part * CHUNK : (part + 1) * CHUNK] = total[start : start + 32, :]
+    total = first[0].astype(f32)
+    for group in range(1, first.shape[0]):
+        total = total + first[group].astype(f32)
+    rows = qkv_o.shape[0]
+    qkv_o[...] = total[:rows, :]
+    columns = total[rows:, :BLOCK]
+    tall = jnp.concatenate([columns, jnp.zeros((BLOCK - 32, BLOCK), f32)], axis=0)
+    table = jnp.transpose(tall)
+    for index, vector in enumerate(vectors[:3] + vectors[4:]):
+        vector[...] = table[index : index + 1, :32]
+    for col in range(4):
+        vectors[3][:, 32 * col : 32 * (col + 1)] = table[8 + col : 9 + col, :32]
+
+
+def unpack_sums(first, seconds, sizes):
+    _, _, model = first.shape
+    dims = [(96, model), (32, model), (model, BLOCK), (32, 4 * model)]
+    dims += [(1, size) for size in sizes]
+    return pl.pallas_call(
+        unpack_kernel,
+        out_shape=[shape(dim, f32) for dim in dims],
+        name="unpack",
+        cost_estimate=cost(2),
+    )(first, *seconds)
+
+
 def exchange(block, axis, size, distance):
     return lax.ppermute(block, axis, [(k, k ^ distance) for k in range(size)])
 
 
-def gather(block, aside):
-    me = lax.axis_index("fsdp")
-    block = block[None]
-    for distance in (4, 2, 1):
-        if distance == 2:
-            block, aside = lax.optimization_barrier((block, aside))
-        other = exchange(block, "fsdp", OWNERS, distance)
-        upper = (me & distance) != 0
-        pair = jnp.stack(
-            [jnp.where(upper, other, block), jnp.where(upper, block, other)], axis=1
-        )
-        block = pair.reshape((-1,) + block.shape[1:])
-    return block, aside
+def doubled(block, distance):
+    return in_pairs(block, exchange(block, "fsdp", OWNERS, distance), distance)
+
+
+def in_pairs(block, other, distance):
+    upper = (lax.axis_index("fsdp") & distance) != 0
+    pair = jnp.stack([jnp.where(upper, other, block), jnp.where(upper, block, other)], axis=1)
+    return pair.reshape((-1,) + block.shape[1:])
 
 
 def pair_sum(parts):
@@ -1092,11 +1155,6 @@
     for block in got:
         total = total + block.astype(f32)
     return total
-
-
-def group_sum(total):
-    groups = lax.all_gather(total.astype(bf16), "dp", axis=0)
-    return jnp.sum(groups.astype(f32), axis=0)
 
 
 def in_order(parts):
@@ -1127,15 +1185,15 @@
     cot = cotangent.reshape(tokens, model)
     seg = segments.reshape(chunks, 1, CHUNK)
     per_row = length // CHUNK
-    packed = out_weight.shape[1] * OWNERS == model
+    packed = out_weight.shape[1] * OWNERS == model and lax.axis_size("dp") == 4
     if packed:
-        first_own = pack_first(qkv_weight.T, vectors)[0]
-        first_own, out_own, up_own, down_own = lax.optimization_barrier(
-            (first_own, out_weight.T, up_weight, down_weight.T)
-        )
-        second_own = pack_second(out_own, up_own, down_own)[0]
-        first_weights, second_own = gather(first_own, second_own)
-        second_weights = lax.all_gather(second_own, "fsdp", axis=0)
+        first_own, second_own = pack_own(
+            qkv_weight.T, out_weight.T, up_weight, down_weight.T, vectors
+        )
+        first_weights = doubled(doubled(doubled(first_own[None], 4), 2), 1)
+        second_weights = doubled(second_own[None], 4)
+        first_weights, second_weights = lax.optimization_barrier((first_weights, second_weights))
+        second_other = exchange(second_weights, "fsdp", OWNERS, 2)
     else:
 
         def gathered(array, axis):
@@ -1148,6 +1206,10 @@
             gathered(out_weight, 1).T, gathered(up_weight, 1), gathered(down_weight, 1).T
         )
     saved = run_one(x, inj, seg, first_weights, per_row)
+    if packed:
+        second_other, context = lax.optimization_barrier((second_other, saved[-1]))
+        saved = (*saved[:-1], context)
+        second_weights = doubled(in_pairs(second_weights, second_other, 2), 1)
     result, dm, dc, du2, second_grads, sum_qkv, vec_mid = run_two(
         x, saved[-1], inj, cot, seg, first_weights, second_weights, per_row
     )
@@ -1159,12 +1221,15 @@
     )
     if packed:
         second_column, first_grads = lax.optimization_barrier((second_column, first_grads))
+        seconds = [second_column]
+        seconds += [exchange(second_column, "dp", 4, distance) for distance in (1, 2, 3)]
         first_column = column_sum(pair_sum(first_grads)).astype(bf16)
-        sums = group_sum(jnp.concatenate([first_column, second_column], axis=0))[None]
-        first_sum, second_sum = sums[:, :128], sums[:, 128:]
-        out_t, up, down_t = unpack_second_grads(second_sum)
-        weight_grads = (first_sum[0, :96].T, out_t.T, up, down_t.T)
-        vector_grads = unpack_vectors(first_sum[:, 96:])
+        firsts = lax.all_gather(first_column, "dp", axis=0)
+        qkv_t, out_t, up, down_t, *rows = unpack_sums(
+            firsts, seconds, [vector.shape[0] for vector in vectors]
+        )
+        weight_grads = (qkv_t.T, out_t.T, up, down_t.T)
+        vector_grads = [row.reshape(-1) for row in rows]
     else:
         first_all = in_order(first_grads).astype(f32)
         out_t, up, down_t = unpack_second_grads(in_order(second_grads).astype(f32))

time: 167 us -> 150 us (0.90)
  between operations: 14.3 us -> 1.14 us
  starting transfers between devices: 13.7 us -> 22.1 us
  waiting for transfers between devices: 23.7 us -> 15.9 us
  local copies, waits for them, and re-layouts: 10.8 us -> 5.06 us
  Pallas kernels: 90.2 us -> 94.1 us
  blocking collectives: 11.4 us -> 9.58 us
    ppermute x11 -> x17, starting transfers between devices: 13.6 us -> 22.1 us  [exchange(): return lax.ppermute(block, axis, [(k, k ^ distance) for k in range(size)])]
    all_gather x1 -> x0, waiting for transfers between devices: 8.07 us -> none  [local(): second_weights = lax.all_gather(second_own, 'fsdp', axis=0)]
    pallas_call x0 -> x2, Pallas kernels: none -> 3.88 us  [the longest x1 2.11 us: unpack_sums(): pl.pallas_call(unpack_kernel, out_shape=[shape(dim, f32) for dim in dims]...]
    reshape x6 -> x0, local copies, waits for them, and re-layouts: 3.81 us -> none  [the longest x1 0.87 us: pack_second(): down_t.reshape(count, 32, 4, 256).transpose(0, 2, 1, 3)]
    squeeze x2 -> x0, other arithmetic: 2.2 us -> none  [the longest x1 1.39 us: local(): second_own = pack_second(out_own, up_own, down_own)[0]]
    all_gather x1, blocking collectives: 11.4 us -> 9.58 us  [local(): firsts = lax.all_gather(first_column, 'dp', axis=0)]
    ppermute x11 -> x17, waiting for transfers between devices: 15.6 us -> 15.9 us  [exchange(): return lax.ppermute(block, axis, [(k, k ^ distance) for k in range(size)])]
  transfers between devices with their start and end apart: 12 -> 17, of which waited for: 9 -> 6; matrix products, arithmetic and copies ran while one was open for 2% -> 0% of each run, Pallas kernels for 18% -> 20%
where the time goes in v3:
time: 150 us
  Pallas kernels  94.1 us (63%)
  starting transfers between devices  22.1 us (15%)
  waiting for transfers between devices  15.9 us (11%)
  blocking collectives  9.58 us (6%)
  local copies, waits for them, and re-layouts  5.06 us (3%)
  other arithmetic  1.75 us (1%)
    pallas_call x1, Pallas kernels, run_two(): pl.pallas_call(partial(kernel_two, per_row, chunks), grid=(2 * turn,), in...  60.2 us
    ppermute x17, starting transfers between devices, exchange(): return lax.ppermute(block, axis, [(k, k ^ distance) for k in range(size)])  22.1 us
    pallas_call x1, Pallas kernels, run_three(): pl.pallas_call(partial(kernel_three, chunks), grid=(chunks + 1,), in_spec...  16.3 us
    ppermute x17, waiting for transfers between devices, exchange(): return lax.ppermute(block, axis, [(k, k ^ distance) for k in range(size)])  15.9 us
    pallas_call x1, Pallas kernels, run_one(): pl.pallas_call(partial(kernel_one, per_row, chunks), grid=(chunks + 1,),...  13.6 us
    all_gather x1, blocking collectives, local(): firsts = lax.all_gather(first_column, 'dp', axis=0)  9.58 us
  transfers between devices with their start and end apart: 17, of which 6 were waited for; matrix products, arithmetic and copies ran while one was open for 0% of the time, Pallas kernels for 20%

profile of v3, /device:TPU:0, one launch (start us, length us, event | category | flops | bytes accessed | tf_op | source)
XLA Modules:
  0.0 149.7 jit_solution(5720142582585238046)
XLA Ops:
  0.7 1.8 %pack.1 = (bf16[128,256]{1,0:T(8,128)(2,1)}, bf16[288,256]{1,0:T(8,128)(2,1)}) custom-call(bf16[96,256]{1,0:T(8,128)(2,1)} %bitcast.121, bf16[32,256]{1,0:T(8,128)(2,1)} %bitcast.122, bf16[256,128]{1,0:T(8,128)(2,1)} %up.1, bf16[32,1024]{1,0:T(8,128)(2,1)} %bitcast.120, bf16[1,32]{1,0:T(2,128)(2,1)} %bitcast.125, bf16[1,32]{1,0:T(2,128)(2,1)} %bitcast.126, ...), custom_call_target="tpu_custom_call" | custom-call | flops 2200000000 | bytes 6000000 | tf_op jit(solution)/shard_map/pack/pallas_call | solution.py:1078
  2.4 4.0 %collective-permute-start = (bf16[1,128,256]{2,1,0:T(8,128)(2,1)}, bf16[1,128,256]{2,1,0:T(8,128)(2,1)S(1)}, u32[]{:S(2)}, u32[]{:S(2)}) collective-permute-start(bf16[1,128,256]{2,1,0:T(8,128)(2,1)} %bitcast.114), channel_id=1, source_target_pairs={{0,4},{1,5},{2,6},{3,7},{4,0},{5,1},{6,2},{7,3},{8,12},{9,13},{10,... | collective-permute-start | bytes 196616 | tf_op jit(solution)/shard_map/ppermute | solution.py:1124
  6.5 3.9 %collective-permute-done = bf16[1,128,256]{2,1,0:T(8,128)(2,1)S(1)} collective-permute-done((bf16[1,128,256]{2,1,0:T(8,128)(2,1)}, bf16[1,128,256]{2,1,0:T(8,128)(2,1)S(1)}, u32[]{:S(2)}, u32[]{:S(2)}) %collective-permute-start) | collective-permute-done | bytes 65568 | tf_op jit(solution)/shard_map/ppermute | solution.py:1124
  11.9 3.3 %collective-permute-start.3 = (bf16[1,288,256]{2,1,0:T(8,128)(2,1)}, bf16[1,288,256]{2,1,0:T(8,128)(2,1)S(1)}, u32[]{:S(2)}, u32[]{:S(2)}) collective-permute-start(bf16[1,288,256]{2,1,0:T(8,128)(2,1)} %bitcast.113), channel_id=1, source_target_pairs={{0,4},{1,5},{2,6},{3,7},{4,0},{5,1},{6,2},{7,3},{8,12},{9,13},{10,... | collective-permute-start | bytes 442376 | tf_op jit(solution)/shard_map/ppermute | solution.py:1124
  15.2 2.8 %collective-permute-done.1 = bf16[2,128,256]{2,1,0:T(8,128)(2,1)S(1)} collective-permute-done((bf16[2,128,256]{2,1,0:T(8,128)(2,1)S(1)}, bf16[2,128,256]{2,1,0:T(8,128)(2,1)S(1)}, u32[]{:S(2)}, u32[]{:S(2)}) %collective-permute-start.1) | collective-permute-done | bytes 131104 | tf_op jit(solution)/shard_map/ppermute | solution.py:1124
  18.2 3.9 %collective-permute-done.3 = bf16[1,288,256]{2,1,0:T(8,128)(2,1)S(1)} collective-permute-done((bf16[1,288,256]{2,1,0:T(8,128)(2,1)}, bf16[1,288,256]{2,1,0:T(8,128)(2,1)S(1)}, u32[]{:S(2)}, u32[]{:S(2)}) %collective-permute-start.3) | collective-permute-done | bytes 147488 | tf_op jit(solution)/shard_map/ppermute | solution.py:1124
  23.1 13.6 %attend_first.1 = (bf16[8,256,256]{2,1,0:T(8,128)(2,1)}, f32[8,1,256]{2,1,0:T(1,128)}, bf16[8,256,256]{2,1,0:T(8,128)(2,1)}, bf16[8,512,256]{2,1,0:T(8,128)(2,1)...) custom-call(bf16[2048,256]{1,0:T(8,128)(2,1)} %bitcast.115, ...), custom_call_target="tpu_custom_call" | custom-call | flops 15399999488 | bytes 42000000 | tf_op jit(solution)/shard_map/attend_first/pallas_call | solution.py:802
  37.0 2.0 %collective-permute-done.5 = bf16[4,288,256]{2,1,0:T(8,128)(2,1)S(1)} collective-permute-done((bf16[4,288,256]{2,1,0:T(8,128)(2,1)S(1)}, bf16[4,288,256]{2,1,0:T(8,128)(2,1)S(1)}, u32[]{:S(2)}, u32[]{:S(2)}) %collective-permute-start.5) | collective-permute-done | bytes 589856 | tf_op jit(solution)/shard_map/ppermute | solution.py:1124
  39.2 1.1 copy.38
  40.3 60.2 %middle.1 = (bf16[2048,256]{1,0:T(8,128)(2,1)}, bf16[8,256,256]{2,1,0:T(8,128)(2,1)}, bf16[8,256,256]{2,1,0:T(8,128)(2,1)}, bf16[8,256,256]{2,1,0:T(8,128)(2,1)}...) custom-call(bf16[2048,256]{1,0:T(8,128)(2,1)} %bitcast.116, ...), custom_call_target="tpu_custom_call" | custom-call | flops 65999998976 | bytes 180000000 | tf_op jit(solution)/shard_map/middle/pallas_call | solution.py:860
  100.6 1.2 dynamic-slice_bitcast_fusion
  102.0 1.9 %collective-permute-done.6 = bf16[4,288,256]{2,1,0:T(8,128)(2,1)S(1)} collective-permute-done((bf16[4,288,256]{2,1,0:T(8,128)(2,1)S(1)}, bf16[4,288,256]{2,1,0:T(8,128)(2,1)S(1)}, u32[]{:S(2)}, u32[]{:S(2)}) %collective-permute-start.6) | collective-permute-done | bytes 589856 | tf_op jit(solution)/shard_map/ppermute | solution.py:1124
  104.0 2.5 %collective-permute-start.7 = (bf16[288,256]{1,0:T(8,128)(2,1)S(1)}, bf16[288,256]{1,0:T(8,128)(2,1)S(1)}, u32[]{:S(2)}, u32[]{:S(2)}) collective-permute-start(bf16[288,256]{1,0:T(8,128)(2,1)S(1)} %get-tuple-element.98), channel_id=1, source_target_pairs={{0,6},{1,7},{2,4},{3,5},{4,2},{5,3},{6,0},{7,1},{8,14},{9,15},{10,... | collective-permute-start | bytes 442376 | tf_op jit(solution)/shard_map/ppermute | solution.py:1124
  106.5 1.0 collective-permute-start.8
  108.5 16.3 %attend_back.1 = (bf16[2048,256]{1,0:T(8,128)(2,1)}, bf16[2048,256]{1,0:T(8,128)(2,1)}, bf16[2,4,128,256]{3,2,1,0:T(8,128)(2,1)}) custom-call(bf16[8,256,256]{2,1,0:T(8,128)(2,1)} %get-tuple-element.64.unit, f32[8,1,256]{2,1,0:T(1,128)} %get-tuple-element.65.inv, bf16[8,256,256]{2,1,0:T(8,128)(2,1)} %get-tuple-element.66.normed, ...), custom_call_target="tpu_custom_call" | custom-call | flops 17600000000 | bytes 48000000 | tf_op jit(solution)/shard_map/attend_back/pallas_call | solution.py:973
  125.0 1.0 dynamic-slice_bitcast_fusion.1
  126.1 1.5 %collective-permute-done.10 = bf16[4,128,256]{2,1,0:T(8,128)(2,1)S(1)} collective-permute-done((bf16[4,128,256]{2,1,0:T(8,128)(2,1)S(1)}, bf16[4,128,256]{2,1,0:T(8,128)(2,1)S(1)}, u32[]{:S(2)}, u32[]{:S(2)}) %collective-permute-start.10) | collective-permute-done | bytes 262176 | tf_op jit(solution)/shard_map/ppermute | solution.py:1124
  127.7 2.5 %collective-permute-start.11 = (bf16[128,256]{1,0:T(8,128)(2,1)S(1)}, bf16[128,256]{1,0:T(8,128)(2,1)S(1)}, u32[]{:S(2)}, u32[]{:S(2)}) collective-permute-start(bf16[128,256]{1,0:T(8,128)(2,1)S(1)} %get-tuple-element.107), channel_id=1, source_target_pairs={{0,6},{1,7},{2,4},{3,5},{4,2},{5,3},{6,0},{7,1},{8,14},{9,15},{10,... | collective-permute-start | bytes 196616 | tf_op jit(solution)/shard_map/ppermute | solution.py:1124
  130.4 1.8 %collective-permute-start.13 = (bf16[128,256]{1,0:T(8,128)(2,1)S(1)}, bf16[128,256]{1,0:T(8,128)(2,1)S(1)}, u32[]{:S(2)}, u32[]{:S(2)}) collective-permute-start(bf16[128,256]{1,0:T(8,128)(2,1)S(1)} %get-tuple-element.108), channel_id=1, source_target_pairs={{0,2},{1,3},{2,0},{3,1},{4,6},{5,7},{6,4},{7,5},{8,10},{9,11},{10,... | collective-permute-start | bytes 196616 | tf_op jit(solution)/shard_map/ppermute | solution.py:1124
  132.2 1.5 collective-permute-start.14
  133.7 1.5 %collective-permute-start.15 = (bf16[288,256]{1,0:T(8,128)(2,1)S(1)}, bf16[288,256]{1,0:T(8,128)(2,1)S(1)}, u32[]{:S(2)}, u32[]{:S(2)}) collective-permute-start(bf16[288,256]{1,0:T(8,128)(2,1)S(1)} %fusion.4.refs_0_), channel_id=1, source_target_pairs={{0,16},{8,24},{16,0},{24,8},{1,17},{9,25},{17,1},{25,9},{2,18},{10... | collective-permute-start | bytes 442376 | tf_op jit(solution)/shard_map/ppermute | solution.py:1124
  135.2 1.7 %collective-permute-start.16 = (bf16[288,256]{1,0:T(8,128)(2,1)S(1)}, bf16[288,256]{1,0:T(8,128)(2,1)S(1)}, u32[]{:S(2)}, u32[]{:S(2)}) collective-permute-start(bf16[288,256]{1,0:T(8,128)(2,1)S(1)} %fusion.4.refs_0_), channel_id=1, source_target_pairs={{0,24},{8,16},{16,8},{24,0},{1,25},{9,17},{17,9},{25,1},{2,26},{10... | collective-permute-start | bytes 442376 | tf_op jit(solution)/shard_map/ppermute | solution.py:1124
  137.0 9.6 %all-gather = bf16[512,256]{1,0:T(8,128)(2,1)} all-gather(bf16[128,256]{1,0:T(8,128)(2,1)S(1)} %fusion.7), channel_id=2, replica_groups=mesh['dp'=4,'fsdp'=8] {'dp'}, dimensions={0}, use_global_device_ids=true | all-gather | bytes 327680 | tf_op jit(solution)/shard_map/all_gather | solution.py:1227
  147.4 2.1 %unpack.1 = (f32[96,256]{1,0:T(8,128)}, f32[32,256]{1,0:T(8,128)}, f32[256,128]{1,0:T(8,128)}, f32[32,1024]{1,0:T(8,128)}, f32[1,32]{1,0:T(1,128)}, /*index=5*/f...) custom-call(bf16[4,128,256]{2,1,0:T(8,128)(2,1)} %bitcast.112, ...), custom_call_target="tpu_custom_call" | custom-call | flops 2200000000 | bytes 6000000 | tf_op jit(solution)/shard_map/unpack/pallas_call | solution.py:1115
  (54 shorter events, 5.7 us)
Async XLA Ops:
  2.4 19.6 %copy-start.3 = (bf16[288,256]{1,0:T(8,128)(2,1)S(1)}, bf16[288,256]{1,0:T(8,128)(2,1)}, u32[]{:S(2)}) copy-start(bf16[288,256]{1,0:T(8,128)(2,1)} %get-tuple-element.57) | copy-start | bytes 442372
  2.4 7.9 %collective-permute-start = (bf16[1,128,256]{2,1,0:T(8,128)(2,1)}, bf16[1,128,256]{2,1,0:T(8,128)(2,1)S(1)}, u32[]{:S(2)}, u32[]{:S(2)}) collective-permute-start(bf16[1,128,256]{2,1,0:T(8,128)(2,1)} %bitcast.114), channel_id=1, source_target_pairs={{0,4},{1,5},{2,6},{3,7},{4,0},{5,1},{6,2},{7,3},{8,12},{9,13},{10,... | collective-permute-start | bytes 196616 | tf_op jit(solution)/shard_map/ppermute | solution.py:1124
  11.2 6.8 %collective-permute-start.1 = (bf16[2,128,256]{2,1,0:T(8,128)(2,1)S(1)}, bf16[2,128,256]{2,1,0:T(8,128)(2,1)S(1)}, u32[]{:S(2)}, u32[]{:S(2)}) collective-permute-start(bf16[2,128,256]{2,1,0:T(8,128)(2,1)S(1)} %maximum_bitcast_fusion.1), channel_id=1, source_target_pairs={{0,2},{1,3},{2,0},{3,1},{4,6},{5,7},{6,4},{7,5},{8,10},{9,11},{10,... | collective-permute-start | bytes 393224 | tf_op jit(solution)/shard_map/ppermute | solution.py:1124
  11.9 10.1 %collective-permute-start.3 = (bf16[1,288,256]{2,1,0:T(8,128)(2,1)}, bf16[1,288,256]{2,1,0:T(8,128)(2,1)S(1)}, u32[]{:S(2)}, u32[]{:S(2)}) collective-permute-start(bf16[1,288,256]{2,1,0:T(8,128)(2,1)} %bitcast.113), channel_id=1, source_target_pairs={{0,4},{1,5},{2,6},{3,7},{4,0},{5,1},{6,2},{7,3},{8,12},{9,13},{10,... | collective-permute-start | bytes 442376 | tf_op jit(solution)/shard_map/ppermute | solution.py:1124
  18.1 4.0 %collective-permute-start.2 = (bf16[4,128,256]{2,1,0:T(8,128)(2,1)S(1)}, bf16[4,128,256]{2,1,0:T(8,128)(2,1)S(1)}, u32[]{:S(2)}, u32[]{:S(2)}) collective-permute-start(bf16[4,128,256]{2,1,0:T(8,128)(2,1)S(1)} %bitcast.108), channel_id=1, source_target_pairs={{0,1},{1,0},{2,3},{3,2},{4,5},{5,4},{6,7},{7,6},{8,9},{9,8},{10,11... | collective-permute-start | bytes 786440 | tf_op jit(solution)/shard_map/ppermute | solution.py:1124
  23.1 13.6 %collective-permute-start.4 = (bf16[2,288,256]{2,1,0:T(8,128)(2,1)S(1)}, bf16[2,288,256]{2,1,0:T(8,128)(2,1)S(1)}, u32[]{:S(2)}, u32[]{:S(2)}) collective-permute-start(bf16[2,288,256]{2,1,0:T(8,128)(2,1)S(1)} %maximum_bitcast_fusion), channel_id=1, source_target_pairs={{0,2},{1,3},{2,0},{3,1},{4,6},{5,7},{6,4},{7,5},{8,10},{9,11},{10,... | collective-permute-start | bytes 884744 | tf_op jit(solution)/shard_map/ppermute | solution.py:1124
  36.9 2.1 %collective-permute-start.5 = (bf16[4,288,256]{2,1,0:T(8,128)(2,1)S(1)}, bf16[4,288,256]{2,1,0:T(8,128)(2,1)S(1)}, u32[]{:S(2)}, u32[]{:S(2)}) collective-permute-start(bf16[4,288,256]{2,1,0:T(8,128)(2,1)S(1)} %bitcast.106), channel_id=1, source_target_pairs={{0,1},{1,0},{2,3},{3,2},{4,5},{5,4},{6,7},{7,6},{8,9},{9,8},{10,11... | collective-permute-start | bytes 1769480 | tf_op jit(solution)/shard_map/ppermute | solution.py:1124
  100.5 3.3 %copy-start = (bf16[2,4,288,256]{3,2,1,0:T(8,128)(2,1)S(1)}, bf16[2,4,288,256]{3,2,1,0:T(8,128)(2,1)}, u32[]{:S(2)}) copy-start(bf16[2,4,288,256]{3,2,1,0:T(8,128)(2,1)} %get-tuple-element.70) | copy-start | bytes 3538948
  101.8 2.1 %collective-permute-start.6 = (bf16[4,288,256]{2,1,0:T(8,128)(2,1)S(1)}, bf16[4,288,256]{2,1,0:T(8,128)(2,1)S(1)}, u32[]{:S(2)}, u32[]{:S(2)}) collective-permute-start(bf16[4,288,256]{2,1,0:T(8,128)(2,1)S(1)} %dynamic-slice_bitcast_fusion), channel_id=1, source_target_pairs={{0,1},{1,0},{2,3},{3,2},{4,5},{5,4},{6,7},{7,6},{8,9},{9,8},{10,11... | collective-permute-start | bytes 1769480 | tf_op jit(solution)/shard_map/ppermute | solution.py:1124
  104.0 20.8 %collective-permute-start.7 = (bf16[288,256]{1,0:T(8,128)(2,1)S(1)}, bf16[288,256]{1,0:T(8,128)(2,1)S(1)}, u32[]{:S(2)}, u32[]{:S(2)}) collective-permute-start(bf16[288,256]{1,0:T(8,128)(2,1)S(1)} %get-tuple-element.98), channel_id=1, source_target_pairs={{0,6},{1,7},{2,4},{3,5},{4,2},{5,3},{6,0},{7,1},{8,14},{9,15},{10,... | collective-permute-start | bytes 442376 | tf_op jit(solution)/shard_map/ppermute | solution.py:1124
  106.5 18.3 %collective-permute-start.8 = (bf16[288,256]{1,0:T(8,128)(2,1)S(1)}, bf16[288,256]{1,0:T(8,128)(2,1)S(1)}, u32[]{:S(2)}, u32[]{:S(2)}) collective-permute-start(bf16[288,256]{1,0:T(8,128)(2,1)S(1)} %get-tuple-element.100), channel_id=1, source_target_pairs={{0,4},{1,5},{2,6},{3,7},{4,0},{5,1},{6,2},{7,3},{8,12},{9,13},{10,... | collective-permute-start | bytes 442376 | tf_op jit(solution)/shard_map/ppermute | solution.py:1124
  107.6 17.3 %collective-permute-start.9 = (bf16[288,256]{1,0:T(8,128)(2,1)S(1)}, bf16[288,256]{1,0:T(8,128)(2,1)S(1)}, u32[]{:S(2)}, u32[]{:S(2)}) collective-permute-start(bf16[288,256]{1,0:T(8,128)(2,1)S(1)} %get-tuple-element.99), channel_id=1, source_target_pairs={{0,2},{1,3},{2,0},{3,1},{4,6},{5,7},{6,4},{7,5},{8,10},{9,11},{10,... | collective-permute-start | bytes 442376 | tf_op jit(solution)/shard_map/ppermute | solution.py:1124
  124.8 2.8 %copy-start.1 = (bf16[2,4,128,256]{3,2,1,0:T(8,128)(2,1)S(1)}, bf16[2,4,128,256]{3,2,1,0:T(8,128)(2,1)}, u32[]{:S(2)}) copy-start(bf16[2,4,128,256]{3,2,1,0:T(8,128)(2,1)} %get-tuple-element.81) | copy-start | bytes 1572868
  125.0 21.6 %copy-start.2 = (bf16[288,256]{1,0:T(8,128)(2,1)}, bf16[288,256]{1,0:T(8,128)(2,1)S(1)}, u32[]{:S(2)}) copy-start(bf16[288,256]{1,0:T(8,128)(2,1)S(1)} %fusion.4.refs_0_) | copy-start | bytes 442372
  126.0 1.6 %collective-permute-start.10 = (bf16[4,128,256]{2,1,0:T(8,128)(2,1)S(1)}, bf16[4,128,256]{2,1,0:T(8,128)(2,1)S(1)}, u32[]{:S(2)}, u32[]{:S(2)}) collective-permute-start(bf16[4,128,256]{2,1,0:T(8,128)(2,1)S(1)} %dynamic-slice_bitcast_fusion.1), channel_id=1, source_target_pairs={{0,1},{1,0},{2,3},{3,2},{4,5},{5,4},{6,7},{7,6},{8,9},{9,8},{10,11... | collective-permute-start | bytes 786440 | tf_op jit(solution)/shard_map/ppermute | solution.py:1124
  127.7 7.5 %collective-permute-start.11 = (bf16[128,256]{1,0:T(8,128)(2,1)S(1)}, bf16[128,256]{1,0:T(8,128)(2,1)S(1)}, u32[]{:S(2)}, u32[]{:S(2)}) collective-permute-start(bf16[128,256]{1,0:T(8,128)(2,1)S(1)} %get-tuple-element.107), channel_id=1, source_target_pairs={{0,6},{1,7},{2,4},{3,5},{4,2},{5,3},{6,0},{7,1},{8,14},{9,15},{10,... | collective-permute-start | bytes 196616 | tf_op jit(solution)/shard_map/ppermute | solution.py:1124
  130.2 6.7 %collective-permute-start.12 = (bf16[128,256]{1,0:T(8,128)(2,1)S(1)}, bf16[128,256]{1,0:T(8,128)(2,1)S(1)}, u32[]{:S(2)}, u32[]{:S(2)}) collective-permute-start(bf16[128,256]{1,0:T(8,128)(2,1)S(1)} %get-tuple-element.109), channel_id=1, source_target_pairs={{0,4},{1,5},{2,6},{3,7},{4,0},{5,1},{6,2},{7,3},{8,12},{9,13},{10,... | collective-permute-start | bytes 196616 | tf_op jit(solution)/shard_map/ppermute | solution.py:1124
  130.4 6.6 %collective-permute-start.13 = (bf16[128,256]{1,0:T(8,128)(2,1)S(1)}, bf16[128,256]{1,0:T(8,128)(2,1)S(1)}, u32[]{:S(2)}, u32[]{:S(2)}) collective-permute-start(bf16[128,256]{1,0:T(8,128)(2,1)S(1)} %get-tuple-element.108), channel_id=1, source_target_pairs={{0,2},{1,3},{2,0},{3,1},{4,6},{5,7},{6,4},{7,5},{8,10},{9,11},{10,... | collective-permute-start | bytes 196616 | tf_op jit(solution)/shard_map/ppermute | solution.py:1124
  132.2 14.4 %collective-permute-start.14 = (bf16[288,256]{1,0:T(8,128)(2,1)S(1)}, bf16[288,256]{1,0:T(8,128)(2,1)S(1)}, u32[]{:S(2)}, u32[]{:S(2)}) collective-permute-start(bf16[288,256]{1,0:T(8,128)(2,1)S(1)} %fusion.4.refs_0_), channel_id=1, source_target_pairs={{0,8},{8,0},{16,24},{24,16},{1,9},{9,1},{17,25},{25,17},{2,10},{10... | collective-permute-start | bytes 442376 | tf_op jit(solution)/shard_map/ppermute | solution.py:1124
  133.7 12.9 %collective-permute-start.15 = (bf16[288,256]{1,0:T(8,128)(2,1)S(1)}, bf16[288,256]{1,0:T(8,128)(2,1)S(1)}, u32[]{:S(2)}, u32[]{:S(2)}) collective-permute-start(bf16[288,256]{1,0:T(8,128)(2,1)S(1)} %fusion.4.refs_0_), channel_id=1, source_target_pairs={{0,16},{8,24},{16,0},{24,8},{1,17},{9,25},{17,1},{25,9},{2,18},{10... | collective-permute-start | bytes 442376 | tf_op jit(solution)/shard_map/ppermute | solution.py:1124
  135.2 11.4 %collective-permute-start.16 = (bf16[288,256]{1,0:T(8,128)(2,1)S(1)}, bf16[288,256]{1,0:T(8,128)(2,1)S(1)}, u32[]{:S(2)}, u32[]{:S(2)}) collective-permute-start(bf16[288,256]{1,0:T(8,128)(2,1)S(1)} %fusion.4.refs_0_), channel_id=1, source_target_pairs={{0,24},{8,16},{16,8},{24,0},{1,25},{9,17},{17,9},{25,1},{2,26},{10... | collective-permute-start | bytes 442376 | tf_op jit(solution)/shard_map/ppermute | solution.py:1124
  146.6 0.7 copy-start.4
  146.6 0.7 copy-start.5
  146.6 0.7 copy-start.6

commit v4 on v3

--- a/solution.py
+++ b/solution.py
@@ -95,11 +95,15 @@
     return key_at <= query_at, key_at == query_at
 
 
-def set_masks(masks):
+def set_masks(masks, turned=None):
     below, _ = below_mask()
     own = jnp.where(twice(below), 1.0, 0.0)
     masks[0] = (1.0 - own).astype(bf16)
     masks[1] = own.astype(bf16)
+    if turned is not None:
+        own = jnp.transpose(own)
+        turned[0] = (1.0 - own).astype(bf16)
+        turned[1] = own.astype(bf16)
 
 
 def stack(side, pair):
@@ -167,7 +171,7 @@
         set_pairs(q_pairs.at[side], qk, half(side))
 
 
-def attend(seg_ref, segprev, masks, q_pairs, key_win, value_win, probs_o, context_o):
+def attend(seg_ref, segprev, first, masks, q_pairs, key_win, value_win, probs_o, context_o):
     below, diagonal = below_mask()
     below2 = twice(below)
     items = [(side, pair) for side in range(2) for pair in range(PAIRS)]
@@ -180,7 +184,10 @@
             if pair == 0:
                 seg_row = seg_ref[:, half(side)].astype(f32)
                 seg_col = jnp.transpose(jnp.broadcast_to(seg_row, (BLOCK, BLOCK)))
-                seg_key = jnp.where(below, seg_col, segprev[...])
+                earlier = segprev[...]
+                if side == 0:
+                    earlier = jnp.where(first, -2.0, earlier)
+                seg_key = jnp.where(below, seg_col, earlier)
                 segprev[...] = seg_col
                 allowed = ((seg_key == seg_row) & (seg_row >= 0)) | diagonal
                 biases[side] = jnp.where(allowed, 0.0, masked_score)
@@ -308,7 +315,7 @@
 
 
 def back_attention(
-    dc_ref, context, qk, kt_prev, vtok, vtok_prev, probs_ref, masks, pairs, carry, dqkv
+    dc_ref, context, qk, kt_prev, vtok, vtok_prev, probs_ref, masks, turned, pairs, carry, dqkv
 ):
     q_pairs, c_pairs = pairs
     dk_carry, dv_carry = carry
@@ -337,10 +344,10 @@
             lanes = half(side)
             base = 64 * (pair % 2)
             rows = slice(64 * pair, 64 * (pair + 1))
-            prob_win, grad_win = windows.pop(turn - 2)
+            prob_win, grad_win, grad_wide = windows.pop(turn - 2)
             dq = mm(key_win[side][rows, :], grad_win) * score_scale
-            dk = mm_nt(q_pairs[side, pair, base : base + 64, :], grad_win) * score_scale
-            dv = mm_nt(c_pairs[side, pair, base : base + 64, :], prob_win)
+            dk = mm(q_pairs[side, pair, base : base + 64, :], grad_wide) * score_scale
+            dv = mm(c_pairs[side, pair, base : base + 64, :], prob_win)
             dqkv[64 * pair : 64 * pair + HD, lanes] = dq[:HD, :BLOCK].astype(bf16)
             dqkv[64 * pair + HD : 64 * (pair + 1), lanes] = dq[HD:, BLOCK:].astype(bf16)
             krows = slice(model + 64 * pair, model + 64 * (pair + 1))
@@ -363,9 +370,16 @@
             )
             probs = probs_ref[stack(side, pair), :]
             grad_scores = probs * (folded - delta).astype(bf16)
-            prob_win = jnp.concatenate([probs * masks[0], probs * masks[1]], axis=0)
             grad_win = jnp.concatenate([grad_scores * masks[0], grad_scores * masks[1]], axis=0)
-            windows[turn - 1] = (prob_win, grad_win)
+            prob_turned = jnp.transpose(probs)
+            grad_turned = jnp.transpose(grad_scores)
+            prob_win = jnp.concatenate(
+                [prob_turned * turned[0], prob_turned * turned[1]], axis=1
+            )
+            grad_wide = jnp.concatenate(
+                [grad_turned * turned[0], grad_turned * turned[1]], axis=1
+            )
+            windows[turn - 1] = (prob_win, grad_win, grad_wide)
         yield
 
 
@@ -439,10 +453,7 @@
         value_win[...] = jnp.zeros_like(value_win)
         q_pairs[...] = jnp.zeros_like(q_pairs)
         set_masks(masks)
-
-    @pl.when(lax.rem(step - 1, rows_chunks) == 0)
-    def _():
-        segprev[...] = jnp.full(segprev.shape, -2.0, f32)
+        segprev[...] = jnp.zeros_like(segprev)
 
     def first():
         token_sum(x[...], inj[...], u_s)
@@ -453,7 +464,9 @@
         )
 
     def second():
-        return attend(seg.at[0], segprev, masks, q_pairs, key_win, value_win, probs_o.at[0], context_o.at[0])
+        return attend(
+            seg.at[0], segprev, lax.rem(step - 1, rows_chunks) == 0, masks, q_pairs, key_win, value_win, probs_o.at[0], context_o.at[0],
+        )
 
     def finish():
         hand_over(qk_o.at[0], v_s, ktok_s, q_pairs, key_win, value_win)
@@ -478,7 +491,7 @@
     x, c1, inj, cot, seg, first_weights, second_weights,
     result_o, dm_o, dc_o, du_o, grads_o, sum_qkv_o, vec_o,
     w_qkv, vec, w_out, w_up_n, w_down, bcast, up_bias, w_up, w_down_n, w_out_n, w_qkv_n,
-    u1_s, u_s, m1_s, m2_s, g1_s, g2_s, v_s, ktok_s, key_win, value_win, segprev, q_pairs, c_pairs, masks,
+    u1_s, u_s, m1_s, m2_s, g1_s, g2_s, v_s, ktok_s, key_win, value_win, segprev, q_pairs, c_pairs, masks, turned,
     unit_m1, inv_m1, norm_m1, hid1, slope1,
     u2, dm2, unit2, inv2, norm2, qk2, vtok2, probs2, ctx2,
     unit_m2, inv_m2, norm_m2, hid2, slope2,
@@ -489,7 +502,7 @@
     step = pl.program_id(0)
     model = w_out.shape[0]
     ff = w_up.shape[0]
-    turn = chunks + 2
+    turn = chunks // 2 + 1
 
     @pl.when(step == 0)
     def _():
@@ -514,39 +527,41 @@
                     sum_down, sum_up, sum_out, sum_up_bias, sum_vec):
             ref[...] = jnp.zeros_like(ref)
         sum_qkv_o[...] = jnp.zeros_like(sum_qkv_o)
-        set_masks(masks)
-
-    @pl.when(lax.rem(step - 1, rows_chunks) == 0)
-    def _():
-        segprev[...] = jnp.full(segprev.shape, -2.0, f32)
-
-    def mlp_one():
-        i = step
+        set_masks(masks, turned)
+        segprev[...] = jnp.zeros_like(segprev)
+
+    def mlp_one(u):
+        i = 2 * step + u
+        tokens = slice(u * CHUNK, (u + 1) * CHUNK)
 
         def finish(side, h):
-            again = mm_nt(identity(model), inj[half(side), :])
+            again = mm_nt(identity(model), inj[tokens, :][half(side), :])
             u_s[:, half(side)] = h + again
             u2[i, :, half(side)] = h + again
 
-        token_sum(x[...], inj[...], u1_s)
+        token_sum(x[tokens, :], inj[tokens, :], u1_s)
         yield
         yield from feed_forward(
-            u1_s, m1_s, c1[0], bcast, up_bias, w_out, w_up, w_down,
+            u1_s, m1_s, c1[u], bcast, up_bias, w_out, w_up, w_down,
             [r.at[i] for r in (unit_m1, inv_m1, norm_m1, hid1, slope1)], finish,
         )
         out = [r.at[i] for r in (unit2, inv2, norm2, qk2, vtok2)]
         yield from project(u_s, bcast, w_qkv, out + [v_s, ktok_s])
 
-    def attention():
-        i = step - 1
-        return attend(seg.at[0], segprev, masks, q_pairs, key_win, value_win, probs2.at[i], ctx2.at[i])
-
-    def mlp_two():
-        i = step - 2
+    def attention(u):
+        i = 2 * step + u - 1
+        return attend(
+            seg.at[i], segprev, lax.rem(i, rows_chunks) == 0, masks, q_pairs, key_win, value_win,
+            probs2.at[i], ctx2.at[i],
+        )
+
+    def mlp_two(u):
+        i = 2 * step + u - 2
 
         def finish(side, h):
             low = h.astype(bf16)
-            result_o[half(side), :] = mm_nt(identity(BLOCK), low).astype(bf16)
+            place = u * CHUNK + side * BLOCK
+            result_o[place : place + BLOCK, :] = mm_nt(identity(BLOCK), low).astype(bf16)
 
         yield from feed_forward(
             u2.at[i], m2_s, ctx2[i], bcast, up_bias, w_out, w_up, w_down,
@@ -555,30 +570,25 @@
 
     lengths = {mlp_one: 21, attention: 10, mlp_two: 13}
 
-    def forward_turn(*which):
-        weave(*[(stream(), lengths[stream]) for stream in which])
+    def forward_turn(u, *which):
+        weave(*[(stream(u), lengths[stream]) for stream in which])
         if mlp_one in which:
-            hand_over(qk2.at[step], v_s, ktok_s, q_pairs, key_win, value_win)
+            hand_over(qk2.at[2 * step + u], v_s, ktok_s, q_pairs, key_win, value_win)
 
     @pl.when(step == 0)
     def _():
-        forward_turn(mlp_one)
-
-    @pl.when(step == 1)
-    def _():
-        forward_turn(attention, mlp_one)
-
-    @pl.when((step >= 2) & (step < chunks))
-    def _():
-        forward_turn(mlp_two, attention, mlp_one)
-
-    @pl.when(step == chunks)
-    def _():
-        forward_turn(mlp_two, attention)
-
-    @pl.when(step == chunks + 1)
-    def _():
-        forward_turn(mlp_two)
+        forward_turn(0, mlp_one)
+        forward_turn(1, attention, mlp_one)
+
+    @pl.when((step > 0) & (step < turn - 1))
+    def _():
+        forward_turn(0, mlp_two, attention, mlp_one)
+        forward_turn(1, mlp_two, attention, mlp_one)
+
+    @pl.when(step == turn - 1)
+    def _():
+        forward_turn(0, mlp_two, attention)
+        forward_turn(1, mlp_two)
 
     @pl.when(step == turn - 1)
     def _():
@@ -590,9 +600,9 @@
     at = step - turn
     sums = (sum_down, sum_up, sum_up_bias, sum_vec)
 
-    def back_mlp_two():
-        i = chunks - 1 - at
-        g2_s[...] = mm_nt(identity(model), cot[...])
+    def back_mlp_two(u):
+        i = chunks - 1 - (2 * at + u)
+        g2_s[...] = mm_nt(identity(model), cot[(1 - u) * CHUNK : (2 - u) * CHUNK, :])
         yield
         yield from back_feed_forward(
             g2_s, dm2.at[i], [unit_m2_s, inv_m2_s, norm_m2_s, hid2.at[i], slope2_s],
@@ -600,21 +610,22 @@
         )
         yield from back_out(do2_s, ctx2.at[i], w_out_n, sum_out, dc_s)
 
-    def back_attend():
-        i = chunks - at
+    def back_attend(u):
+        i = chunks - (2 * at + u)
         before = jnp.maximum(i - 1, 0)
         return back_attention(
             dc_s, ctx2.at[i], qk2.at[i], qk2.at[before, model:, BLOCK:], vtok2.at[i],
-            vtok2.at[before, BLOCK:, :], probs_s, masks, (q_pairs, c_pairs),
+            vtok2.at[before, BLOCK:, :], probs_s, masks, turned, (q_pairs, c_pairs),
             (dk_carry, dv_carry), dqkv_s,
         )
 
-    def back_rest():
-        i = chunks + 1 - at
+    def back_rest(u):
+        i = chunks + 1 - (2 * at + u)
+        place = 1 - u
 
         def finish(side, du):
             g1_s[:, half(side)] = du
-            du_o[0, :, half(side)] = du.astype(bf16)
+            du_o[place, :, half(side)] = du.astype(bf16)
 
         yield from back_project(
             dm2_s, dqkv_s, unit2_s, inv2_s, norm2_s, bcast, w_qkv_n,
@@ -622,49 +633,49 @@
         )
         yield from back_feed_forward(
             g1_s, None, [unit_m1_s, inv_m1_s, norm_m1_s, hid1.at[i], slope1_s],
-            bcast, (w_down_n, w_up_n), sums, dy1_s, dz1_s, dm_o.at[0],
-        )
-        yield from back_out(dm_o.at[0], c1.at[0], w_out_n, sum_out, dc_o.at[0])
+            bcast, (w_down_n, w_up_n), sums, dy1_s, dz1_s, dm_o.at[place],
+        )
+        yield from back_out(dm_o.at[place], c1.at[place], w_out_n, sum_out, dc_o.at[place])
 
     lengths_back = {back_mlp_two: 13, back_attend: 10, back_rest: 16}
 
-    def backward_turn(*which):
-        weave(*[(stream(), lengths_back[stream]) for stream in which])
+    def backward_turn(u, *which):
+        weave(*[(stream(u), lengths_back[stream]) for stream in which])
+        i = chunks - 1 - (2 * at + u)
         if back_mlp_two in which:
-            probs_s[...] = probs2[chunks - 1 - at]
-            slope2_s[...] = slope2[jnp.maximum(chunks - 2 - at, 0)]
-            unit_m2_s[...] = unit_m2[jnp.maximum(chunks - 2 - at, 0)]
-            norm_m2_s[...] = norm_m2[jnp.maximum(chunks - 2 - at, 0)]
-            inv_m2_s[...] = inv_m2[jnp.maximum(chunks - 2 - at, 0)]
+            before = jnp.maximum(i - 1, 0)
+            probs_s[...] = probs2[i]
+            slope2_s[...] = slope2[before]
+            unit_m2_s[...] = unit_m2[before]
+            norm_m2_s[...] = norm_m2[before]
+            inv_m2_s[...] = inv_m2[before]
         if back_attend in which:
-            slope1_s[...] = slope1[chunks - at]
-            unit_m1_s[...] = unit_m1[chunks - at]
-            unit2_s[...] = unit2[chunks - at]
-            norm_m1_s[...] = norm_m1[chunks - at]
-            norm2_s[...] = norm2[chunks - at]
-            dm2_s[...] = dm2[chunks - at]
-            inv_m1_s[...] = inv_m1[chunks - at]
-            inv2_s[...] = inv2[chunks - at]
+            slope1_s[...] = slope1[i + 1]
+            unit_m1_s[...] = unit_m1[i + 1]
+            unit2_s[...] = unit2[i + 1]
+            norm_m1_s[...] = norm_m1[i + 1]
+            norm2_s[...] = norm2[i + 1]
+            dm2_s[...] = dm2[i + 1]
+            inv_m1_s[...] = inv_m1[i + 1]
+            inv2_s[...] = inv2[i + 1]
 
     @pl.when(at == 0)
     def _():
-        backward_turn(back_mlp_two)
-
-    @pl.when(at == 1)
-    def _():
-        backward_turn(back_attend, back_mlp_two)
-
-    @pl.when((at >= 2) & (at < chunks))
-    def _():
-        backward_turn(back_rest, back_attend, back_mlp_two)
-
-    @pl.when(at == chunks)
-    def _():
-        backward_turn(back_rest, back_attend)
-
-    @pl.when(at == chunks + 1)
-    def _():
-        backward_turn(back_rest)
+        backward_turn(0, back_mlp_two)
+        backward_turn(1, back_attend, back_mlp_two)
+
+    @pl.when((at > 0) & (at < turn - 1))
+    def _():
+        backward_turn(0, back_rest, back_attend, back_mlp_two)
+        backward_turn(1, back_rest, back_attend, back_mlp_two)
+
+    @pl.when(at == turn - 1)
+    def _():
+        backward_turn(0, back_rest, back_attend)
+        backward_turn(1, back_rest)
+
+    @pl.when(at == turn - 1)
+    def _():
         owners = OWNERS
         for part in range(ff // CHUNK):
             rows = slice(part * CHUNK, (part + 1) * CHUNK)
@@ -696,7 +707,7 @@
     chunks,
     unit, inv, normed, qk, kt_prev, vtok, vtok_prev, probs, ctx, dm, dc, du2, first_weights, sum_qkv_i, vec_i,
     gin_o, ginj_o, grads_o,
-    w_qkv, vec, bcast, w_qkv_n, q_pairs, c_pairs, masks, dqkv_s, dk_carry, dv_carry, sum_qkv, sum_vec,
+    w_qkv, vec, bcast, w_qkv_n, q_pairs, c_pairs, masks, turned, dqkv_s, dk_carry, dv_carry, sum_qkv, sum_vec,
 ):
     step = pl.program_id(0)
     model = w_qkv.shape[1]
@@ -712,12 +723,12 @@
         for ref in (q_pairs, c_pairs, dk_carry, dv_carry, sum_vec):
             ref[...] = jnp.zeros_like(ref)
         sum_qkv[...] = sum_qkv_i[...]
-        set_masks(masks)
+        set_masks(masks, turned)
 
     def attention():
         return back_attention(
             dc.at[0], ctx.at[0], qk.at[0], kt_prev.at[0], vtok.at[0], vtok_prev.at[0], probs.at[0],
-            masks, (q_pairs, c_pairs), (dk_carry, dv_carry), dqkv_s,
+            masks, turned, (q_pairs, c_pairs), (dk_carry, dv_carry), dqkv_s,
         )
 
     def rest():
@@ -830,8 +841,8 @@
     owners = second_weights.shape[0]
     ff = BLOCK * owners
     second_grads = shape((2, owners // 2) + second_weights.shape[1:], bf16)
-    last = chunks - 1
-    turn = chunks + 2
+    last = chunks // 2 - 1
+    turn = chunks // 2 + 1
 
     def up(lag):
         return lambda j: jnp.clip(j - lag, 0, last)
@@ -840,13 +851,13 @@
         return lambda j: jnp.clip(last - (j - turn - lag), 0, last)
 
     def up_then_down(j):
-        return jnp.where(j < turn, jnp.minimum(j, last), jnp.clip(last - (j - turn - 2), 0, last))
+        return jnp.where(j < turn, jnp.minimum(j, last), jnp.clip(last - (j - turn - 1), 0, last))
 
     def lead(dims, order):
-        return pl.BlockSpec((1,) + dims, lambda j: (order(j),) + (0,) * len(dims))
+        return pl.BlockSpec((2,) + dims, lambda j: (order(j),) + (0,) * len(dims))
 
     def tok(order):
-        return pl.BlockSpec((CHUNK, model), lambda j: (order(j), 0))
+        return pl.BlockSpec((2 * CHUNK, model), lambda j: (order(j), 0))
 
     square = (model, CHUNK)
     mlp_saved = [
@@ -865,15 +876,15 @@
             lead(square, up_then_down),
             tok(up(0)),
             tok(down(0)),
-            lead((1, CHUNK), up(1)),
+            whole(seg),
             whole(first_weights),
             whole(second_weights),
         ],
         out_specs=[
-            tok(up(2)),
-            lead(square, down(2)),
-            lead(square, down(2)),
-            lead(square, down(2)),
+            tok(up(1)),
+            lead(square, down(1)),
+            lead(square, down(1)),
+            lead(square, down(1)),
             whole(second_grads),
             pl.BlockSpec((3 * model, model), lambda j: (0, 0)),
             pl.BlockSpec((model, BLOCK), lambda j: (0, 0)),
@@ -910,6 +921,7 @@
             vmem((2, PAIRS, BLOCK, CHUNK), bf16),
             vmem((2, PAIRS, BLOCK, CHUNK), bf16),
             vmem((2, BLOCK, CHUNK), bf16),
+            vmem((2, CHUNK, BLOCK), bf16),
         ]
         + mlp_saved
         + [
@@ -1008,6 +1020,7 @@
             vmem((2, PAIRS, BLOCK, CHUNK), bf16),
             vmem((2, PAIRS, BLOCK, CHUNK), bf16),
             vmem((2, BLOCK, CHUNK), bf16),
+            vmem((2, CHUNK, BLOCK), bf16),
             vmem((3 * model, CHUNK), bf16),
             vmem((model, BLOCK), f32),
             vmem((model, BLOCK), f32),

time: 150 us -> 145 us (0.967)
  Pallas kernels: 94.1 us -> 88.5 us
    pallas_call x1, Pallas kernels: 60.2 us -> 55.7 us  [run_two(): pl.pallas_call(partial(kernel_two, per_row, chunks), grid=(2 * turn,), in...]
where the time goes in v4:
time: 145 us; the launch traced here: 144 us
  Pallas kernels  88.5 us (61%)
  starting transfers between devices  22.1 us (15%)
  waiting for transfers between devices  15.9 us (11%)
  blocking collectives  9.56 us (7%)
  local copies, waits for them, and re-layouts  5.06 us (3%)
  other arithmetic  1.75 us (1%)
    pallas_call x1, Pallas kernels, run_two(): pl.pallas_call(partial(kernel_two, per_row, chunks), grid=(2 * turn,), in...  55.7 us
    ppermute x17, starting transfers between devices, exchange(): return lax.ppermute(block, axis, [(k, k ^ distance) for k in range(size)])  22.1 us
    ppermute x17, waiting for transfers between devices, exchange(): return lax.ppermute(block, axis, [(k, k ^ distance) for k in range(size)])  15.9 us
    pallas_call x1, Pallas kernels, run_three(): pl.pallas_call(partial(kernel_three, chunks), grid=(chunks + 1,), in_spec...  15.6 us
    pallas_call x1, Pallas kernels, run_one(): pl.pallas_call(partial(kernel_one, per_row, chunks), grid=(chunks + 1,),...  13.4 us
    all_gather x1, blocking collectives, local(): firsts = lax.all_gather(first_column, 'dp', axis=0)  9.56 us
  transfers between devices with their start and end apart: 17, of which 6 were waited for; matrix products, arithmetic and copies ran while one was open for 0% of the time, Pallas kernels for 20%

profile of v4, /device:TPU:0, one launch (start us, length us, event | category | flops | bytes accessed | tf_op | source)
XLA Modules:
  0.0 144.1 jit_solution(17818982083761068479)
XLA Ops:
  0.7 1.8 %pack.1 = (bf16[128,256]{1,0:T(8,128)(2,1)}, bf16[288,256]{1,0:T(8,128)(2,1)}) custom-call(bf16[96,256]{1,0:T(8,128)(2,1)} %bitcast.121, bf16[32,256]{1,0:T(8,128)(2,1)} %bitcast.122, bf16[256,128]{1,0:T(8,128)(2,1)} %up.1, bf16[32,1024]{1,0:T(8,128)(2,1)} %bitcast.120, bf16[1,32]{1,0:T(2,128)(2,1)} %bitcast.125, bf16[1,32]{1,0:T(2,128)(2,1)} %bitcast.126, ...), custom_call_target="tpu_custom_call" | custom-call | flops 2200000000 | bytes 6000000 | tf_op jit(solution)/shard_map/pack/pallas_call | solution.py:1091
  2.4 4.0 %collective-permute-start = (bf16[1,128,256]{2,1,0:T(8,128)(2,1)}, bf16[1,128,256]{2,1,0:T(8,128)(2,1)S(1)}, u32[]{:S(2)}, u32[]{:S(2)}) collective-permute-start(bf16[1,128,256]{2,1,0:T(8,128)(2,1)} %bitcast.114), channel_id=1, source_target_pairs={{0,4},{1,5},{2,6},{3,7},{4,0},{5,1},{6,2},{7,3},{8,12},{9,13},{10,... | collective-permute-start | bytes 196616 | tf_op jit(solution)/shard_map/ppermute | solution.py:1137
  6.5 3.9 %collective-permute-done = bf16[1,128,256]{2,1,0:T(8,128)(2,1)S(1)} collective-permute-done((bf16[1,128,256]{2,1,0:T(8,128)(2,1)}, bf16[1,128,256]{2,1,0:T(8,128)(2,1)S(1)}, u32[]{:S(2)}, u32[]{:S(2)}) %collective-permute-start) | collective-permute-done | bytes 65568 | tf_op jit(solution)/shard_map/ppermute | solution.py:1137
  11.9 3.3 %collective-permute-start.3 = (bf16[1,288,256]{2,1,0:T(8,128)(2,1)}, bf16[1,288,256]{2,1,0:T(8,128)(2,1)S(1)}, u32[]{:S(2)}, u32[]{:S(2)}) collective-permute-start(bf16[1,288,256]{2,1,0:T(8,128)(2,1)} %bitcast.113), channel_id=1, source_target_pairs={{0,4},{1,5},{2,6},{3,7},{4,0},{5,1},{6,2},{7,3},{8,12},{9,13},{10,... | collective-permute-start | bytes 442376 | tf_op jit(solution)/shard_map/ppermute | solution.py:1137
  15.2 2.8 %collective-permute-done.1 = bf16[2,128,256]{2,1,0:T(8,128)(2,1)S(1)} collective-permute-done((bf16[2,128,256]{2,1,0:T(8,128)(2,1)S(1)}, bf16[2,128,256]{2,1,0:T(8,128)(2,1)S(1)}, u32[]{:S(2)}, u32[]{:S(2)}) %collective-permute-start.1) | collective-permute-done | bytes 131104 | tf_op jit(solution)/shard_map/ppermute | solution.py:1137
  18.2 3.9 %collective-permute-done.3 = bf16[1,288,256]{2,1,0:T(8,128)(2,1)S(1)} collective-permute-done((bf16[1,288,256]{2,1,0:T(8,128)(2,1)}, bf16[1,288,256]{2,1,0:T(8,128)(2,1)S(1)}, u32[]{:S(2)}, u32[]{:S(2)}) %collective-permute-start.3) | collective-permute-done | bytes 147488 | tf_op jit(solution)/shard_map/ppermute | solution.py:1137
  23.1 13.4 %attend_first.1 = (bf16[8,256,256]{2,1,0:T(8,128)(2,1)}, f32[8,1,256]{2,1,0:T(1,128)}, bf16[8,256,256]{2,1,0:T(8,128)(2,1)}, bf16[8,512,256]{2,1,0:T(8,128)(2,1)...) custom-call(bf16[2048,256]{1,0:T(8,128)(2,1)} %bitcast.115, ...), custom_call_target="tpu_custom_call" | custom-call | flops 15399999488 | bytes 42000000 | tf_op jit(solution)/shard_map/attend_first/pallas_call | solution.py:813
  36.7 2.0 %collective-permute-done.5 = bf16[4,288,256]{2,1,0:T(8,128)(2,1)S(1)} collective-permute-done((bf16[4,288,256]{2,1,0:T(8,128)(2,1)S(1)}, bf16[4,288,256]{2,1,0:T(8,128)(2,1)S(1)}, u32[]{:S(2)}, u32[]{:S(2)}) %collective-permute-start.5) | collective-permute-done | bytes 589856 | tf_op jit(solution)/shard_map/ppermute | solution.py:1137
  38.9 1.1 copy.38
  40.0 55.7 %middle.1 = (bf16[2048,256]{1,0:T(8,128)(2,1)}, bf16[8,256,256]{2,1,0:T(8,128)(2,1)}, bf16[8,256,256]{2,1,0:T(8,128)(2,1)}, bf16[8,256,256]{2,1,0:T(8,128)(2,1)}...) custom-call(bf16[2048,256]{1,0:T(8,128)(2,1)} %bitcast.116, ...), custom_call_target="tpu_custom_call" | custom-call | flops 65999998976 | bytes 180000000 | tf_op jit(solution)/shard_map/middle/pallas_call | solution.py:871
  95.8 1.2 dynamic-slice_bitcast_fusion
  97.2 1.9 %collective-permute-done.6 = bf16[4,288,256]{2,1,0:T(8,128)(2,1)S(1)} collective-permute-done((bf16[4,288,256]{2,1,0:T(8,128)(2,1)S(1)}, bf16[4,288,256]{2,1,0:T(8,128)(2,1)S(1)}, u32[]{:S(2)}, u32[]{:S(2)}) %collective-permute-start.6) | collective-permute-done | bytes 589856 | tf_op jit(solution)/shard_map/ppermute | solution.py:1137
  99.3 2.5 %collective-permute-start.7 = (bf16[288,256]{1,0:T(8,128)(2,1)S(1)}, bf16[288,256]{1,0:T(8,128)(2,1)S(1)}, u32[]{:S(2)}, u32[]{:S(2)}) collective-permute-start(bf16[288,256]{1,0:T(8,128)(2,1)S(1)} %get-tuple-element.98), channel_id=1, source_target_pairs={{0,6},{1,7},{2,4},{3,5},{4,2},{5,3},{6,0},{7,1},{8,14},{9,15},{10,... | collective-permute-start | bytes 442376 | tf_op jit(solution)/shard_map/ppermute | solution.py:1137
  101.8 1.0 collective-permute-start.8
  103.7 15.6 %attend_back.1 = (bf16[2048,256]{1,0:T(8,128)(2,1)}, bf16[2048,256]{1,0:T(8,128)(2,1)}, bf16[2,4,128,256]{3,2,1,0:T(8,128)(2,1)}) custom-call(bf16[8,256,256]{2,1,0:T(8,128)(2,1)} %get-tuple-element.64.unit, f32[8,1,256]{2,1,0:T(1,128)} %get-tuple-element.65.inv, bf16[8,256,256]{2,1,0:T(8,128)(2,1)} %get-tuple-element.66.normed, ...), custom_call_target="tpu_custom_call" | custom-call | flops 17600000000 | bytes 48000000 | tf_op jit(solution)/shard_map/attend_back/pallas_call | solution.py:985
  119.4 1.0 dynamic-slice_bitcast_fusion.1
  120.5 1.5 %collective-permute-done.10 = bf16[4,128,256]{2,1,0:T(8,128)(2,1)S(1)} collective-permute-done((bf16[4,128,256]{2,1,0:T(8,128)(2,1)S(1)}, bf16[4,128,256]{2,1,0:T(8,128)(2,1)S(1)}, u32[]{:S(2)}, u32[]{:S(2)}) %collective-permute-start.10) | collective-permute-done | bytes 262176 | tf_op jit(solution)/shard_map/ppermute | solution.py:1137
  122.2 2.5 %collective-permute-start.11 = (bf16[128,256]{1,0:T(8,128)(2,1)S(1)}, bf16[128,256]{1,0:T(8,128)(2,1)S(1)}, u32[]{:S(2)}, u32[]{:S(2)}) collective-permute-start(bf16[128,256]{1,0:T(8,128)(2,1)S(1)} %get-tuple-element.107), channel_id=1, source_target_pairs={{0,6},{1,7},{2,4},{3,5},{4,2},{5,3},{6,0},{7,1},{8,14},{9,15},{10,... | collective-permute-start | bytes 196616 | tf_op jit(solution)/shard_map/ppermute | solution.py:1137
  124.8 1.8 %collective-permute-start.13 = (bf16[128,256]{1,0:T(8,128)(2,1)S(1)}, bf16[128,256]{1,0:T(8,128)(2,1)S(1)}, u32[]{:S(2)}, u32[]{:S(2)}) collective-permute-start(bf16[128,256]{1,0:T(8,128)(2,1)S(1)} %get-tuple-element.108), channel_id=1, source_target_pairs={{0,2},{1,3},{2,0},{3,1},{4,6},{5,7},{6,4},{7,5},{8,10},{9,11},{10,... | collective-permute-start | bytes 196616 | tf_op jit(solution)/shard_map/ppermute | solution.py:1137
  126.6 1.5 %collective-permute-start.14 = (bf16[288,256]{1,0:T(8,128)(2,1)S(1)}, bf16[288,256]{1,0:T(8,128)(2,1)S(1)}, u32[]{:S(2)}, u32[]{:S(2)}) collective-permute-start(bf16[288,256]{1,0:T(8,128)(2,1)S(1)} %fusion.4.refs_0_), channel_id=1, source_target_pairs={{0,8},{8,0},{16,24},{24,16},{1,9},{9,1},{17,25},{25,17},{2,10},{10... | collective-permute-start | bytes 442376 | tf_op jit(solution)/shard_map/ppermute | solution.py:1137
  128.1 1.5 %collective-permute-start.15 = (bf16[288,256]{1,0:T(8,128)(2,1)S(1)}, bf16[288,256]{1,0:T(8,128)(2,1)S(1)}, u32[]{:S(2)}, u32[]{:S(2)}) collective-permute-start(bf16[288,256]{1,0:T(8,128)(2,1)S(1)} %fusion.4.refs_0_), channel_id=1, source_target_pairs={{0,16},{8,24},{16,0},{24,8},{1,17},{9,25},{17,1},{25,9},{2,18},{10... | collective-permute-start | bytes 442376 | tf_op jit(solution)/shard_map/ppermute | solution.py:1137
  129.6 1.8 %collective-permute-start.16 = (bf16[288,256]{1,0:T(8,128)(2,1)S(1)}, bf16[288,256]{1,0:T(8,128)(2,1)S(1)}, u32[]{:S(2)}, u32[]{:S(2)}) collective-permute-start(bf16[288,256]{1,0:T(8,128)(2,1)S(1)} %fusion.4.refs_0_), channel_id=1, source_target_pairs={{0,24},{8,16},{16,8},{24,0},{1,25},{9,17},{17,9},{25,1},{2,26},{10... | collective-permute-start | bytes 442376 | tf_op jit(solution)/shard_map/ppermute | solution.py:1137
  131.5 9.6 %all-gather = bf16[512,256]{1,0:T(8,128)(2,1)} all-gather(bf16[128,256]{1,0:T(8,128)(2,1)S(1)} %fusion.7), channel_id=2, replica_groups=mesh['dp'=4,'fsdp'=8] {'dp'}, dimensions={0}, use_global_device_ids=true | all-gather | bytes 327680 | tf_op jit(solution)/shard_map/all_gather | solution.py:1240
  141.8 2.1 %unpack.1 = (f32[96,256]{1,0:T(8,128)}, f32[32,256]{1,0:T(8,128)}, f32[256,128]{1,0:T(8,128)}, f32[32,1024]{1,0:T(8,128)}, f32[1,32]{1,0:T(1,128)}, /*index=5*/f...) custom-call(bf16[4,128,256]{2,1,0:T(8,128)(2,1)} %bitcast.112, ...), custom_call_target="tpu_custom_call" | custom-call | flops 2200000000 | bytes 6000000 | tf_op jit(solution)/shard_map/unpack/pallas_call | solution.py:1128
  (54 shorter events, 5.7 us)
Async XLA Ops:
  2.4 19.6 %copy-start.3 = (bf16[288,256]{1,0:T(8,128)(2,1)S(1)}, bf16[288,256]{1,0:T(8,128)(2,1)}, u32[]{:S(2)}) copy-start(bf16[288,256]{1,0:T(8,128)(2,1)} %get-tuple-element.57) | copy-start | bytes 442372
  2.4 7.9 %collective-permute-start = (bf16[1,128,256]{2,1,0:T(8,128)(2,1)}, bf16[1,128,256]{2,1,0:T(8,128)(2,1)S(1)}, u32[]{:S(2)}, u32[]{:S(2)}) collective-permute-start(bf16[1,128,256]{2,1,0:T(8,128)(2,1)} %bitcast.114), channel_id=1, source_target_pairs={{0,4},{1,5},{2,6},{3,7},{4,0},{5,1},{6,2},{7,3},{8,12},{9,13},{10,... | collective-permute-start | bytes 196616 | tf_op jit(solution)/shard_map/ppermute | solution.py:1137
  11.2 6.8 %collective-permute-start.1 = (bf16[2,128,256]{2,1,0:T(8,128)(2,1)S(1)}, bf16[2,128,256]{2,1,0:T(8,128)(2,1)S(1)}, u32[]{:S(2)}, u32[]{:S(2)}) collective-permute-start(bf16[2,128,256]{2,1,0:T(8,128)(2,1)S(1)} %maximum_bitcast_fusion.1), channel_id=1, source_target_pairs={{0,2},{1,3},{2,0},{3,1},{4,6},{5,7},{6,4},{7,5},{8,10},{9,11},{10,... | collective-permute-start | bytes 393224 | tf_op jit(solution)/shard_map/ppermute | solution.py:1137
  11.9 10.1 %collective-permute-start.3 = (bf16[1,288,256]{2,1,0:T(8,128)(2,1)}, bf16[1,288,256]{2,1,0:T(8,128)(2,1)S(1)}, u32[]{:S(2)}, u32[]{:S(2)}) collective-permute-start(bf16[1,288,256]{2,1,0:T(8,128)(2,1)} %bitcast.113), channel_id=1, source_target_pairs={{0,4},{1,5},{2,6},{3,7},{4,0},{5,1},{6,2},{7,3},{8,12},{9,13},{10,... | collective-permute-start | bytes 442376 | tf_op jit(solution)/shard_map/ppermute | solution.py:1137
  18.1 4.0 %collective-permute-start.2 = (bf16[4,128,256]{2,1,0:T(8,128)(2,1)S(1)}, bf16[4,128,256]{2,1,0:T(8,128)(2,1)S(1)}, u32[]{:S(2)}, u32[]{:S(2)}) collective-permute-start(bf16[4,128,256]{2,1,0:T(8,128)(2,1)S(1)} %bitcast.108), channel_id=1, source_target_pairs={{0,1},{1,0},{2,3},{3,2},{4,5},{5,4},{6,7},{7,6},{8,9},{9,8},{10,11... | collective-permute-start | bytes 786440 | tf_op jit(solution)/shard_map/ppermute | solution.py:1137
  23.1 13.4 %collective-permute-start.4 = (bf16[2,288,256]{2,1,0:T(8,128)(2,1)S(1)}, bf16[2,288,256]{2,1,0:T(8,128)(2,1)S(1)}, u32[]{:S(2)}, u32[]{:S(2)}) collective-permute-start(bf16[2,288,256]{2,1,0:T(8,128)(2,1)S(1)} %maximum_bitcast_fusion), channel_id=1, source_target_pairs={{0,2},{1,3},{2,0},{3,1},{4,6},{5,7},{6,4},{7,5},{8,10},{9,11},{10,... | collective-permute-start | bytes 884744 | tf_op jit(solution)/shard_map/ppermute | solution.py:1137
  36.6 2.1 %collective-permute-start.5 = (bf16[4,288,256]{2,1,0:T(8,128)(2,1)S(1)}, bf16[4,288,256]{2,1,0:T(8,128)(2,1)S(1)}, u32[]{:S(2)}, u32[]{:S(2)}) collective-permute-start(bf16[4,288,256]{2,1,0:T(8,128)(2,1)S(1)} %bitcast.106), channel_id=1, source_target_pairs={{0,1},{1,0},{2,3},{3,2},{4,5},{5,4},{6,7},{7,6},{8,9},{9,8},{10,11... | collective-permute-start | bytes 1769480 | tf_op jit(solution)/shard_map/ppermute | solution.py:1137
  95.8 3.3 %copy-start = (bf16[2,4,288,256]{3,2,1,0:T(8,128)(2,1)S(1)}, bf16[2,4,288,256]{3,2,1,0:T(8,128)(2,1)}, u32[]{:S(2)}) copy-start(bf16[2,4,288,256]{3,2,1,0:T(8,128)(2,1)} %get-tuple-element.70) | copy-start | bytes 3538948
  97.0 2.1 %collective-permute-start.6 = (bf16[4,288,256]{2,1,0:T(8,128)(2,1)S(1)}, bf16[4,288,256]{2,1,0:T(8,128)(2,1)S(1)}, u32[]{:S(2)}, u32[]{:S(2)}) collective-permute-start(bf16[4,288,256]{2,1,0:T(8,128)(2,1)S(1)} %dynamic-slice_bitcast_fusion), channel_id=1, source_target_pairs={{0,1},{1,0},{2,3},{3,2},{4,5},{5,4},{6,7},{7,6},{8,9},{9,8},{10,11... | collective-permute-start | bytes 1769480 | tf_op jit(solution)/shard_map/ppermute | solution.py:1137
  99.3 20.0 %collective-permute-start.7 = (bf16[288,256]{1,0:T(8,128)(2,1)S(1)}, bf16[288,256]{1,0:T(8,128)(2,1)S(1)}, u32[]{:S(2)}, u32[]{:S(2)}) collective-permute-start(bf16[288,256]{1,0:T(8,128)(2,1)S(1)} %get-tuple-element.98), channel_id=1, source_target_pairs={{0,6},{1,7},{2,4},{3,5},{4,2},{5,3},{6,0},{7,1},{8,14},{9,15},{10,... | collective-permute-start | bytes 442376 | tf_op jit(solution)/shard_map/ppermute | solution.py:1137
  101.8 17.5 %collective-permute-start.8 = (bf16[288,256]{1,0:T(8,128)(2,1)S(1)}, bf16[288,256]{1,0:T(8,128)(2,1)S(1)}, u32[]{:S(2)}, u32[]{:S(2)}) collective-permute-start(bf16[288,256]{1,0:T(8,128)(2,1)S(1)} %get-tuple-element.100), channel_id=1, source_target_pairs={{0,4},{1,5},{2,6},{3,7},{4,0},{5,1},{6,2},{7,3},{8,12},{9,13},{10,... | collective-permute-start | bytes 442376 | tf_op jit(solution)/shard_map/ppermute | solution.py:1137
  102.8 16.5 %collective-permute-start.9 = (bf16[288,256]{1,0:T(8,128)(2,1)S(1)}, bf16[288,256]{1,0:T(8,128)(2,1)S(1)}, u32[]{:S(2)}, u32[]{:S(2)}) collective-permute-start(bf16[288,256]{1,0:T(8,128)(2,1)S(1)} %get-tuple-element.99), channel_id=1, source_target_pairs={{0,2},{1,3},{2,0},{3,1},{4,6},{5,7},{6,4},{7,5},{8,10},{9,11},{10,... | collective-permute-start | bytes 442376 | tf_op jit(solution)/shard_map/ppermute | solution.py:1137
  119.3 2.8 %copy-start.1 = (bf16[2,4,128,256]{3,2,1,0:T(8,128)(2,1)S(1)}, bf16[2,4,128,256]{3,2,1,0:T(8,128)(2,1)}, u32[]{:S(2)}) copy-start(bf16[2,4,128,256]{3,2,1,0:T(8,128)(2,1)} %get-tuple-element.81) | copy-start | bytes 1572868
  119.4 21.6 %copy-start.2 = (bf16[288,256]{1,0:T(8,128)(2,1)}, bf16[288,256]{1,0:T(8,128)(2,1)S(1)}, u32[]{:S(2)}) copy-start(bf16[288,256]{1,0:T(8,128)(2,1)S(1)} %fusion.4.refs_0_) | copy-start | bytes 442372
  120.5 1.6 %collective-permute-start.10 = (bf16[4,128,256]{2,1,0:T(8,128)(2,1)S(1)}, bf16[4,128,256]{2,1,0:T(8,128)(2,1)S(1)}, u32[]{:S(2)}, u32[]{:S(2)}) collective-permute-start(bf16[4,128,256]{2,1,0:T(8,128)(2,1)S(1)} %dynamic-slice_bitcast_fusion.1), channel_id=1, source_target_pairs={{0,1},{1,0},{2,3},{3,2},{4,5},{5,4},{6,7},{7,6},{8,9},{9,8},{10,11... | collective-permute-start | bytes 786440 | tf_op jit(solution)/shard_map/ppermute | solution.py:1137
  122.2 7.5 %collective-permute-start.11 = (bf16[128,256]{1,0:T(8,128)(2,1)S(1)}, bf16[128,256]{1,0:T(8,128)(2,1)S(1)}, u32[]{:S(2)}, u32[]{:S(2)}) collective-permute-start(bf16[128,256]{1,0:T(8,128)(2,1)S(1)} %get-tuple-element.107), channel_id=1, source_target_pairs={{0,6},{1,7},{2,4},{3,5},{4,2},{5,3},{6,0},{7,1},{8,14},{9,15},{10,... | collective-permute-start | bytes 196616 | tf_op jit(solution)/shard_map/ppermute | solution.py:1137
  124.7 6.7 %collective-permute-start.12 = (bf16[128,256]{1,0:T(8,128)(2,1)S(1)}, bf16[128,256]{1,0:T(8,128)(2,1)S(1)}, u32[]{:S(2)}, u32[]{:S(2)}) collective-permute-start(bf16[128,256]{1,0:T(8,128)(2,1)S(1)} %get-tuple-element.109), channel_id=1, source_target_pairs={{0,4},{1,5},{2,6},{3,7},{4,0},{5,1},{6,2},{7,3},{8,12},{9,13},{10,... | collective-permute-start | bytes 196616 | tf_op jit(solution)/shard_map/ppermute | solution.py:1137
  124.8 6.6 %collective-permute-start.13 = (bf16[128,256]{1,0:T(8,128)(2,1)S(1)}, bf16[128,256]{1,0:T(8,128)(2,1)S(1)}, u32[]{:S(2)}, u32[]{:S(2)}) collective-permute-start(bf16[128,256]{1,0:T(8,128)(2,1)S(1)} %get-tuple-element.108), channel_id=1, source_target_pairs={{0,2},{1,3},{2,0},{3,1},{4,6},{5,7},{6,4},{7,5},{8,10},{9,11},{10,... | collective-permute-start | bytes 196616 | tf_op jit(solution)/shard_map/ppermute | solution.py:1137
  126.6 14.4 %collective-permute-start.14 = (bf16[288,256]{1,0:T(8,128)(2,1)S(1)}, bf16[288,256]{1,0:T(8,128)(2,1)S(1)}, u32[]{:S(2)}, u32[]{:S(2)}) collective-permute-start(bf16[288,256]{1,0:T(8,128)(2,1)S(1)} %fusion.4.refs_0_), channel_id=1, source_target_pairs={{0,8},{8,0},{16,24},{24,16},{1,9},{9,1},{17,25},{25,17},{2,10},{10... | collective-permute-start | bytes 442376 | tf_op jit(solution)/shard_map/ppermute | solution.py:1137
  128.1 12.9 %collective-permute-start.15 = (bf16[288,256]{1,0:T(8,128)(2,1)S(1)}, bf16[288,256]{1,0:T(8,128)(2,1)S(1)}, u32[]{:S(2)}, u32[]{:S(2)}) collective-permute-start(bf16[288,256]{1,0:T(8,128)(2,1)S(1)} %fusion.4.refs_0_), channel_id=1, source_target_pairs={{0,16},{8,24},{16,0},{24,8},{1,17},{9,25},{17,1},{25,9},{2,18},{10... | collective-permute-start | bytes 442376 | tf_op jit(solution)/shard_map/ppermute | solution.py:1137
  129.6 11.4 %collective-permute-start.16 = (bf16[288,256]{1,0:T(8,128)(2,1)S(1)}, bf16[288,256]{1,0:T(8,128)(2,1)S(1)}, u32[]{:S(2)}, u32[]{:S(2)}) collective-permute-start(bf16[288,256]{1,0:T(8,128)(2,1)S(1)} %fusion.4.refs_0_), channel_id=1, source_target_pairs={{0,24},{8,16},{16,8},{24,0},{1,25},{9,17},{17,9},{25,1},{2,26},{10... | collective-permute-start | bytes 442376 | tf_op jit(solution)/shard_map/ppermute | solution.py:1137
  141.0 0.7 copy-start.4
  141.1 0.7 copy-start.5
  141.1 0.7 copy-start.6

commit v5 on v4

--- a/solution.py
+++ b/solution.py
@@ -125,11 +125,12 @@
 
 def weave(*streams):
     order = []
-    for index, (_, steps) in enumerate(streams):
-        order += [((turn + 0.5) / steps, index) for turn in range(steps)]
+    for index, (_, steps, *part) in enumerate(streams):
+        start, end = part or (0.0, 1.0)
+        order += [(start + (end - start) * (turn + 0.5) / steps, index) for turn in range(steps)]
     for _, index in sorted(order):
         next(streams[index][0], None)
-    for generator, _ in streams:
+    for generator, *_ in streams:
         for _ in generator:
             pass
 
@@ -171,7 +172,7 @@
         set_pairs(q_pairs.at[side], qk, half(side))
 
 
-def attend(seg_ref, segprev, first, masks, q_pairs, key_win, value_win, probs_o, context_o):
+def attend(seg, item, rows_chunks, masks, q_pairs, key_win, value_win, probs_o, context_o):
     below, diagonal = below_mask()
     below2 = twice(below)
     items = [(side, pair) for side in range(2) for pair in range(PAIRS)]
@@ -182,13 +183,15 @@
             span = slice(side * BLOCK, side * BLOCK + CHUNK)
             scores[turn] = mm(key_win[span, half(pair // 2)], q_pairs[side, pair])
             if pair == 0:
-                seg_row = seg_ref[:, half(side)].astype(f32)
+                seg_row = seg[item][:, half(side)].astype(f32)
+                if side == 0:
+                    earlier = seg[jnp.maximum(item - 1, 0)][:, BLOCK:].astype(f32)
+                    earlier = jnp.transpose(jnp.broadcast_to(earlier, (BLOCK, BLOCK)))
+                    earlier = jnp.where(lax.rem(item, rows_chunks) == 0, -2.0, earlier)
+                else:
+                    earlier = seg_col
                 seg_col = jnp.transpose(jnp.broadcast_to(seg_row, (BLOCK, BLOCK)))
-                earlier = segprev[...]
-                if side == 0:
-                    earlier = jnp.where(first, -2.0, earlier)
                 seg_key = jnp.where(below, seg_col, earlier)
-                segprev[...] = seg_col
                 allowed = ((seg_key == seg_row) & (seg_row >= 0)) | diagonal
                 biases[side] = jnp.where(allowed, 0.0, masked_score)
         if turn >= 2:
@@ -441,9 +444,10 @@
 def kernel_one(
     rows_chunks, chunks, x, inj, seg, first_weights,
     unit_o, inv_o, normed_o, qk_o, vtok_o, probs_o, context_o,
-    w_qkv, vec, bcast, u_s, v_s, ktok_s, key_win, value_win, segprev, q_pairs, masks,
+    w_qkv, vec, bcast, u_s, v_s, ktok_s, key_win, value_win, q_pairs, masks,
 ):
     step = pl.program_id(0)
+    last = chunks // 2
 
     @pl.when(step == 0)
     def _():
@@ -453,37 +457,50 @@
         value_win[...] = jnp.zeros_like(value_win)
         q_pairs[...] = jnp.zeros_like(q_pairs)
         set_masks(masks)
-        segprev[...] = jnp.zeros_like(segprev)
-
-    def first():
-        token_sum(x[...], inj[...], u_s)
+
+    def first(u):
+        tokens = slice(u * CHUNK, (u + 1) * CHUNK)
+        token_sum(x[tokens, :], inj[tokens, :], u_s.at[u])
         yield
-        yield from project(
-            u_s, bcast, w_qkv,
-            [r.at[0] for r in (unit_o, inv_o, normed_o, qk_o, vtok_o)] + [v_s, ktok_s],
-        )
-
-    def second():
+        out = [r.at[u] for r in (unit_o, inv_o, normed_o, qk_o, vtok_o, v_s, ktok_s)]
+        yield from project(u_s.at[u], bcast, w_qkv, out)
+
+    def second(u):
+        window = slice(u * CHUNK, u * CHUNK + CHUNK + BLOCK)
         return attend(
-            seg.at[0], segprev, lax.rem(step - 1, rows_chunks) == 0, masks, q_pairs, key_win, value_win, probs_o.at[0], context_o.at[0],
+            seg, 2 * step - 2 + u, rows_chunks, masks, q_pairs.at[u], key_win.at[window, :],
+            value_win.at[:, window], probs_o.at[u], context_o.at[u],
         )
 
     def finish():
-        hand_over(qk_o.at[0], v_s, ktok_s, q_pairs, key_win, value_win)
+        key_win[:BLOCK, :] = key_win[2 * CHUNK :, :]
+        value_win[:, :BLOCK] = value_win[:, 2 * CHUNK :]
+        for u in range(2):
+            place = slice(BLOCK + u * CHUNK, BLOCK + (u + 1) * CHUNK)
+            key_win[place, :] = ktok_s[u]
+            value_win[:, place] = v_s[u]
+            for side in range(2):
+                set_pairs(q_pairs.at[u, side], qk_o.at[u], half(side))
+
+    def firsts():
+        return [(first(0), 8), (first(1), 8)]
+
+    def seconds():
+        return [(second(0), 10), (second(1), 10)]
 
     @pl.when(step == 0)
     def _():
-        weave((first(), 8))
+        weave(*firsts())
         finish()
 
-    @pl.when((step > 0) & (step < chunks))
-    def _():
-        weave((second(), 10), (first(), 8))
+    @pl.when((step > 0) & (step < last))
+    def _():
+        weave(*seconds(), *firsts())
         finish()
 
-    @pl.when(step == chunks)
-    def _():
-        weave((second(), 10))
+    @pl.when(step == last)
+    def _():
+        weave(*seconds())
 
 
 def kernel_two(
@@ -491,7 +508,7 @@
     x, c1, inj, cot, seg, first_weights, second_weights,
     result_o, dm_o, dc_o, du_o, grads_o, sum_qkv_o, vec_o,
     w_qkv, vec, w_out, w_up_n, w_down, bcast, up_bias, w_up, w_down_n, w_out_n, w_qkv_n,
-    u1_s, u_s, m1_s, m2_s, g1_s, g2_s, v_s, ktok_s, key_win, value_win, segprev, q_pairs, c_pairs, masks, turned,
+    u1_s, u_s, m1_s, m2_s, g1_s, g2_s, v_s, ktok_s, key_win, value_win, q_pairs, c_pairs, masks, turned,
     unit_m1, inv_m1, norm_m1, hid1, slope1,
     u2, dm2, unit2, inv2, norm2, qk2, vtok2, probs2, ctx2,
     unit_m2, inv_m2, norm_m2, hid2, slope2,
@@ -528,7 +545,6 @@
             ref[...] = jnp.zeros_like(ref)
         sum_qkv_o[...] = jnp.zeros_like(sum_qkv_o)
         set_masks(masks, turned)
-        segprev[...] = jnp.zeros_like(segprev)
 
     def mlp_one(u):
         i = 2 * step + u
@@ -551,7 +567,7 @@
     def attention(u):
         i = 2 * step + u - 1
         return attend(
-            seg.at[i], segprev, lax.rem(i, rows_chunks) == 0, masks, q_pairs, key_win, value_win,
+            seg, i, rows_chunks, masks, q_pairs, key_win, value_win,
             probs2.at[i], ctx2.at[i],
         )
 
@@ -789,7 +805,7 @@
 def run_one(x, inj, seg, first_weights, per_row):
     tokens, model = x.shape
     chunks = tokens // CHUNK
-    last = chunks - 1
+    last = chunks // 2 - 1
 
     def early(j):
         return jnp.minimum(j, last)
@@ -798,9 +814,9 @@
         return jnp.maximum(j - 1, 0)
 
     def lead(dims, order):
-        return pl.BlockSpec((1,) + dims, lambda j: (order(j),) + (0,) * len(dims))
-
-    token_spec = pl.BlockSpec((CHUNK, model), lambda j: (early(j), 0))
+        return pl.BlockSpec((2,) + dims, lambda j: (order(j),) + (0,) * len(dims))
+
+    token_spec = pl.BlockSpec((2 * CHUNK, model), lambda j: (early(j), 0))
     outs = [
         ((model, CHUNK), bf16, early),
         ((1, CHUNK), f32, early),
@@ -812,21 +828,20 @@
     ]
     return pl.pallas_call(
         partial(kernel_one, per_row, chunks),
-        grid=(chunks + 1,),
-        in_specs=[token_spec, token_spec, lead((1, CHUNK), late), whole(first_weights)],
+        grid=(chunks // 2 + 1,),
+        in_specs=[token_spec, token_spec, whole(seg), whole(first_weights)],
         out_specs=[lead(dims, order) for dims, _, order in outs],
         out_shape=[shape((chunks,) + dims, kind) for dims, kind, _ in outs],
         scratch_shapes=[
             vmem((3 * model, model), bf16),
             vmem((model, BLOCK), f32),
             vmem((8, model, BLOCK), f32),
-            vmem((model, CHUNK), f32),
-            vmem((model, CHUNK), bf16),
-            vmem((CHUNK, model), bf16),
-            vmem((CHUNK + BLOCK, model), bf16),
-            vmem((model, CHUNK + BLOCK), bf16),
-            vmem((BLOCK, BLOCK), f32),
-            vmem((2, PAIRS, BLOCK, CHUNK), bf16),
+            vmem((2, model, CHUNK), f32),
+            vmem((2, model, CHUNK), bf16),
+            vmem((2, CHUNK, model), bf16),
+            vmem((2 * CHUNK + BLOCK, model), bf16),
+            vmem((model, 2 * CHUNK + BLOCK), bf16),
+            vmem((2, 2, PAIRS, BLOCK, CHUNK), bf16),
             vmem((2, BLOCK, CHUNK), bf16),
         ],
         compiler_params=params,
@@ -917,7 +932,6 @@
             vmem((CHUNK, model), bf16),
             vmem((CHUNK + BLOCK, model), bf16),
             vmem((model, CHUNK + BLOCK), bf16),
-            vmem((BLOCK, BLOCK), f32),
             vmem((2, PAIRS, BLOCK, CHUNK), bf16),
             vmem((2, PAIRS, BLOCK, CHUNK), bf16),
             vmem((2, BLOCK, CHUNK), bf16),

time: 145 us -> 143 us (0.986)
  Pallas kernels: 88.5 us -> 86.6 us
    pallas_call x1, Pallas kernels: 13.4 us -> 11.5 us  [run_one(): pl.pallas_call(partial(kernel_one, per_row, chunks), grid=(chunks // 2 +...]
  transfers between devices with their start and end apart: 17 -> 17, of which waited for: 6 -> 6; matrix products, arithmetic and copies ran while one was open for 0% -> 0% of each run, Pallas kernels for 20% -> 19%
where the time goes in v5:
time: 143 us; the launch traced here: 142 us
  Pallas kernels  86.6 us (61%)
  starting transfers between devices  22.2 us (16%)
  waiting for transfers between devices  15.9 us (11%)
  blocking collectives  9.58 us (7%)
  local copies, waits for them, and re-layouts  5.06 us (4%)
  other arithmetic  1.75 us (1%)
    pallas_call x1, Pallas kernels, run_two(): pl.pallas_call(partial(kernel_two, per_row, chunks), grid=(2 * turn,), in...  55.7 us
    ppermute x17, starting transfers between devices, exchange(): return lax.ppermute(block, axis, [(k, k ^ distance) for k in range(size)])  22.2 us
    ppermute x17, waiting for transfers between devices, exchange(): return lax.ppermute(block, axis, [(k, k ^ distance) for k in range(size)])  15.9 us
    pallas_call x1, Pallas kernels, run_three(): pl.pallas_call(partial(kernel_three, chunks), grid=(chunks + 1,), in_spec...  15.6 us
    pallas_call x1, Pallas kernels, run_one(): pl.pallas_call(partial(kernel_one, per_row, chunks), grid=(chunks // 2 +...  11.5 us
    all_gather x1, blocking collectives, local(): firsts = lax.all_gather(first_column, 'dp', axis=0)  9.58 us
  transfers between devices with their start and end apart: 17, of which 6 were waited for; matrix products, arithmetic and copies ran while one was open for 0% of the time, Pallas kernels for 19%

profile of v5, /device:TPU:0, one launch (start us, length us, event | category | flops | bytes accessed | tf_op | source)
XLA Modules:
  0.0 142.2 jit_solution(5960822061153078429)
XLA Ops:
  0.7 1.8 %pack.1 = (bf16[128,256]{1,0:T(8,128)(2,1)}, bf16[288,256]{1,0:T(8,128)(2,1)}) custom-call(bf16[96,256]{1,0:T(8,128)(2,1)} %bitcast.121, bf16[32,256]{1,0:T(8,128)(2,1)} %bitcast.122, bf16[256,128]{1,0:T(8,128)(2,1)} %up.1, bf16[32,1024]{1,0:T(8,128)(2,1)} %bitcast.120, bf16[1,32]{1,0:T(2,128)(2,1)} %bitcast.125, bf16[1,32]{1,0:T(2,128)(2,1)} %bitcast.126, ...), custom_call_target="tpu_custom_call" | custom-call | flops 2200000000 | bytes 6000000 | tf_op jit(solution)/shard_map/pack/pallas_call | solution.py:1105
  2.4 4.0 %collective-permute-start = (bf16[1,128,256]{2,1,0:T(8,128)(2,1)}, bf16[1,128,256]{2,1,0:T(8,128)(2,1)S(1)}, u32[]{:S(2)}, u32[]{:S(2)}) collective-permute-start(bf16[1,128,256]{2,1,0:T(8,128)(2,1)} %bitcast.114), channel_id=1, source_target_pairs={{0,4},{1,5},{2,6},{3,7},{4,0},{5,1},{6,2},{7,3},{8,12},{9,13},{10,... | collective-permute-start | bytes 196616 | tf_op jit(solution)/shard_map/ppermute | solution.py:1151
  6.5 3.9 %collective-permute-done = bf16[1,128,256]{2,1,0:T(8,128)(2,1)S(1)} collective-permute-done((bf16[1,128,256]{2,1,0:T(8,128)(2,1)}, bf16[1,128,256]{2,1,0:T(8,128)(2,1)S(1)}, u32[]{:S(2)}, u32[]{:S(2)}) %collective-permute-start) | collective-permute-done | bytes 65568 | tf_op jit(solution)/shard_map/ppermute | solution.py:1151
  11.9 3.3 %collective-permute-start.3 = (bf16[1,288,256]{2,1,0:T(8,128)(2,1)}, bf16[1,288,256]{2,1,0:T(8,128)(2,1)S(1)}, u32[]{:S(2)}, u32[]{:S(2)}) collective-permute-start(bf16[1,288,256]{2,1,0:T(8,128)(2,1)} %bitcast.113), channel_id=1, source_target_pairs={{0,4},{1,5},{2,6},{3,7},{4,0},{5,1},{6,2},{7,3},{8,12},{9,13},{10,... | collective-permute-start | bytes 442376 | tf_op jit(solution)/shard_map/ppermute | solution.py:1151
  15.2 2.8 %collective-permute-done.1 = bf16[2,128,256]{2,1,0:T(8,128)(2,1)S(1)} collective-permute-done((bf16[2,128,256]{2,1,0:T(8,128)(2,1)S(1)}, bf16[2,128,256]{2,1,0:T(8,128)(2,1)S(1)}, u32[]{:S(2)}, u32[]{:S(2)}) %collective-permute-start.1) | collective-permute-done | bytes 131104 | tf_op jit(solution)/shard_map/ppermute | solution.py:1151
  18.2 3.9 %collective-permute-done.3 = bf16[1,288,256]{2,1,0:T(8,128)(2,1)S(1)} collective-permute-done((bf16[1,288,256]{2,1,0:T(8,128)(2,1)}, bf16[1,288,256]{2,1,0:T(8,128)(2,1)S(1)}, u32[]{:S(2)}, u32[]{:S(2)}) %collective-permute-start.3) | collective-permute-done | bytes 147488 | tf_op jit(solution)/shard_map/ppermute | solution.py:1151
  23.1 11.5 %attend_first.1 = (bf16[8,256,256]{2,1,0:T(8,128)(2,1)}, f32[8,1,256]{2,1,0:T(1,128)}, bf16[8,256,256]{2,1,0:T(8,128)(2,1)}, bf16[8,512,256]{2,1,0:T(8,128)(2,1)...) custom-call(bf16[2048,256]{1,0:T(8,128)(2,1)} %bitcast.115, ...), custom_call_target="tpu_custom_call" | custom-call | flops 15399999488 | bytes 42000000 | tf_op jit(solution)/shard_map/attend_first/pallas_call | solution.py:829
  34.8 2.0 %collective-permute-done.5 = bf16[4,288,256]{2,1,0:T(8,128)(2,1)S(1)} collective-permute-done((bf16[4,288,256]{2,1,0:T(8,128)(2,1)S(1)}, bf16[4,288,256]{2,1,0:T(8,128)(2,1)S(1)}, u32[]{:S(2)}, u32[]{:S(2)}) %collective-permute-start.5) | collective-permute-done | bytes 589856 | tf_op jit(solution)/shard_map/ppermute | solution.py:1151
  37.0 1.1 copy.38
  38.1 55.7 %middle.1 = (bf16[2048,256]{1,0:T(8,128)(2,1)}, bf16[8,256,256]{2,1,0:T(8,128)(2,1)}, bf16[8,256,256]{2,1,0:T(8,128)(2,1)}, bf16[8,256,256]{2,1,0:T(8,128)(2,1)}...) custom-call(bf16[2048,256]{1,0:T(8,128)(2,1)} %bitcast.116, ...), custom_call_target="tpu_custom_call" | custom-call | flops 65999998976 | bytes 180000000 | tf_op jit(solution)/shard_map/middle/pallas_call | solution.py:886
  93.8 1.2 dynamic-slice_bitcast_fusion
  95.2 1.9 %collective-permute-done.6 = bf16[4,288,256]{2,1,0:T(8,128)(2,1)S(1)} collective-permute-done((bf16[4,288,256]{2,1,0:T(8,128)(2,1)S(1)}, bf16[4,288,256]{2,1,0:T(8,128)(2,1)S(1)}, u32[]{:S(2)}, u32[]{:S(2)}) %collective-permute-start.6) | collective-permute-done | bytes 589856 | tf_op jit(solution)/shard_map/ppermute | solution.py:1151
  97.3 2.5 %collective-permute-start.7 = (bf16[288,256]{1,0:T(8,128)(2,1)S(1)}, bf16[288,256]{1,0:T(8,128)(2,1)S(1)}, u32[]{:S(2)}, u32[]{:S(2)}) collective-permute-start(bf16[288,256]{1,0:T(8,128)(2,1)S(1)} %get-tuple-element.98), channel_id=1, source_target_pairs={{0,6},{1,7},{2,4},{3,5},{4,2},{5,3},{6,0},{7,1},{8,14},{9,15},{10,... | collective-permute-start | bytes 442376 | tf_op jit(solution)/shard_map/ppermute | solution.py:1151
  99.8 1.0 collective-permute-start.8
  101.8 15.6 %attend_back.1 = (bf16[2048,256]{1,0:T(8,128)(2,1)}, bf16[2048,256]{1,0:T(8,128)(2,1)}, bf16[2,4,128,256]{3,2,1,0:T(8,128)(2,1)}) custom-call(bf16[8,256,256]{2,1,0:T(8,128)(2,1)} %get-tuple-element.64.unit, f32[8,1,256]{2,1,0:T(1,128)} %get-tuple-element.65.inv, bf16[8,256,256]{2,1,0:T(8,128)(2,1)} %get-tuple-element.66.normed, ...), custom_call_target="tpu_custom_call" | custom-call | flops 17600000000 | bytes 48000000 | tf_op jit(solution)/shard_map/attend_back/pallas_call | solution.py:999
  117.5 1.0 dynamic-slice_bitcast_fusion.1
  118.6 1.5 %collective-permute-done.10 = bf16[4,128,256]{2,1,0:T(8,128)(2,1)S(1)} collective-permute-done((bf16[4,128,256]{2,1,0:T(8,128)(2,1)S(1)}, bf16[4,128,256]{2,1,0:T(8,128)(2,1)S(1)}, u32[]{:S(2)}, u32[]{:S(2)}) %collective-permute-start.10) | collective-permute-done | bytes 262176 | tf_op jit(solution)/shard_map/ppermute | solution.py:1151
  120.2 2.5 %collective-permute-start.11 = (bf16[128,256]{1,0:T(8,128)(2,1)S(1)}, bf16[128,256]{1,0:T(8,128)(2,1)S(1)}, u32[]{:S(2)}, u32[]{:S(2)}) collective-permute-start(bf16[128,256]{1,0:T(8,128)(2,1)S(1)} %get-tuple-element.107), channel_id=1, source_target_pairs={{0,6},{1,7},{2,4},{3,5},{4,2},{5,3},{6,0},{7,1},{8,14},{9,15},{10,... | collective-permute-start | bytes 196616 | tf_op jit(solution)/shard_map/ppermute | solution.py:1151
  122.8 1.8 %collective-permute-start.13 = (bf16[128,256]{1,0:T(8,128)(2,1)S(1)}, bf16[128,256]{1,0:T(8,128)(2,1)S(1)}, u32[]{:S(2)}, u32[]{:S(2)}) collective-permute-start(bf16[128,256]{1,0:T(8,128)(2,1)S(1)} %get-tuple-element.108), channel_id=1, source_target_pairs={{0,2},{1,3},{2,0},{3,1},{4,6},{5,7},{6,4},{7,5},{8,10},{9,11},{10,... | collective-permute-start | bytes 196616 | tf_op jit(solution)/shard_map/ppermute | solution.py:1151
  124.7 1.5 %collective-permute-start.14 = (bf16[288,256]{1,0:T(8,128)(2,1)S(1)}, bf16[288,256]{1,0:T(8,128)(2,1)S(1)}, u32[]{:S(2)}, u32[]{:S(2)}) collective-permute-start(bf16[288,256]{1,0:T(8,128)(2,1)S(1)} %fusion.4.refs_0_), channel_id=1, source_target_pairs={{0,8},{8,0},{16,24},{24,16},{1,9},{9,1},{17,25},{25,17},{2,10},{10... | collective-permute-start | bytes 442376 | tf_op jit(solution)/shard_map/ppermute | solution.py:1151
  126.2 1.5 %collective-permute-start.15 = (bf16[288,256]{1,0:T(8,128)(2,1)S(1)}, bf16[288,256]{1,0:T(8,128)(2,1)S(1)}, u32[]{:S(2)}, u32[]{:S(2)}) collective-permute-start(bf16[288,256]{1,0:T(8,128)(2,1)S(1)} %fusion.4.refs_0_), channel_id=1, source_target_pairs={{0,16},{8,24},{16,0},{24,8},{1,17},{9,25},{17,1},{25,9},{2,18},{10... | collective-permute-start | bytes 442376 | tf_op jit(solution)/shard_map/ppermute | solution.py:1151
  127.7 1.8 %collective-permute-start.16 = (bf16[288,256]{1,0:T(8,128)(2,1)S(1)}, bf16[288,256]{1,0:T(8,128)(2,1)S(1)}, u32[]{:S(2)}, u32[]{:S(2)}) collective-permute-start(bf16[288,256]{1,0:T(8,128)(2,1)S(1)} %fusion.4.refs_0_), channel_id=1, source_target_pairs={{0,24},{8,16},{16,8},{24,0},{1,25},{9,17},{17,9},{25,1},{2,26},{10... | collective-permute-start | bytes 442376 | tf_op jit(solution)/shard_map/ppermute | solution.py:1151
  129.5 9.6 %all-gather = bf16[512,256]{1,0:T(8,128)(2,1)} all-gather(bf16[128,256]{1,0:T(8,128)(2,1)S(1)} %fusion.7), channel_id=2, replica_groups=mesh['dp'=4,'fsdp'=8] {'dp'}, dimensions={0}, use_global_device_ids=true | all-gather | bytes 327680 | tf_op jit(solution)/shard_map/all_gather | solution.py:1254
  139.9 2.1 %unpack.1 = (f32[96,256]{1,0:T(8,128)}, f32[32,256]{1,0:T(8,128)}, f32[256,128]{1,0:T(8,128)}, f32[32,1024]{1,0:T(8,128)}, f32[1,32]{1,0:T(1,128)}, /*index=5*/f...) custom-call(bf16[4,128,256]{2,1,0:T(8,128)(2,1)} %bitcast.112, ...), custom_call_target="tpu_custom_call" | custom-call | flops 2200000000 | bytes 6000000 | tf_op jit(solution)/shard_map/unpack/pallas_call | solution.py:1142
  (54 shorter events, 5.7 us)
Async XLA Ops:
  2.4 19.6 %copy-start.3 = (bf16[288,256]{1,0:T(8,128)(2,1)S(1)}, bf16[288,256]{1,0:T(8,128)(2,1)}, u32[]{:S(2)}) copy-start(bf16[288,256]{1,0:T(8,128)(2,1)} %get-tuple-element.57) | copy-start | bytes 442372
  2.4 7.9 %collective-permute-start = (bf16[1,128,256]{2,1,0:T(8,128)(2,1)}, bf16[1,128,256]{2,1,0:T(8,128)(2,1)S(1)}, u32[]{:S(2)}, u32[]{:S(2)}) collective-permute-start(bf16[1,128,256]{2,1,0:T(8,128)(2,1)} %bitcast.114), channel_id=1, source_target_pairs={{0,4},{1,5},{2,6},{3,7},{4,0},{5,1},{6,2},{7,3},{8,12},{9,13},{10,... | collective-permute-start | bytes 196616 | tf_op jit(solution)/shard_map/ppermute | solution.py:1151
  11.2 6.8 %collective-permute-start.1 = (bf16[2,128,256]{2,1,0:T(8,128)(2,1)S(1)}, bf16[2,128,256]{2,1,0:T(8,128)(2,1)S(1)}, u32[]{:S(2)}, u32[]{:S(2)}) collective-permute-start(bf16[2,128,256]{2,1,0:T(8,128)(2,1)S(1)} %maximum_bitcast_fusion.1), channel_id=1, source_target_pairs={{0,2},{1,3},{2,0},{3,1},{4,6},{5,7},{6,4},{7,5},{8,10},{9,11},{10,... | collective-permute-start | bytes 393224 | tf_op jit(solution)/shard_map/ppermute | solution.py:1151
  11.9 10.1 %collective-permute-start.3 = (bf16[1,288,256]{2,1,0:T(8,128)(2,1)}, bf16[1,288,256]{2,1,0:T(8,128)(2,1)S(1)}, u32[]{:S(2)}, u32[]{:S(2)}) collective-permute-start(bf16[1,288,256]{2,1,0:T(8,128)(2,1)} %bitcast.113), channel_id=1, source_target_pairs={{0,4},{1,5},{2,6},{3,7},{4,0},{5,1},{6,2},{7,3},{8,12},{9,13},{10,... | collective-permute-start | bytes 442376 | tf_op jit(solution)/shard_map/ppermute | solution.py:1151
  18.1 4.0 %collective-permute-start.2 = (bf16[4,128,256]{2,1,0:T(8,128)(2,1)S(1)}, bf16[4,128,256]{2,1,0:T(8,128)(2,1)S(1)}, u32[]{:S(2)}, u32[]{:S(2)}) collective-permute-start(bf16[4,128,256]{2,1,0:T(8,128)(2,1)S(1)} %bitcast.108), channel_id=1, source_target_pairs={{0,1},{1,0},{2,3},{3,2},{4,5},{5,4},{6,7},{7,6},{8,9},{9,8},{10,11... | collective-permute-start | bytes 786440 | tf_op jit(solution)/shard_map/ppermute | solution.py:1151
  23.1 11.5 %collective-permute-start.4 = (bf16[2,288,256]{2,1,0:T(8,128)(2,1)S(1)}, bf16[2,288,256]{2,1,0:T(8,128)(2,1)S(1)}, u32[]{:S(2)}, u32[]{:S(2)}) collective-permute-start(bf16[2,288,256]{2,1,0:T(8,128)(2,1)S(1)} %maximum_bitcast_fusion), channel_id=1, source_target_pairs={{0,2},{1,3},{2,0},{3,1},{4,6},{5,7},{6,4},{7,5},{8,10},{9,11},{10,... | collective-permute-start | bytes 884744 | tf_op jit(solution)/shard_map/ppermute | solution.py:1151
  34.7 2.1 %collective-permute-start.5 = (bf16[4,288,256]{2,1,0:T(8,128)(2,1)S(1)}, bf16[4,288,256]{2,1,0:T(8,128)(2,1)S(1)}, u32[]{:S(2)}, u32[]{:S(2)}) collective-permute-start(bf16[4,288,256]{2,1,0:T(8,128)(2,1)S(1)} %bitcast.106), channel_id=1, source_target_pairs={{0,1},{1,0},{2,3},{3,2},{4,5},{5,4},{6,7},{7,6},{8,9},{9,8},{10,11... | collective-permute-start | bytes 1769480 | tf_op jit(solution)/shard_map/ppermute | solution.py:1151
  93.8 3.3 %copy-start = (bf16[2,4,288,256]{3,2,1,0:T(8,128)(2,1)S(1)}, bf16[2,4,288,256]{3,2,1,0:T(8,128)(2,1)}, u32[]{:S(2)}) copy-start(bf16[2,4,288,256]{3,2,1,0:T(8,128)(2,1)} %get-tuple-element.70) | copy-start | bytes 3538948
  95.0 2.1 %collective-permute-start.6 = (bf16[4,288,256]{2,1,0:T(8,128)(2,1)S(1)}, bf16[4,288,256]{2,1,0:T(8,128)(2,1)S(1)}, u32[]{:S(2)}, u32[]{:S(2)}) collective-permute-start(bf16[4,288,256]{2,1,0:T(8,128)(2,1)S(1)} %dynamic-slice_bitcast_fusion), channel_id=1, source_target_pairs={{0,1},{1,0},{2,3},{3,2},{4,5},{5,4},{6,7},{7,6},{8,9},{9,8},{10,11... | collective-permute-start | bytes 1769480 | tf_op jit(solution)/shard_map/ppermute | solution.py:1151
  97.3 20.0 %collective-permute-start.7 = (bf16[288,256]{1,0:T(8,128)(2,1)S(1)}, bf16[288,256]{1,0:T(8,128)(2,1)S(1)}, u32[]{:S(2)}, u32[]{:S(2)}) collective-permute-start(bf16[288,256]{1,0:T(8,128)(2,1)S(1)} %get-tuple-element.98), channel_id=1, source_target_pairs={{0,6},{1,7},{2,4},{3,5},{4,2},{5,3},{6,0},{7,1},{8,14},{9,15},{10,... | collective-permute-start | bytes 442376 | tf_op jit(solution)/shard_map/ppermute | solution.py:1151
  99.8 17.5 %collective-permute-start.8 = (bf16[288,256]{1,0:T(8,128)(2,1)S(1)}, bf16[288,256]{1,0:T(8,128)(2,1)S(1)}, u32[]{:S(2)}, u32[]{:S(2)}) collective-permute-start(bf16[288,256]{1,0:T(8,128)(2,1)S(1)} %get-tuple-element.100), channel_id=1, source_target_pairs={{0,4},{1,5},{2,6},{3,7},{4,0},{5,1},{6,2},{7,3},{8,12},{9,13},{10,... | collective-permute-start | bytes 442376 | tf_op jit(solution)/shard_map/ppermute | solution.py:1151
  100.8 16.5 %collective-permute-start.9 = (bf16[288,256]{1,0:T(8,128)(2,1)S(1)}, bf16[288,256]{1,0:T(8,128)(2,1)S(1)}, u32[]{:S(2)}, u32[]{:S(2)}) collective-permute-start(bf16[288,256]{1,0:T(8,128)(2,1)S(1)} %get-tuple-element.99), channel_id=1, source_target_pairs={{0,2},{1,3},{2,0},{3,1},{4,6},{5,7},{6,4},{7,5},{8,10},{9,11},{10,... | collective-permute-start | bytes 442376 | tf_op jit(solution)/shard_map/ppermute | solution.py:1151
  117.3 2.8 %copy-start.1 = (bf16[2,4,128,256]{3,2,1,0:T(8,128)(2,1)S(1)}, bf16[2,4,128,256]{3,2,1,0:T(8,128)(2,1)}, u32[]{:S(2)}) copy-start(bf16[2,4,128,256]{3,2,1,0:T(8,128)(2,1)} %get-tuple-element.81) | copy-start | bytes 1572868
  117.5 21.6 %copy-start.2 = (bf16[288,256]{1,0:T(8,128)(2,1)}, bf16[288,256]{1,0:T(8,128)(2,1)S(1)}, u32[]{:S(2)}) copy-start(bf16[288,256]{1,0:T(8,128)(2,1)S(1)} %fusion.4.refs_0_) | copy-start | bytes 442372
  118.5 1.6 %collective-permute-start.10 = (bf16[4,128,256]{2,1,0:T(8,128)(2,1)S(1)}, bf16[4,128,256]{2,1,0:T(8,128)(2,1)S(1)}, u32[]{:S(2)}, u32[]{:S(2)}) collective-permute-start(bf16[4,128,256]{2,1,0:T(8,128)(2,1)S(1)} %dynamic-slice_bitcast_fusion.1), channel_id=1, source_target_pairs={{0,1},{1,0},{2,3},{3,2},{4,5},{5,4},{6,7},{7,6},{8,9},{9,8},{10,11... | collective-permute-start | bytes 786440 | tf_op jit(solution)/shard_map/ppermute | solution.py:1151
  120.2 7.5 %collective-permute-start.11 = (bf16[128,256]{1,0:T(8,128)(2,1)S(1)}, bf16[128,256]{1,0:T(8,128)(2,1)S(1)}, u32[]{:S(2)}, u32[]{:S(2)}) collective-permute-start(bf16[128,256]{1,0:T(8,128)(2,1)S(1)} %get-tuple-element.107), channel_id=1, source_target_pairs={{0,6},{1,7},{2,4},{3,5},{4,2},{5,3},{6,0},{7,1},{8,14},{9,15},{10,... | collective-permute-start | bytes 196616 | tf_op jit(solution)/shard_map/ppermute | solution.py:1151
  122.7 6.8 %collective-permute-start.12 = (bf16[128,256]{1,0:T(8,128)(2,1)S(1)}, bf16[128,256]{1,0:T(8,128)(2,1)S(1)}, u32[]{:S(2)}, u32[]{:S(2)}) collective-permute-start(bf16[128,256]{1,0:T(8,128)(2,1)S(1)} %get-tuple-element.109), channel_id=1, source_target_pairs={{0,4},{1,5},{2,6},{3,7},{4,0},{5,1},{6,2},{7,3},{8,12},{9,13},{10,... | collective-permute-start | bytes 196616 | tf_op jit(solution)/shard_map/ppermute | solution.py:1151
  122.8 6.6 %collective-permute-start.13 = (bf16[128,256]{1,0:T(8,128)(2,1)S(1)}, bf16[128,256]{1,0:T(8,128)(2,1)S(1)}, u32[]{:S(2)}, u32[]{:S(2)}) collective-permute-start(bf16[128,256]{1,0:T(8,128)(2,1)S(1)} %get-tuple-element.108), channel_id=1, source_target_pairs={{0,2},{1,3},{2,0},{3,1},{4,6},{5,7},{6,4},{7,5},{8,10},{9,11},{10,... | collective-permute-start | bytes 196616 | tf_op jit(solution)/shard_map/ppermute | solution.py:1151
  124.7 14.4 %collective-permute-start.14 = (bf16[288,256]{1,0:T(8,128)(2,1)S(1)}, bf16[288,256]{1,0:T(8,128)(2,1)S(1)}, u32[]{:S(2)}, u32[]{:S(2)}) collective-permute-start(bf16[288,256]{1,0:T(8,128)(2,1)S(1)} %fusion.4.refs_0_), channel_id=1, source_target_pairs={{0,8},{8,0},{16,24},{24,16},{1,9},{9,1},{17,25},{25,17},{2,10},{10... | collective-permute-start | bytes 442376 | tf_op jit(solution)/shard_map/ppermute | solution.py:1151
  126.2 13.0 %collective-permute-start.15 = (bf16[288,256]{1,0:T(8,128)(2,1)S(1)}, bf16[288,256]{1,0:T(8,128)(2,1)S(1)}, u32[]{:S(2)}, u32[]{:S(2)}) collective-permute-start(bf16[288,256]{1,0:T(8,128)(2,1)S(1)} %fusion.4.refs_0_), channel_id=1, source_target_pairs={{0,16},{8,24},{16,0},{24,8},{1,17},{9,25},{17,1},{25,9},{2,18},{10... | collective-permute-start | bytes 442376 | tf_op jit(solution)/shard_map/ppermute | solution.py:1151
  127.7 11.5 %collective-permute-start.16 = (bf16[288,256]{1,0:T(8,128)(2,1)S(1)}, bf16[288,256]{1,0:T(8,128)(2,1)S(1)}, u32[]{:S(2)}, u32[]{:S(2)}) collective-permute-start(bf16[288,256]{1,0:T(8,128)(2,1)S(1)} %fusion.4.refs_0_), channel_id=1, source_target_pairs={{0,24},{8,16},{16,8},{24,0},{1,25},{9,17},{17,9},{25,1},{2,26},{10... | collective-permute-start | bytes 442376 | tf_op jit(solution)/shard_map/ppermute | solution.py:1151
  139.1 0.7 copy-start.4
  139.1 0.7 copy-start.5
  139.2 0.7 copy-start.6
